TPU v7x, 32 devices: a whole 2x2x4 slice. The times are simulated.
32 devices in a mesh: groups: 2 (over y), blk: 8 (over z, x), win: 2 (over core).
Axes of the slice: x: 2, y: 2, z: 4, core: 2. Of those that a mesh axis runs over, the one named last changes fastest.
Arguments:
- spectra: bfloat16 [4, 16, 2, 32, 512], P('win', ('groups', 'blk')), parts along dimension 1, may hold values from -6 to 6
- block_pairs: int32 [32, 2], P('groups'), parts along dimension 0, may hold values from 0 to 7, as said below
- owners: int32 [32, 1], P('groups'), parts along dimension 0, may hold values from 0 to 7; in each aligned block of 16 rows (0 to 15, 16 to 31, ...) at most 3 rows name the same one
- window_mask: int32 [4, 16], P(None, 'groups'), parts along dimension 1, may hold values 0 or 1
Outputs:
- spectra_grad: bfloat16 [4, 16, 2, 32, 512], P('win', ('groups', 'blk')), parts along dimension 1
- slot_misfit: float32 [48], P(('groups', 'blk')), parts along dimension 0
There are 2 independent parts, one for each index of `groups`. A program takes and returns all parts, laid end to end along the dimension named above; each array names one. Nothing has to cross between parts.
Inputs may be any that keep to these rules, and one draw needn't show every extreme that they name: `block_pairs`: each row names two blocks, the first smaller than the second; a pair may be listed more than once. `owners`: no index of blk owns more than 3 pairs, and some index owns exactly 3; every index owns at least one.
All inputs are finite; a program needn't handle non-finite values.
Results may differ from a plain program's by a relative error of at most 0.0047.
Values may be sent and summed in bfloat16 or wider, within the bound.
No kernel may reach another device: no remote copies, remote signals or barrier semaphores. Data moves between devices by JAX's collectives and lax.ppermute only.
A program may use at most 128 MiB of HBM per device.

v0:
```python
import functools
import math

import jax
import jax.numpy as jnp
import ml_dtypes
import numpy as np
from jax import lax
from jax.experimental import pallas as pl
from jax.experimental.pallas import tpu as pltpu
from jax.sharding import PartitionSpec as P

CAP = 3
PARTS = 4
TEAM = 8
SUBSETS = ((0, 1), (0, 1), (0, 2), (0, 3), (1, 2), (1, 3), (2, 3), (2, 3))
GROUP = 4


@functools.lru_cache(maxsize=None)
def tables(freq_count):
    lag_count = 2 * freq_count
    f = np.arange(freq_count)[:, None]
    t = np.arange(freq_count)[None, :]
    phase = (f * t % lag_count) * (2.0 * np.pi / lag_count)
    cos = np.cos(phase)
    sin = -np.sin(phase)
    alternate = np.where(np.arange(freq_count) % 2 == 0, 1.0, -1.0)
    extra = np.zeros((freq_count, 128))
    extra[:, 0] = alternate
    forward_re = np.concatenate([cos, extra], axis=1)
    cos_back = cos.T
    cos_mirror = cos_back.copy()
    cos_mirror[0] = alternate
    back_re = np.concatenate([cos_back, cos_mirror], axis=0)
    back_im = np.concatenate([sin.T, -sin.T], axis=0)
    taper = 1.0 + np.cos(np.pi * np.arange(lag_count) / lag_count)
    mirror = np.concatenate([[freq_count], lag_count - np.arange(1, freq_count)])
    weight = np.stack([taper[:freq_count], taper[mirror]]) / 8.0
    as_bf16 = lambda x: x.astype(np.float32).astype(ml_dtypes.bfloat16)
    return (
        as_bf16(forward_re),
        as_bf16(sin),
        as_bf16(back_re),
        as_bf16(back_im),
        weight.astype(np.float32),
    )


def pair_kernel(
    meta,
    pairs,
    mask,
    own,
    other,
    forward_re,
    forward_im,
    back_re,
    back_im,
    weight,
    own_grad,
    other_grad,
    misfit,
    first,
    second,
    cross_re,
    cross_im,
    adj,
    out_re,
    out_im,
):
    pair_count = misfit.shape[0]
    freq = own.shape[-1]
    part = own.shape[3] // 2
    local = own.shape[1]
    base = meta[0]
    first_part = meta[1] * part
    second_part = meta[2] * part
    core = meta[3]
    rows = part * part
    lanes = 256

    own_grad[...] = jnp.zeros_like(own_grad)
    other_grad[...] = jnp.zeros_like(other_grad)

    def work(step, carry):
        counts = []
        for k in range(GROUP):
            p = step * GROUP + k
            i = pairs[base + p, 0]
            j = pairs[base + p, 1]
            shared = jnp.int32(0)
            for w in range(2 * local):
                is_own = w < local
                source = own if is_own else other
                side = core if is_own else 1 - core
                where = side * local + w % local
                m = mask[where, i] * mask[where, j]
                shared = shared + m
                m = m.astype(jnp.float32)
                for c in range(2):
                    at = k * 4 * local + w * 2 + c
                    first[at] = source[i, w % local, c, pl.ds(first_part, part)].astype(jnp.float32) * m
                    second[at] = source[j, w % local, c, pl.ds(second_part, part)].astype(jnp.float32) * m
            counts.append(jnp.maximum(shared, 1).astype(jnp.float32) * (2.0 * freq))
            for chunk in range(freq // lanes):
                cut = pl.ds(chunk * lanes, lanes)
                right = [second[k * 4 * local + n, :, cut] for n in range(4 * local)]
                for c1 in range(part):
                    re = None
                    for w in range(2 * local):
                        a = first[k * 4 * local + 2 * w, pl.ds(c1, 1), cut]
                        b = first[k * 4 * local + 2 * w + 1, pl.ds(c1, 1), cut]
                        aa = a * right[2 * w] + b * right[2 * w + 1]
                        ab = a * right[2 * w + 1] - b * right[2 * w]
                        re = aa if re is None else re + aa
                        im = ab if w == 0 else im + ab
                    cross_re[pl.ds(k * rows + c1 * part, part), cut] = re.astype(jnp.bfloat16)
                    cross_im[pl.ds(k * rows + c1 * part, part), cut] = im.astype(jnp.bfloat16)

        cos_sum = jnp.dot(cross_re[...], forward_re[...], preferred_element_type=jnp.float32)
        sin_sum = jnp.dot(cross_im[...], forward_im[...], preferred_element_type=jnp.float32)
        lane = lax.broadcasted_iota(jnp.int32, (rows, freq), 1)
        for k in range(GROUP):
            cut = slice(k * rows, (k + 1) * rows)
            scale = 0.5 * lax.rsqrt(jnp.full((1, freq), counts[k], jnp.float32))
            even = cos_sum[cut, :freq] * scale
            odd = sin_sum[cut] * (3.0 * scale)
            middle = cos_sum[cut, freq : freq + 1] * scale
            plus = even + odd
            minus = jnp.where(lane == 0, middle, even - odd)
            plus_adj = plus * plus * plus * weight[0:1, :]
            minus_adj = minus * minus * minus * weight[1:2, :]
            adj[cut, :freq] = plus_adj.astype(jnp.bfloat16)
            adj[cut, freq:] = minus_adj.astype(jnp.bfloat16)
            total = plus_adj * plus + minus_adj * minus
            misfit[pl.ds(step * GROUP + k, 1), :] = jnp.sum(total, axis=0, keepdims=True)
        g_sum = jnp.dot(adj[...], back_re[...], preferred_element_type=jnp.float32)
        h_sum = jnp.dot(adj[...], back_im[...], preferred_element_type=jnp.float32)
        for k in range(GROUP):
            cut = slice(k * rows, (k + 1) * rows)
            scale = lax.rsqrt(jnp.full((1, freq), counts[k] * (4.0 * part), jnp.float32))
            g_out = (g_sum[cut] * scale).astype(jnp.bfloat16).astype(jnp.float32)
            h_out = (h_sum[cut] * scale).astype(jnp.bfloat16).astype(jnp.float32)
            for chunk in range(freq // 128):
                out_re[chunk, cut] = g_out[:, chunk * 128 : (chunk + 1) * 128]
                out_im[chunk, cut] = h_out[:, chunk * 128 : (chunk + 1) * 128]

        for k in range(GROUP):
            p = step * GROUP + k
            i = pairs[base + p, 0]
            j = pairs[base + p, 1]
            at = k * 4 * local
            for chunk in range(freq // 128):
                cut = pl.ds(chunk * 128, 128)
                to_second = [None] * (4 * local)
                to_first = [None] * (4 * local)
                add = lambda total, term: term if total is None else total + term
                for c in range(part):
                    g = out_re[chunk, pl.ds(k * rows + c * part, part)]
                    h = out_im[chunk, pl.ds(k * rows + c * part, part)]
                    for w in range(2 * local):
                        a = first[at + 2 * w, pl.ds(c, 1), cut]
                        b = first[at + 2 * w + 1, pl.ds(c, 1), cut]
                        to_second[2 * w] = add(to_second[2 * w], g * a - h * b)
                        to_second[2 * w + 1] = add(to_second[2 * w + 1], g * b + h * a)
                for w in range(2 * local):
                    target = own_grad if w < local else other_grad
                    for c in range(2):
                        target[j, w % local, c, pl.ds(second_part, part), cut] += to_second[2 * w + c]
                for c in range(part):
                    g = out_re[chunk, pl.ds(k * rows + c, part, stride=part)]
                    h = out_im[chunk, pl.ds(k * rows + c, part, stride=part)]
                    for w in range(2 * local):
                        a = second[at + 2 * w, pl.ds(c, 1), cut]
                        b = second[at + 2 * w + 1, pl.ds(c, 1), cut]
                        to_first[2 * w] = add(to_first[2 * w], g * a + h * b)
                        to_first[2 * w + 1] = add(to_first[2 * w + 1], g * b - h * a)
                for w in range(2 * local):
                    target = own_grad if w < local else other_grad
                    for c in range(2):
                        target[i, w % local, c, pl.ds(first_part, part), cut] += to_first[2 * w + c]
        return carry

    lax.fori_loop(0, pair_count // GROUP, work, 0)


def per_device(spectra, block_pairs, owners, window_mask):
    blk_count = lax.axis_size("blk")
    win_count = lax.axis_size("win")
    blk_index = lax.axis_index("blk")
    core = lax.axis_index("win")
    local = spectra.shape[0]
    channels = spectra.shape[3]
    freq = spectra.shape[4]
    part = channels // PARTS
    pair_total = block_pairs.shape[0]
    teams = blk_count // TEAM
    pair_count = pair_total // teams
    rank = blk_index % TEAM
    team = blk_index // TEAM

    pieces = spectra[:, 0].reshape(local, 2, PARTS, part, freq)
    outgoing = jnp.stack(
        [jnp.stack([pieces[:, :, s] for s in SUBSETS[r]], axis=2) for r in range(TEAM)]
    ).reshape(TEAM, local, 2, 2 * part, freq)
    outgoing = jnp.tile(outgoing, (teams, 1, 1, 1, 1))
    own = lax.all_to_all(outgoing, "blk", split_axis=0, concat_axis=0, tiled=True)
    swap = [(0, 1), (1, 0)]
    other = lax.ppermute(own, "win", swap)

    same = (rank == 0) | (rank == TEAM - 1)
    meta = jnp.stack(
        [team * pair_count, core, jnp.where(same, core, 1 - core), core]
    ).astype(jnp.int32)
    forward_re, forward_im, back_re, back_im, weight = tables(freq)
    smem = pl.BlockSpec(memory_space=pltpu.SMEM)
    vmem = pl.BlockSpec(memory_space=pltpu.VMEM)
    grad_type = jax.ShapeDtypeStruct((blk_count, local, 2, 2 * part, freq), jnp.float32)
    rows = part * part * GROUP
    grad_bytes = math.prod(grad_type.shape) * 4
    own_grad, other_grad, misfit = pl.pallas_call(
        pair_kernel,
        out_shape=(grad_type, grad_type, jax.ShapeDtypeStruct((pair_count, freq), jnp.float32)),
        in_specs=[smem] * 3 + [vmem] * 7,
        out_specs=(vmem, vmem, vmem),
        scratch_shapes=[
            pltpu.VMEM((GROUP * 4 * local, part, freq), jnp.float32),
            pltpu.VMEM((GROUP * 4 * local, part, freq), jnp.float32),
            pltpu.VMEM((rows, freq), jnp.bfloat16),
            pltpu.VMEM((rows, freq), jnp.bfloat16),
            pltpu.VMEM((rows, 2 * freq), jnp.bfloat16),
            pltpu.VMEM((freq // 128, rows, 128), jnp.float32),
            pltpu.VMEM((freq // 128, rows, 128), jnp.float32),
        ],
        compiler_params=pltpu.CompilerParams(vmem_limit_bytes=(16 << 20) + 3 * grad_bytes),
    )(
        meta,
        block_pairs,
        window_mask,
        own,
        other,
        forward_re,
        forward_im,
        back_re,
        back_im,
        weight,
    )

    came = lax.ppermute(other_grad.astype(jnp.bfloat16), "win", swap)
    terms = jnp.sum(misfit, axis=1)
    terms = terms + lax.ppermute(terms, "win", swap)
    chip_grad = (own_grad + came.astype(jnp.float32)).astype(jnp.bfloat16)
    high = terms.astype(jnp.bfloat16)
    low = (terms - high.astype(jnp.float32)).astype(jnp.bfloat16)
    note = jnp.zeros((8, freq), jnp.bfloat16).at[0, :pair_count].set(high).at[1, :pair_count].set(low)
    grad_rows = local * 2 * 2 * part
    payload = jnp.concatenate(
        [
            chip_grad.reshape(blk_count, grad_rows, freq),
            jnp.broadcast_to(note[None], (blk_count, 8, freq)),
        ],
        axis=1,
    )
    arrived = lax.all_to_all(payload, "blk", split_axis=0, concat_axis=0, tiled=True)
    wide = arrived[:, :grad_rows].reshape(teams, TEAM, local, 2, 2, part, freq).astype(jnp.float32)
    wide = jnp.sum(wide, axis=0)
    gradient = jnp.stack(
        [
            sum(wide[r, :, :, SUBSETS[r].index(s)] for r in range(TEAM) if s in SUBSETS[r])
            for s in range(PARTS)
        ],
        axis=2,
    )
    gradient = gradient.reshape(local, 1, 2, channels, freq).astype(jnp.bfloat16)
    notes = arrived[:, grad_rows:, :pair_count].astype(jnp.float32)
    notes = jnp.sum((notes[:, 0] + notes[:, 1]).reshape(teams, TEAM, pair_count), axis=1)
    pair_misfit = notes.reshape(pair_total) / (channels * channels * 2.0 * freq)

    owner_ids = owners[:, 0]
    order = jnp.arange(pair_total, dtype=jnp.int32)
    earlier = (owner_ids[:, None] == owner_ids[None, :]) & (order[None, :] < order[:, None])
    slot = owner_ids * CAP + jnp.sum(earlier.astype(jnp.int32), axis=1)
    mine = blk_index * CAP + jnp.arange(CAP, dtype=jnp.int32)
    totals = jnp.sum(jnp.where(slot[None, :] == mine[:, None], pair_misfit[None, :], 0.0), axis=1)
    return (gradient, totals)


def solution(mesh):
    return jax.shard_map(
        per_device,
        mesh=mesh,
        in_specs=(
            P("win", ("groups", "blk"), None, None, None),
            P("groups", None),
            P("groups", None),
            P(None, "groups"),
        ),
        out_specs=(P("win", ("groups", "blk"), None, None, None), P(("groups", "blk"))),
        check_vma=False,
    )
```

profile of v0, /device:TPU:0, one launch (start us, length us, event | category | flops | bytes accessed | tf_op | source)
XLA Modules:
  0.0 71.9 jit_solution(1219480953873066555)
XLA Ops:
  0.6 0.0 copy-start.7
  0.6 0.9 %fusion.23 = bf16[8,2,2,16,512]{4,3,2,1,0:T(8,128)(2,1)S(1)} fusion(bf16[2,2,4,8,512]{4,3,2,1,0:T(8,128)(2,1)} %bitcast.173), kind=kLoop, calls=%fused_computation.48 | loop fusion | bytes 131072
  1.6 0.0 copy-start.1
  1.6 0.9 %fusion.33 = (bf16[2,2,1,8,512]{4,3,2,1,0:T(8,128)(2,1)S(1)}, bf16[2,2,1,8,512]{4,3,2,1,0:T(8,128)(2,1)S(1)}, bf16[2,2,1,8,512]{4,3,2,1,0:T(8,128)(2,1)S(1)}, bf16[2,2,1,8,512]{4,3,2,1,0:T(8,128)(2,1)S(1)}) fusion(bf16[2,2,4,8,512]{4,3,2,1,0:T(8,128)(2,1)} %bitcast.174), kind=kLoop, calls=%fused_computation.69 | loop fusion | bytes 262144 | tf_op jit(solution)/shard_map/slice | solution.py:205
  2.5 0.0 copy-start.8
  2.5 0.0 copy-start
  2.5 0.0 copy-start.5
  2.5 0.0 copy-start.6
  2.5 0.9 %fusion.24 = bf16[8,2,2,16,512]{4,3,2,1,0:T(8,128)(2,1)S(1)} fusion(bf16[8,2,2,16,512]{4,3,2,1,0:T(8,128)(2,1)S(1)} %fusion.23, bf16[2,2,4,8,512]{4,3,2,1,0:T(8,128)(2,1)} %bitcast.175), kind=kLoop, calls=%fused_computation.49 | loop fusion | bytes 131072
  3.5 0.9 %fusion.22 = bf16[8,2,2,16,512]{4,3,2,1,0:T(8,128)(2,1)S(1)} fusion(bf16[8,2,2,16,512]{4,3,2,1,0:T(8,128)(2,1)S(1)} %fusion.5, bf16[2,2,4,8,512]{4,3,2,1,0:T(8,128)(2,1)} %bitcast.176), kind=kLoop, calls=%fused_computation.46 | loop fusion | bytes 131072
  4.3 0.0 copy-done.7
  4.4 21.6 %all_to_all.10.own = bf16[8,2,2,16,512]{4,3,2,1,0:T(8,128)(2,1)S(1)} all-to-all(bf16[8,2,2,16,512]{4,3,2,1,0:T(8,128)(2,1)S(1)} %fusion.26), channel_id=1, replica_groups=mesh['groups'=2,'blk'=8,'win'=2] {'blk'}, dimensions={0} | all-to-all | bytes 1048576 | tf_op jit(solution)/shard_map/all_to_all | solution.py:208
  26.0 0.0 collective-permute-start
  26.0 0.0 copy-done.8
  26.0 0.1 copy.28.pairs
  26.0 0.1 pad_add_fusion.meta
  26.1 1.7 %collective-permute-done.other = bf16[8,2,2,16,512]{4,3,2,1,0:T(8,128)(2,1)S(1)} collective-permute-done((bf16[8,2,2,16,512]{4,3,2,1,0:T(8,128)(2,1)S(1)}, bf16[8,2,2,16,512]{4,3,2,1,0:T(8,128)(2,1)S(1)}, u32[]{:S(2)}, u32[]{:S(2)}) %collective-permute-start) | collective-permute-done | bytes 524320 | tf_op jit(solution)/shard_map/ppermute | solution.py:210
  27.9 0.0 copy-done.1
  27.9 0.0 copy-done
  27.9 0.0 copy-done.5
  27.9 0.0 copy-done.6
  27.9 0.0 copy-start.3
  27.9 1.1 %copy-done.3 = bf16[512,640]{1,0:T(8,128)(2,1)S(1)} copy-done((bf16[512,640]{1,0:T(8,128)(2,1)S(1)}, bf16[512,640]{1,0:T(8,128)(2,1)}, u32[]{:S(2)}) %copy-start.3) | copy-done | bytes 655384
  29.0 0.0 copy-start.4
  29.0 1.0 %copy-done.4 = bf16[512,512]{1,0:T(8,128)(2,1)S(1)} copy-done((bf16[512,512]{1,0:T(8,128)(2,1)S(1)}, bf16[512,512]{1,0:T(8,128)(2,1)}, u32[]{:S(2)}) %copy-start.4) | copy-done | bytes 524312
  30.0 14.8 %shard_map.104 = (f32[8,2,2,16,512]{4,3,2,1,0:T(8,128)S(1)}, f32[8,2,2,16,512]{4,3,2,1,0:T(8,128)S(1)}, f32[16,512]{1,0:T(8,128)S(1)}) custom-call(s32[4]{0:T(128)S(1)} %pad_add_fusion.meta, s32[16,2]{1,0:T(8,128)S(1)} %copy.28.pairs, s32[4,8]{1,0:T(4,128)S(1)} %copy-done.6, bf16[8,2,2,16,512]{4,3,2,1,0:T(8,128)(2,1)S(1)} %all_to_all.10.own, ...), custom_call_target="tpu_custom_call" | custom-call | tf_op jit(solution)/shard_map/pallas_call | solution.py:222
  44.8 0.0 copy-start.2
  44.8 0.1 convert_element_type.45
  44.9 0.9 %copy-done.2 = f32[8,2,2,16,512]{4,3,2,1,0:T(8,128)} copy-done((f32[8,2,2,16,512]{4,3,2,1,0:T(8,128)}, f32[8,2,2,16,512]{4,3,2,1,0:T(8,128)S(1)}, u32[]{:S(2)}) %copy-start.2) | copy-done | bytes 1048600
  45.8 0.2 collective-permute-start.1
  46.0 0.1 reduce_sum.40
  46.1 0.3 collective-permute-start.2
  46.5 1.2 %collective-permute-done.2 = f32[16]{0:T(128)S(1)} collective-permute-done((f32[16]{0:T(128)S(1)}, f32[16]{0:T(128)S(1)}, u32[]{:S(2)}, u32[]{:S(2)}) %collective-permute-start.2) | collective-permute-done | bytes 96 | tf_op jit(solution)/shard_map/ppermute | solution.py:252
  47.7 0.2 scatter.9
  47.9 0.0 collective-permute-done.1
  47.9 1.4 %add_convert_fusion = bf16[8,2,2,16,512]{4,3,2,1,0:T(8,128)(2,1)S(1)} fusion(f32[8,2,2,16,512]{4,3,2,1,0:T(8,128)} %copy-done.2, bf16[8,2,2,16,512]{4,3,2,1,0:T(8,128)(2,1)S(1)} %collective-permute-done.1), kind=kLoop, calls=%fused_computation | loop fusion | flops 786432 | bytes 2097152 | tf_op jit(solution)/shard_map/convert_element_type | solution.py:253
  49.3 0.0 copy-start.9
  49.3 0.9 %pad_maximum_fusion = bf16[8,72,512]{2,1,0:T(8,128)(2,1)} fusion(bf16[8,8,512]{2,1,0:T(8,128)(2,1)S(1)} %broadcast_in_dim.13, bf16[8,64,512]{2,1,0:T(8,128)(2,1)S(1)} %bitcast.172), kind=kLoop, calls=%fused_computation.1 | loop fusion | flops 1179648 | bytes 1179648 | tf_op jit(solution)/shard_map/concatenate | solution.py:258
  50.2 3.6 %all-to-all-start.1 = ((bf16[8,72,512]{2,1,0:T(8,128)(2,1)}), bf16[8,72,512]{2,1,0:T(8,128)(2,1)S(1)}, u32[]{:S(2)}, u32[]{:S(2)}) async-start(bf16[8,72,512]{2,1,0:T(8,128)(2,1)} %pad_maximum_fusion), calls=%async_computation.1 | async-start | bytes 1179648 | tf_op jit(solution)/shard_map/all_to_all | solution.py:265
  53.8 0.0 copy-done.9
  53.8 0.2 convert_reduce_fusion
  54.0 16.2 %all-to-all-done.1 = bf16[8,72,512]{2,1,0:T(8,128)(2,1)S(1)} async-done(((bf16[8,72,512]{2,1,0:T(8,128)(2,1)}), bf16[8,72,512]{2,1,0:T(8,128)(2,1)S(1)}, u32[]{:S(2)}, u32[]{:S(2)}) %all-to-all-start.1) | async-done | bytes 589856 | tf_op jit(solution)/shard_map/all_to_all | solution.py:265
  70.3 0.1 convert.21
  70.4 0.1 fusion.27
  70.5 0.7 select_reduce_fusion
  71.2 0.7 maximum_bitcast_fusion
  (14 shorter events, 0.1 us)
Async XLA Ops:
  0.6 3.7 %copy-start.7 = (bf16[2,1,2,32,512]{4,3,2,1,0:T(8,128)(2,1)S(1)}, bf16[2,1,2,32,512]{4,3,2,1,0:T(8,128)(2,1)}, u32[]{:S(2)}) copy-start(bf16[2,1,2,32,512]{4,3,2,1,0:T(8,128)(2,1)} %param.13) | copy-start | bytes 393220
  1.6 26.3 %copy-start.1 = (bf16[1024,512]{1,0:T(8,128)(2,1)S(1)}, bf16[1024,512]{1,0:T(8,128)(2,1)}, u32[]{:S(2)}) copy-start(bf16[1024,512]{1,0:T(8,128)(2,1)} %constant.115.clone.back_im) | copy-start | bytes 3145732
  2.5 23.5 %copy-start.8 = (s32[16,2]{0,1:T(2,128)S(1)}, s32[16,2]{0,1:T(2,128)}, u32[]{:S(2)}) copy-start(s32[16,2]{0,1:T(2,128)} %param.14) | copy-start | bytes 388
  2.5 25.4 %copy-start = (bf16[1024,512]{1,0:T(8,128)(2,1)S(1)}, bf16[1024,512]{1,0:T(8,128)(2,1)}, u32[]{:S(2)}) copy-start(bf16[1024,512]{1,0:T(8,128)(2,1)} %constant.114.clone.back_re) | copy-start | bytes 3145732
  2.5 25.4 %copy-start.5 = (f32[2,512]{1,0:T(2,128)S(1)}, f32[2,512]{1,0:T(2,128)}, u32[]{:S(2)}) copy-start(f32[2,512]{1,0:T(2,128)} %constant.116.clone.weight) | copy-start | bytes 12292
  2.5 25.4 %copy-start.6 = (s32[4,8]{1,0:T(4,128)S(1)}, s32[4,8]{1,0:T(4,128)}, u32[]{:S(2)}) copy-start(s32[4,8]{1,0:T(4,128)} %mask.1) | copy-start | bytes 388
  26.0 1.9 %collective-permute-start = (bf16[8,2,2,16,512]{4,3,2,1,0:T(8,128)(2,1)S(1)}, bf16[8,2,2,16,512]{4,3,2,1,0:T(8,128)(2,1)S(1)}, u32[]{:S(2)}, u32[]{:S(2)}) collective-permute-start(bf16[8,2,2,16,512]{4,3,2,1,0:T(8,128)(2,1)S(1)} %all_to_all.10.own), channel_id=1, source_target_pairs={{0,1},{1,0},{2,3},{3,2},{4,5},{5,4},{6,7},{7,6},{8,9},{9,8},{10,11... | collective-permute-start | bytes 1572872 | tf_op jit(solution)/shard_map/ppermute | solution.py:210
  27.9 1.1 %copy-start.3 = (bf16[512,640]{1,0:T(8,128)(2,1)S(1)}, bf16[512,640]{1,0:T(8,128)(2,1)}, u32[]{:S(2)}) copy-start(bf16[512,640]{1,0:T(8,128)(2,1)} %constant.112.clone.forward_re) | copy-start | bytes 1966084
  29.0 1.0 %copy-start.4 = (bf16[512,512]{1,0:T(8,128)(2,1)S(1)}, bf16[512,512]{1,0:T(8,128)(2,1)}, u32[]{:S(2)}) copy-start(bf16[512,512]{1,0:T(8,128)(2,1)} %constant.113.clone.forward_im) | copy-start | bytes 1572868
  44.8 1.0 %copy-start.2 = (f32[8,2,2,16,512]{4,3,2,1,0:T(8,128)}, f32[8,2,2,16,512]{4,3,2,1,0:T(8,128)S(1)}, u32[]{:S(2)}) copy-start(f32[8,2,2,16,512]{4,3,2,1,0:T(8,128)S(1)} %get-tuple-element.29) | copy-start | bytes 3145732
  45.8 2.1 %collective-permute-start.1 = (bf16[8,2,2,16,512]{4,3,2,1,0:T(8,128)(2,1)S(1)}, bf16[8,2,2,16,512]{4,3,2,1,0:T(8,128)(2,1)S(1)}, u32[]{:S(2)}, u32[]{:S(2)}) collective-permute-start(bf16[8,2,2,16,512]{4,3,2,1,0:T(8,128)(2,1)S(1)} %convert_element_type.45), channel_id=1, source_target_pairs={{0,1},{1,0},{2,3},{3,2},{4,5},{5,4},{6,7},{7,6},{8,9},{9,8},{10,11... | collective-permute-start | bytes 1572872 | tf_op jit(solution)/shard_map/ppermute | solution.py:250
  46.1 1.6 %collective-permute-start.2 = (f32[16]{0:T(128)S(1)}, f32[16]{0:T(128)S(1)}, u32[]{:S(2)}, u32[]{:S(2)}) collective-permute-start(f32[16]{0:T(128)S(1)} %reduce_sum.40), channel_id=1, source_target_pairs={{0,1},{1,0},{2,3},{3,2},{4,5},{5,4},{6,7},{7,6},{8,9},{9,8},{10,11... | collective-permute-start | bytes 200 | tf_op jit(solution)/shard_map/ppermute | solution.py:252
  49.3 4.5 %copy-start.9 = (s32[16,1]{0,1:T(1,128)S(1)}, s32[16,1]{0,1:T(1,128)}, u32[]{:S(2)}) copy-start(s32[16,1]{0,1:T(1,128)} %param.15) | copy-start | bytes 196
  50.2 20.0 %all-to-all-start.1 = ((bf16[8,72,512]{2,1,0:T(8,128)(2,1)}), bf16[8,72,512]{2,1,0:T(8,128)(2,1)S(1)}, u32[]{:S(2)}, u32[]{:S(2)}) async-start(bf16[8,72,512]{2,1,0:T(8,128)(2,1)} %pad_maximum_fusion), calls=%async_computation.1 | async-start | bytes 1179648 | tf_op jit(solution)/shard_map/all_to_all | solution.py:265
where the time goes:
time: 72.3 us; the launch traced here: 71.9 us
  blocking collectives  21.6 us (30%)
  waiting for transfers between devices  19.2 us (27%)
  Pallas kernels  14.8 us (20%)
  local copies, waits for them, and re-layouts  6.96 us (10%)
  other arithmetic  4.34 us (6%)
  starting transfers between devices  4.16 us (6%)
  between operations  0.85 us (1%)
    all_to_all x1, blocking collectives, per_device(): lax.all_to_all(outgoing, 'blk', split_axis=0, concat_axis=0, tiled=True)  21.6 us
    all_to_all x1, waiting for transfers between devices, per_device(): lax.all_to_all(payload, 'blk', split_axis=0, concat_axis=0, tiled=True)  16.2 us
    pallas_call x1, Pallas kernels, per_device(): pl.pallas_call(pair_kernel, out_shape=(grad_type, grad_type, jax.ShapeDty...  14.8 us
    unnamed x25, local copies, waits for them, and re-layouts  5.83 us
    all_to_all x1, starting transfers between devices, per_device(): lax.all_to_all(payload, 'blk', split_axis=0, concat_axis=0, tiled=True)  3.59 us
    ppermute x1, waiting for transfers between devices, per_device(): other = lax.ppermute(own, 'win', swap)  1.74 us
  transfers between devices with their start and end apart: 4, of which 3 were waited for; matrix products, arithmetic and copies ran while one was open for 1% of the time, Pallas kernels for 0%

commit v1 on v0

v1 whole, which is shorter than its diff:
```python
import functools
import math

import jax
import jax.numpy as jnp
import ml_dtypes
import numpy as np
from jax import lax
from jax.experimental import pallas as pl
from jax.experimental.pallas import tpu as pltpu
from jax.sharding import PartitionSpec as P

CAP = 3
PARTS = 4
TEAM = 8
SUBSETS = ((0, 1), (0, 1), (0, 2), (0, 3), (1, 2), (1, 3), (2, 3), (2, 3))
GROUP = 4
HOPS = ((6, 4, 2, 0), (7, 5, 3, 1))


@functools.lru_cache(maxsize=None)
def tables(freq_count):
    lag_count = 2 * freq_count
    f = np.arange(freq_count)[:, None]
    t = np.arange(freq_count)[None, :]
    phase = (f * t % lag_count) * (2.0 * np.pi / lag_count)
    cos = np.cos(phase)
    sin = -np.sin(phase)
    alternate = np.where(np.arange(freq_count) % 2 == 0, 1.0, -1.0)
    extra = np.zeros((freq_count, 128))
    extra[:, 0] = alternate
    forward_re = np.concatenate([cos, extra], axis=1)
    cos_back = cos.T
    cos_mirror = cos_back.copy()
    cos_mirror[0] = alternate
    back_re = np.concatenate([cos_back, cos_mirror], axis=0)
    back_im = np.concatenate([sin.T, -sin.T], axis=0)
    taper = 1.0 + np.cos(np.pi * np.arange(lag_count) / lag_count)
    mirror = np.concatenate([[freq_count], lag_count - np.arange(1, freq_count)])
    weight = np.stack([taper[:freq_count], taper[mirror]]) / 8.0
    as_bf16 = lambda x: x.astype(np.float32).astype(ml_dtypes.bfloat16)
    return (
        as_bf16(forward_re),
        as_bf16(sin),
        as_bf16(back_re),
        as_bf16(back_im),
        weight.astype(np.float32),
    )


@functools.lru_cache(maxsize=None)
def positions():
    out = np.zeros((TEAM, 2, 20), np.int32)
    for rank in range(TEAM):
        for core in range(2):
            same = rank in (0, TEAM - 1)
            row = [0, core, core if same else 1 - core, core]
            row += [rank ^ hop for hop in HOPS[core]]
            row += [rank ^ hop for hop in HOPS[1 - core]]
            for hop in HOPS[core]:
                row += SUBSETS[rank ^ hop]
            out[rank, core] = row
    return out


def pack_kernel(meta, own, other, *refs):
    parcels, wide = refs[:-1], refs[-1]
    local = own.shape[0]
    core = meta[3]
    for source, side in ((own, core), (other, 1 - core)):
        for w in range(local):
            for c in range(2):
                wide[...] = source[w, 0, c].astype(jnp.float32).reshape(wide.shape)
                for r, parcel in enumerate(parcels):
                    both = [wide[meta[12 + 2 * r + n]] for n in range(2)]
                    parcel[side * local + w, c] = jnp.concatenate(both, axis=0).astype(jnp.bfloat16)


def add_kernel(keep, came, terms, *parcels):
    count = len(parcels)
    rows = keep.shape[0] // count
    pair_count = terms.shape[0]
    half = pair_count // 2
    arrived = came[count * rows :].astype(jnp.float32)
    total = terms[...] + jnp.concatenate(
        [arrived[:, :128] + arrived[:, 256:384], arrived[:, 128:256] + arrived[:, 384:512]], axis=0
    )
    note = note_of(total, half)
    for r, parcel in enumerate(parcels):
        cut = slice(r * rows, (r + 1) * rows)
        parcel[:rows] = (keep[cut] + came[cut].astype(jnp.float32)).astype(jnp.bfloat16)
        parcel[rows:] = note


def note_of(total, half):
    high = total.astype(jnp.bfloat16).astype(jnp.float32)
    low = total - high
    return jnp.concatenate([high[:half], high[half:], low[:half], low[half:]], axis=1).astype(
        jnp.bfloat16
    )


def merge_kernel(meta, *refs):
    parcels, (mine, give, total) = refs[: len(HOPS[0])], refs[len(HOPS[0]) :]
    windows, _, _, part, freq = total.shape
    channels = PARTS * part
    local = windows // 2
    core = meta[3]
    rows = windows * 2 * 2 * part
    note = None
    total[...] = jnp.zeros_like(total)
    for r, parcel in enumerate(parcels):
        for w in range(windows):
            for c in range(2):
                for n in range(2):
                    start = ((w * 2 + c) * 2 + n) * part
                    term = parcel[start : start + part].astype(jnp.float32)
                    total[w, c, meta[12 + 2 * r + n]] += term
        tail = parcel[rows:].astype(jnp.float32)
        tail = jnp.concatenate(
            [tail[:, :128] + tail[:, 256:384], tail[:, 128:256] + tail[:, 384:512]], axis=0
        )
        note = tail if note is None else note + tail
    for w in range(local):
        for c in range(2):
            to = slice((w * 2 + c) * channels, (w * 2 + c + 1) * channels)
            mine[to] = total[core * local + w, c].reshape(channels, freq)
            give[to] = total[(1 - core) * local + w, c].reshape(channels, freq)
    body = local * 2 * channels
    pad = jnp.zeros((note.shape[0], freq - 128), jnp.float32)
    mine[body:] = jnp.concatenate([note, pad], axis=1)
    give[body:] = jnp.concatenate([note, pad], axis=1)


def finish_kernel(mine, came, chosen, gradient, totals, scale):
    local, _, _, channels, _ = gradient.shape
    for w in range(local):
        for c in range(2):
            cut = slice((w * 2 + c) * channels, (w * 2 + c + 1) * channels)
            gradient[w, 0, c] = (mine[cut] + came[cut]).astype(jnp.bfloat16)
    body = local * 2 * channels
    note = mine[body:, :128] + came[body:, :128]
    pair = jnp.sum(note, axis=1, keepdims=True) * scale
    totals[...] = jnp.sum(pair * chosen[...], axis=0, keepdims=True)


def pair_kernel(
    direct,
    pair_count,
    meta,
    pairs,
    mask,
    *refs,
):
    sources = 2 * len(HOPS[0]) if direct else 2
    came, refs = refs[:sources], refs[sources:]
    (
        forward_re_hbm,
        forward_im_hbm,
        back_re_hbm,
        back_im_hbm,
        weight,
        own_grad,
        other_grad,
        misfit,
        first,
        second,
        cross_re,
        cross_im,
        adj,
        out_re,
        out_im,
        forward_re,
        forward_im,
        back_re,
        back_im,
        sems,
    ) = refs[:20]
    copies = [
        pltpu.make_async_copy(source, target, sems.at[n])
        for n, (source, target) in enumerate(
            (
                (forward_re_hbm, forward_re),
                (forward_im_hbm, forward_im),
                (back_re_hbm, back_re),
                (back_im_hbm, back_im),
            )
        )
    ]
    for copy in copies:
        copy.start()
    freq = came[0].shape[-1]
    part = came[0].shape[-2] // 2
    local = mask.shape[0] // 2
    base = meta[0]
    first_part = meta[1]
    second_part = meta[2]
    core = meta[3]
    rows = part * part
    lanes = 256

    if direct:
        field, grad = refs[20:]
        for n, parcel in enumerate(came):
            index = meta[4 + n]
            for w in range(2 * local):
                m = mask[w, index].astype(jnp.float32)
                for c in range(2):
                    field[index, w, c] = (parcel[w, c].astype(jnp.float32) * m).reshape(2, part, freq)
        grad[...] = jnp.zeros_like(grad)
    else:
        own_grad[...] = jnp.zeros_like(own_grad)
        other_grad[...] = jnp.zeros_like(other_grad)

    def block(index, w, c, which):
        both = came[w // local][index, w % local, c].astype(jnp.float32)
        return jnp.where(which == 0, both[:part], both[part:])

    def first_row(k, i, w, c, row, cut):
        if direct:
            return field[i, w, c, first_part, pl.ds(row, 1), cut]
        return first[(k * 2 * local + w) * 2 + c, pl.ds(row, 1), cut]

    def second_row(k, j, w, c, row, cut):
        if direct:
            return field[j, w, c, second_part, pl.ds(row, 1), cut]
        return second[(k * 2 * local + w) * 2 + c, pl.ds(row, 1), cut]

    def add_to(index, w, c, which, cut, term):
        if direct:
            grad[index, w, c, which, :, cut] += term
        else:
            target = own_grad if w < local else other_grad
            target[index, w % local, c, pl.ds(which * part, part), cut] += term

    def work(step, carry):
        counts = []
        for k in range(GROUP):
            p = step * GROUP + k
            i = pairs[base + p, 0]
            j = pairs[base + p, 1]
            shared = jnp.int32(0)
            for w in range(2 * local):
                side = core if w < local else 1 - core
                where = w if direct else side * local + w % local
                m = mask[where, i] * mask[where, j]
                shared = shared + m
                if direct:
                    continue
                m = m.astype(jnp.float32)
                for c in range(2):
                    at = k * 4 * local + w * 2 + c
                    first[at] = block(i, w, c, first_part) * m
                    second[at] = block(j, w, c, second_part) * m
            counts.append(jnp.maximum(shared, 1).astype(jnp.float32) * (2.0 * freq))
            for chunk in range(freq // lanes):
                cut = pl.ds(chunk * lanes, lanes)
                if direct:
                    right = [field[j, n // 2, n % 2, second_part, :, cut] for n in range(4 * local)]
                else:
                    right = [second[k * 4 * local + n, :, cut] for n in range(4 * local)]
                for c1 in range(part):
                    re = None
                    for w in range(2 * local):
                        a = first_row(k, i, w, 0, c1, cut)
                        b = first_row(k, i, w, 1, c1, cut)
                        aa = a * right[2 * w] + b * right[2 * w + 1]
                        ab = a * right[2 * w + 1] - b * right[2 * w]
                        re = aa if re is None else re + aa
                        im = ab if w == 0 else im + ab
                    cross_re[pl.ds(k * rows + c1 * part, part), cut] = re.astype(jnp.bfloat16)
                    cross_im[pl.ds(k * rows + c1 * part, part), cut] = im.astype(jnp.bfloat16)

        @pl.when(step == 0)
        def _():
            for copy in copies:
                copy.wait()

        cos_sum = jnp.dot(cross_re[...], forward_re[...], preferred_element_type=jnp.float32)
        sin_sum = jnp.dot(cross_im[...], forward_im[...], preferred_element_type=jnp.float32)
        lane = lax.broadcasted_iota(jnp.int32, (rows, freq), 1)
        for k in range(GROUP):
            cut = slice(k * rows, (k + 1) * rows)
            scale = 0.5 * lax.rsqrt(jnp.full((1, freq), counts[k], jnp.float32))
            even = cos_sum[cut, :freq] * scale
            odd = sin_sum[cut] * (3.0 * scale)
            middle = cos_sum[cut, freq : freq + 1] * scale
            plus = even + odd
            minus = jnp.where(lane == 0, middle, even - odd)
            plus_adj = plus * plus * plus * weight[0:1, :]
            minus_adj = minus * minus * minus * weight[1:2, :]
            adj[cut, :freq] = plus_adj.astype(jnp.bfloat16)
            adj[cut, freq:] = minus_adj.astype(jnp.bfloat16)
            total = plus_adj * plus + minus_adj * minus
            total = jnp.sum(total, axis=0, keepdims=True)
            total = sum(total[:, n : n + 128] for n in range(0, freq, 128))
            misfit[pl.ds(step * GROUP + k, 1), :] = total
        g_sum = jnp.dot(adj[...], back_re[...], preferred_element_type=jnp.float32)
        h_sum = jnp.dot(adj[...], back_im[...], preferred_element_type=jnp.float32)
        for k in range(GROUP):
            cut = slice(k * rows, (k + 1) * rows)
            scale = lax.rsqrt(jnp.full((1, freq), counts[k] * (4.0 * part), jnp.float32))
            g_out = (g_sum[cut] * scale).astype(jnp.bfloat16).astype(jnp.float32)
            h_out = (h_sum[cut] * scale).astype(jnp.bfloat16).astype(jnp.float32)
            for chunk in range(freq // 128):
                out_re[chunk, cut] = g_out[:, chunk * 128 : (chunk + 1) * 128]
                out_im[chunk, cut] = h_out[:, chunk * 128 : (chunk + 1) * 128]

        for k in range(GROUP):
            p = step * GROUP + k
            i = pairs[base + p, 0]
            j = pairs[base + p, 1]
            for chunk in range(freq // 128):
                cut = pl.ds(chunk * 128, 128)
                to_second = [None] * (4 * local)
                to_first = [None] * (4 * local)
                add = lambda total, term: term if total is None else total + term
                for c in range(part):
                    g = out_re[chunk, pl.ds(k * rows + c * part, part)]
                    h = out_im[chunk, pl.ds(k * rows + c * part, part)]
                    for w in range(2 * local):
                        a = first_row(k, i, w, 0, c, cut)
                        b = first_row(k, i, w, 1, c, cut)
                        to_second[2 * w] = add(to_second[2 * w], g * a - h * b)
                        to_second[2 * w + 1] = add(to_second[2 * w + 1], g * b + h * a)
                for w in range(2 * local):
                    for c in range(2):
                        add_to(j, w, c, second_part, cut, to_second[2 * w + c])
                for c in range(part):
                    g = out_re[chunk, pl.ds(k * rows + c, part, stride=part)]
                    h = out_im[chunk, pl.ds(k * rows + c, part, stride=part)]
                    for w in range(2 * local):
                        a = second_row(k, j, w, 0, c, cut)
                        b = second_row(k, j, w, 1, c, cut)
                        to_first[2 * w] = add(to_first[2 * w], g * a + h * b)
                        to_first[2 * w + 1] = add(to_first[2 * w + 1], g * b - h * a)
                for w in range(2 * local):
                    for c in range(2):
                        add_to(i, w, c, first_part, cut, to_first[2 * w + c])
        return carry

    lax.fori_loop(0, pair_count // GROUP, work, 0)

    if direct:
        count = len(HOPS[0])
        size = 2 * part
        for n in range(2 * count):
            index = meta[4 + n]
            target = own_grad if n < count else other_grad
            for w in range(2 * local):
                m = mask[w, index].astype(jnp.float32)
                for c in range(2):
                    to = pl.ds((((n % count) * 2 * local + w) * 2 + c) * size, size)
                    term = grad[index, w, c].reshape(size, freq) * m
                    target[to] = term.astype(target.dtype)
        other_grad[count * 4 * local * size :] = note_of(misfit[...], pair_count // 2)


def per_device(spectra, block_pairs, owners, window_mask):
    blk_count = lax.axis_size("blk")
    blk_index = lax.axis_index("blk")
    core = lax.axis_index("win")
    local = spectra.shape[0]
    channels = spectra.shape[3]
    freq = spectra.shape[4]
    part = channels // PARTS
    pair_total = block_pairs.shape[0]
    teams = blk_count // TEAM
    pair_count = pair_total // teams
    direct = teams == 1
    swap = [(0, 1), (1, 0)]
    smem = pl.BlockSpec(memory_space=pltpu.SMEM)
    vmem = pl.BlockSpec(memory_space=pltpu.VMEM)
    hbm = pl.BlockSpec(memory_space=pl.ANY)
    count = len(HOPS[0])
    hop_pairs = [
        [(2 * b + c, 2 * (b ^ HOPS[c][r]) + c) for b in range(TEAM) for c in range(2)]
        for r in range(count)
    ]
    meta = jnp.asarray(positions())[blk_index % TEAM, core]
    meta = meta.at[0].set(blk_index // TEAM * pair_count)

    owner_ids = owners[:, 0]
    order = jnp.arange(pair_total, dtype=jnp.int32)
    earlier = (owner_ids[:, None] == owner_ids[None, :]) & (order[None, :] < order[:, None])
    slot = owner_ids * CAP + jnp.sum(earlier.astype(jnp.int32), axis=1)
    mine_slots = blk_index * CAP + jnp.arange(CAP, dtype=jnp.int32)
    chosen = (slot[:, None] == mine_slots[None, :]).astype(jnp.float32)
    misfit_scale = 1.0 / (channels * channels * 2.0 * freq)

    if direct:
        other = lax.ppermute(spectra, "win", swap)
        parcel_type = jax.ShapeDtypeStruct((2 * local, 2, 2 * part, freq), jnp.bfloat16)
        parcels = pl.pallas_call(
            pack_kernel,
            out_shape=(parcel_type,) * count,
            in_specs=[smem, vmem, vmem],
            out_specs=(vmem,) * count,
            scratch_shapes=[pltpu.VMEM((PARTS, part, freq), jnp.float32)],
        )(meta, spectra, other)
        landed = [
            lax.ppermute(parcel, ("blk", "win"), pairs) for parcel, pairs in zip(parcels, hop_pairs)
        ]
        came = landed + [lax.ppermute(parcel, "win", swap) for parcel in landed]
    else:
        pieces = spectra[:, 0].reshape(local, 2, PARTS, part, freq)
        outgoing = jnp.stack(
            [jnp.stack([pieces[:, :, s] for s in SUBSETS[r]], axis=2) for r in range(TEAM)]
        ).reshape(TEAM, local, 2, 2 * part, freq)
        outgoing = jnp.tile(outgoing, (teams, 1, 1, 1, 1))
        own = lax.all_to_all(outgoing, "blk", split_axis=0, concat_axis=0, tiled=True)
        came = [own, lax.ppermute(own, "win", swap)]

    table_arrays = tables(freq)
    grad_shape = (blk_count, 2 * local, 2, 2 * part, freq)
    grad_bytes = math.prod(grad_shape) * 4
    rows = part * part * GROUP
    parcel_rows = 2 * local * 2 * 2 * part
    misfit_type = jax.ShapeDtypeStruct((pair_count, 128), jnp.float32)
    scratch = [
        pltpu.VMEM((GROUP * 4 * local, part, freq), jnp.float32),
        pltpu.VMEM((GROUP * 4 * local, part, freq), jnp.float32),
        pltpu.VMEM((rows, freq), jnp.bfloat16),
        pltpu.VMEM((rows, freq), jnp.bfloat16),
        pltpu.VMEM((rows, 2 * freq), jnp.bfloat16),
        pltpu.VMEM((freq // 128, rows, 128), jnp.float32),
        pltpu.VMEM((freq // 128, rows, 128), jnp.float32),
    ]
    scratch += [pltpu.VMEM(table.shape, jnp.bfloat16) for table in table_arrays[:4]]
    scratch += [pltpu.SemaphoreType.DMA((4,))]
    if direct:
        split_shape = (blk_count, 2 * local, 2, 2, part, freq)
        scratch += [pltpu.VMEM(split_shape, jnp.float32)] * 2
        out_types = (
            jax.ShapeDtypeStruct((count * parcel_rows, freq), jnp.float32),
            jax.ShapeDtypeStruct((count * parcel_rows + pair_count // 2, freq), jnp.bfloat16),
            misfit_type,
        )
    else:
        half = jax.ShapeDtypeStruct((blk_count, local, 2, 2 * part, freq), jnp.float32)
        out_types = (half, half, misfit_type)
    own_grad, other_grad, misfit = pl.pallas_call(
        functools.partial(pair_kernel, direct, pair_count),
        out_shape=out_types,
        in_specs=[smem] * 3 + [vmem] * len(came) + [hbm] * 4 + [vmem],
        out_specs=(vmem, vmem, vmem),
        scratch_shapes=scratch,
        compiler_params=pltpu.CompilerParams(
            vmem_limit_bytes=(16 << 20) + grad_bytes * 3 // (1 if direct else 2)
        ),
    )(meta, block_pairs, window_mask, *came, *table_arrays)

    if direct:
        swapped = lax.ppermute(other_grad, "win", swap)
        parcel_type = jax.ShapeDtypeStruct((parcel_rows + pair_count // 2, freq), jnp.bfloat16)
        parcels = pl.pallas_call(
            add_kernel,
            out_shape=(parcel_type,) * count,
            in_specs=[vmem] * 3,
            out_specs=(vmem,) * count,
        )(own_grad, swapped, misfit)
        landed = [
            lax.ppermute(parcel, ("blk", "win"), pairs) for parcel, pairs in zip(parcels, hop_pairs)
        ]
        half_type = jax.ShapeDtypeStruct((local * 2 * channels + pair_count, freq), jnp.float32)
        mine, give = pl.pallas_call(
            merge_kernel,
            out_shape=(half_type, half_type),
            in_specs=[smem] + [vmem] * count,
            out_specs=(vmem, vmem),
            scratch_shapes=[pltpu.VMEM((2 * local, 2, PARTS, part, freq), jnp.float32)],
        )(meta, *landed)
        swapped = lax.ppermute(give, "win", swap)
        gradient, totals = pl.pallas_call(
            functools.partial(finish_kernel, scale=misfit_scale),
            out_shape=(
                jax.ShapeDtypeStruct(spectra.shape, jnp.bfloat16),
                jax.ShapeDtypeStruct((1, CAP), jnp.float32),
            ),
            in_specs=[vmem] * 3,
            out_specs=(vmem, vmem),
        )(mine, swapped, chosen)
        return (gradient, totals.reshape(CAP))

    swapped = lax.ppermute(other_grad.astype(jnp.bfloat16), "win", swap)
    terms = jnp.sum(misfit, axis=1)
    terms = terms + lax.ppermute(terms, "win", swap)
    chip_grad = (own_grad + swapped.astype(jnp.float32)).astype(jnp.bfloat16)
    high = terms.astype(jnp.bfloat16)
    low = (terms - high.astype(jnp.float32)).astype(jnp.bfloat16)
    note = jnp.zeros((8, freq), jnp.bfloat16).at[0, :pair_count].set(high).at[1, :pair_count].set(low)
    grad_rows = local * 2 * 2 * part
    payload = jnp.concatenate(
        [
            chip_grad.reshape(blk_count, grad_rows, freq),
            jnp.broadcast_to(note[None], (blk_count, 8, freq)),
        ],
        axis=1,
    )
    arrived = lax.all_to_all(payload, "blk", split_axis=0, concat_axis=0, tiled=True)
    wide = arrived[:, :grad_rows].reshape(teams, TEAM, local, 2, 2, part, freq).astype(jnp.float32)
    wide = jnp.sum(wide, axis=0)
    gradient = jnp.stack(
        [
            sum(wide[r, :, :, SUBSETS[r].index(s)] for r in range(TEAM) if s in SUBSETS[r])
            for s in range(PARTS)
        ],
        axis=2,
    )
    gradient = gradient.reshape(local, 1, 2, channels, freq).astype(jnp.bfloat16)
    notes = arrived[:, grad_rows:, :pair_count].astype(jnp.float32)
    notes = jnp.sum((notes[:, 0] + notes[:, 1]).reshape(teams, TEAM, pair_count), axis=1)
    pair_misfit = notes.reshape(pair_total) * misfit_scale
    totals = jnp.sum(pair_misfit[:, None] * chosen, axis=0)
    return (gradient, totals)


def solution(mesh):
    return jax.shard_map(
        per_device,
        mesh=mesh,
        in_specs=(
            P("win", ("groups", "blk"), None, None, None),
            P("groups", None),
            P("groups", None),
            P(None, "groups"),
        ),
        out_specs=(P("win", ("groups", "blk"), None, None, None), P(("groups", "blk"))),
        check_vma=False,
    )
```

time: 72.3 us -> 73.4 us (1.015)
  blocking collectives: 21.6 us -> 0 us
  starting transfers between devices: 4.16 us -> 14.5 us
  Pallas kernels: 14.8 us -> 23.4 us
  local copies, waits for them, and re-layouts: 6.96 us -> 11.1 us
  other arithmetic: 4.34 us -> 0.85 us
  waiting for transfers between devices: 19.2 us -> 22.3 us
    all_to_all x1 -> x0, blocking collectives: 21.6 us -> none  [per_device(): lax.all_to_all(outgoing, 'blk', split_axis=0, concat_axis=0, tiled=True)]
    ppermute x3 -> x15, waiting for transfers between devices: 2.97 us -> 22.3 us  [the longest x8 18.7 us: per_device(): lax.ppermute(parcel, ('blk', 'win'), pairs)]
    all_to_all x1 -> x0, waiting for transfers between devices: 16.2 us -> none  [per_device(): lax.all_to_all(payload, 'blk', split_axis=0, concat_axis=0, tiled=True)]
    ppermute x3 -> x15, starting transfers between devices: 0.57 us -> 14.5 us  [the longest x8 13.1 us: per_device(): lax.ppermute(parcel, ('blk', 'win'), pairs)]
    pallas_call x1 -> x5, Pallas kernels: 14.8 us -> 23.4 us  [the longest x1 15.4 us: per_device(): pl.pallas_call(functools.partial(pair_kernel, direct, pair_count), out_sh...]
    unnamed x25 -> x39, local copies, waits for them, and re-layouts: 5.83 us -> 10.4 us
    all_to_all x1 -> x0, starting transfers between devices: 3.59 us -> none  [per_device(): lax.all_to_all(payload, 'blk', split_axis=0, concat_axis=0, tiled=True)]
    convert_element_type x5 -> x1, other arithmetic: 2.27 us -> 0.67 us  [per_device(): chosen = (slot[:, None] == mine_slots[None, :]).astype(jnp.float32)]
  transfers between devices with their start and end apart: 4 -> 15, of which waited for: 3 -> 10; matrix products, arithmetic and copies ran while one was open for 1% -> 2% of each run, Pallas kernels for 0% -> 0%
where the time goes in v1:
time: 73.4 us; the launch traced here: 72.9 us
  Pallas kernels  23.4 us (32%)
  waiting for transfers between devices  22.3 us (30%)
  starting transfers between devices  14.5 us (20%)
  local copies, waits for them, and re-layouts  11.1 us (15%)
  other arithmetic  0.85 us (1%)
    ppermute x8, waiting for transfers between devices, per_device(): lax.ppermute(parcel, ('blk', 'win'), pairs)  18.7 us
    pallas_call x1, Pallas kernels, per_device(): pl.pallas_call(functools.partial(pair_kernel, direct, pair_count), out_sh...  15.4 us
    ppermute x8, starting transfers between devices, per_device(): lax.ppermute(parcel, ('blk', 'win'), pairs)  13.1 us
    unnamed x39, local copies, waits for them, and re-layouts  10.4 us
    pallas_call x1, Pallas kernels, per_device(): pl.pallas_call(add_kernel, out_shape=(parcel_type,) * count, in_specs=[vm...  2.22 us
    pallas_call x1, Pallas kernels, per_device(): pl.pallas_call(merge_kernel, out_shape=(half_type, half_type), in_specs=[...  2.17 us
    pallas_call x1, Pallas kernels, per_device(): pl.pallas_call(pack_kernel, out_shape=(parcel_type,) * count, in_specs=[s...  1.89 us
    pallas_call x1, Pallas kernels, per_device(): pl.pallas_call(functools.partial(finish_kernel, scale=misfit_scale), out_...  1.74 us
  transfers between devices with their start and end apart: 15, of which 10 were waited for; matrix products, arithmetic and copies ran while one was open for 2% of the time, Pallas kernels for 0%

profile of v1, /device:TPU:0, one launch (start us, length us, event | category | flops | bytes accessed | tf_op | source)
XLA Modules:
  0.0 72.9 jit_solution(10827539026330918007)
XLA Ops:
  0.6 0.5 collective-permute-start
  1.1 0.7 dynamic-slice_bitcast_fusion
  1.9 0.5 collective-permute-done.other
  2.3 0.0 copy-done.6
  2.4 0.7 copy-done.16
  3.0 1.9 %shard_map.113 = (bf16[4,2,16,512]{3,2,1,0:T(8,128)(2,1)}, bf16[4,2,16,512]{3,2,1,0:T(8,128)(2,1)}, bf16[4,2,16,512]{3,2,1,0:T(8,128)(2,1)}, bf16[4,2,16,512]{3,2,1,0:T(8,128)(2,1)}) custom-call(s32[20]{0:T(128)} %copy-done.6, bf16[2,1,2,32,512]{4,3,2,1,0:T(8,128)(2,1)} %own.1, bf16[2,1,2,32,512]{4,3,2,1,0:T(8,128)(2,1)} %copy-done.16), custom_call_target="tpu_custom_call" | custom-call | tf_op jit(solution)/shard_map/pallas_call | solution.py:394
  4.9 4.9 %collective-permute-start.1 = (bf16[4,2,16,512]{3,2,1,0:T(8,128)(2,1)}, bf16[4,2,16,512]{3,2,1,0:T(8,128)(2,1)S(1)}, u32[]{:S(2)}, u32[]{:S(2)}) collective-permute-start(bf16[4,2,16,512]{3,2,1,0:T(8,128)(2,1)} %get-tuple-element.29), channel_id=1, source_target_pairs={{0,12},{1,15},{2,14},{3,13},{4,8},{5,11},{6,10},{7,9},{8,4},{9,7},... | collective-permute-start | bytes 393224 | tf_op jit(solution)/shard_map/ppermute | solution.py:402
  9.8 0.6 collective-permute-start.3
  10.4 1.7 %collective-permute-start.4 = (bf16[4,2,16,512]{3,2,1,0:T(8,128)(2,1)}, bf16[4,2,16,512]{3,2,1,0:T(8,128)(2,1)S(1)}, u32[]{:S(2)}, u32[]{:S(2)}) collective-permute-start(bf16[4,2,16,512]{3,2,1,0:T(8,128)(2,1)} %get-tuple-element.32), channel_id=1, source_target_pairs={{0,0},{1,3},{2,2},{3,1},{4,4},{5,7},{6,6},{7,5},{8,8},{9,11},{10,1... | collective-permute-start | bytes 393224 | tf_op jit(solution)/shard_map/ppermute | solution.py:402
  12.1 2.2 %collective-permute-done.1.refs_0_ = bf16[4,2,16,512]{3,2,1,0:T(8,128)(2,1)S(1)} collective-permute-done((bf16[4,2,16,512]{3,2,1,0:T(8,128)(2,1)}, bf16[4,2,16,512]{3,2,1,0:T(8,128)(2,1)S(1)}, u32[]{:S(2)}, u32[]{:S(2)}) %collective-permute-start.1) | collective-permute-done | bytes 131104 | tf_op jit(solution)/shard_map/ppermute | solution.py:402
  14.3 0.0 collective-permute-start.5
  14.3 7.8 %collective-permute-done.2.refs_1_ = bf16[4,2,16,512]{3,2,1,0:T(8,128)(2,1)S(1)} collective-permute-done((bf16[4,2,16,512]{3,2,1,0:T(8,128)(2,1)}, bf16[4,2,16,512]{3,2,1,0:T(8,128)(2,1)S(1)}, u32[]{:S(2)}, u32[]{:S(2)}) %collective-permute-start.2) | collective-permute-done | bytes 131104 | tf_op jit(solution)/shard_map/ppermute | solution.py:402
  22.1 0.5 collective-permute-start.7
  22.7 0.1 collective-permute-start.8
  22.7 0.1 copy.13.pairs
  22.8 0.0 collective-permute-done.5.refs_4_
  22.8 0.7 collective-permute-done.6.refs_5_
  23.5 0.2 collective-permute-done.7.refs_6_
  23.7 0.3 collective-permute-done.8.refs_7_
  24.0 0.0 copy-start
  24.0 1.2 %copy-done = bf16[1024,512]{1,0:T(8,128)(2,1)S(1)} copy-done((bf16[1024,512]{1,0:T(8,128)(2,1)S(1)}, bf16[1024,512]{1,0:T(8,128)(2,1)}, u32[]{:S(2)}) %copy-start) | copy-done | bytes 1048600
  25.3 1.2 %copy-done.1 = bf16[1024,512]{1,0:T(8,128)(2,1)S(1)} copy-done((bf16[1024,512]{1,0:T(8,128)(2,1)S(1)}, bf16[1024,512]{1,0:T(8,128)(2,1)}, u32[]{:S(2)}) %copy-start.1) | copy-done | bytes 1048600
  26.5 1.1 %copy-done.3 = bf16[512,640]{1,0:T(8,128)(2,1)S(1)} copy-done((bf16[512,640]{1,0:T(8,128)(2,1)S(1)}, bf16[512,640]{1,0:T(8,128)(2,1)}, u32[]{:S(2)}) %copy-start.3) | copy-done | bytes 655384
  27.6 1.0 %copy-done.4 = bf16[512,512]{1,0:T(8,128)(2,1)S(1)} copy-done((bf16[512,512]{1,0:T(8,128)(2,1)S(1)}, bf16[512,512]{1,0:T(8,128)(2,1)}, u32[]{:S(2)}) %copy-start.4) | copy-done | bytes 524312
  28.6 15.4 %shard_map.114 = (f32[512,512]{1,0:T(8,128)S(1)}, bf16[520,512]{1,0:T(8,128)(2,1)S(1)}, f32[16,128]{1,0:T(8,128)S(1)}) custom-call(s32[20]{0:T(128)S(1)} %copy-done.7, s32[16,2]{1,0:T(8,128)S(1)} %copy.13.pairs, s32[4,8]{1,0:T(4,128)S(1)} %copy-done.9, bf16[4,2,16,512]{3,2,1,0:T(8,128)(2,1)S(1)} %collective-permute-done.1.refs_0_, ...), custom_call_target="tpu_custom_call" | custom-call | tf_op jit(solution)/shard_map/pallas_call | solution.py:442
  44.0 1.0 %copy-done.2 = f32[512,512]{1,0:T(8,128)} copy-done((f32[512,512]{1,0:T(8,128)}, f32[512,512]{1,0:T(8,128)S(1)}, u32[]{:S(2)}) %copy-start.2) | copy-done | bytes 1048600
  45.0 0.6 copy-done.5
  45.6 0.2 collective-permute-start.9
  45.8 0.7 copy-done.18
  46.4 0.2 convert_reduce_fusion
  46.6 0.9 %collective-permute-done.9.came = bf16[520,512]{1,0:T(8,128)(2,1)S(1)} collective-permute-done((bf16[520,512]{1,0:T(8,128)(2,1)S(1)}, bf16[520,512]{1,0:T(8,128)(2,1)S(1)}, u32[]{:S(2)}, u32[]{:S(2)}) %collective-permute-start.9) | collective-permute-done | bytes 532512 | tf_op jit(solution)/shard_map/ppermute | solution.py:454
  47.5 0.8 %copy-done.10 = bf16[520,512]{1,0:T(8,128)(2,1)} copy-done((bf16[520,512]{1,0:T(8,128)(2,1)}, bf16[520,512]{1,0:T(8,128)(2,1)S(1)}, u32[]{:S(2)}) %copy-start.10) | copy-done | bytes 532504
  48.3 2.2 %shard_map.115 = (bf16[136,512]{1,0:T(8,128)(2,1)}, bf16[136,512]{1,0:T(8,128)(2,1)}, bf16[136,512]{1,0:T(8,128)(2,1)}, bf16[136,512]{1,0:T(8,128)(2,1)}) custom-call(f32[512,512]{1,0:T(8,128)} %copy-done.2, bf16[520,512]{1,0:T(8,128)(2,1)} %copy-done.10, f32[16,128]{1,0:T(8,128)} %copy-done.5), custom_call_target="tpu_custom_call" | custom-call | tf_op jit(solution)/shard_map/pallas_call | solution.py:456
  50.5 2.5 %collective-permute-start.10 = (bf16[136,512]{1,0:T(8,128)(2,1)}, bf16[136,512]{1,0:T(8,128)(2,1)S(1)}, u32[]{:S(2)}, u32[]{:S(2)}) collective-permute-start(bf16[136,512]{1,0:T(8,128)(2,1)} %get-tuple-element.36), channel_id=1, source_target_pairs={{0,12},{1,15},{2,14},{3,13},{4,8},{5,11},{6,10},{7,9},{8,4},{9,7},... | collective-permute-start | bytes 417800 | tf_op jit(solution)/shard_map/ppermute | solution.py:463
  53.0 0.0 collective-permute-start.11
  53.0 1.9 %collective-permute-start.12 = (bf16[136,512]{1,0:T(8,128)(2,1)}, bf16[136,512]{1,0:T(8,128)(2,1)S(1)}, u32[]{:S(2)}, u32[]{:S(2)}) collective-permute-start(bf16[136,512]{1,0:T(8,128)(2,1)} %get-tuple-element.38), channel_id=1, source_target_pairs={{0,4},{1,7},{2,6},{3,5},{4,0},{5,3},{6,2},{7,1},{8,12},{9,15},{10,... | collective-permute-start | bytes 417800 | tf_op jit(solution)/shard_map/ppermute | solution.py:463
  54.9 1.6 %collective-permute-start.13 = (bf16[136,512]{1,0:T(8,128)(2,1)}, bf16[136,512]{1,0:T(8,128)(2,1)S(1)}, u32[]{:S(2)}, u32[]{:S(2)}) collective-permute-start(bf16[136,512]{1,0:T(8,128)(2,1)} %get-tuple-element.39), channel_id=1, source_target_pairs={{0,0},{1,3},{2,2},{3,1},{4,4},{5,7},{6,6},{7,5},{8,8},{9,11},{10,1... | collective-permute-start | bytes 417800 | tf_op jit(solution)/shard_map/ppermute | solution.py:463
  56.5 2.8 %collective-permute-done.10.refs_0_ = bf16[136,512]{1,0:T(8,128)(2,1)S(1)} collective-permute-done((bf16[136,512]{1,0:T(8,128)(2,1)}, bf16[136,512]{1,0:T(8,128)(2,1)S(1)}, u32[]{:S(2)}, u32[]{:S(2)}) %collective-permute-start.10) | collective-permute-done | bytes 139296 | tf_op jit(solution)/shard_map/ppermute | solution.py:463
  59.2 5.9 %collective-permute-done.11.refs_1_ = bf16[136,512]{1,0:T(8,128)(2,1)S(1)} collective-permute-done((bf16[136,512]{1,0:T(8,128)(2,1)}, bf16[136,512]{1,0:T(8,128)(2,1)S(1)}, u32[]{:S(2)}, u32[]{:S(2)}) %collective-permute-start.11) | collective-permute-done | bytes 139296 | tf_op jit(solution)/shard_map/ppermute | solution.py:463
  65.1 0.6 copy-done.13
  65.8 0.0 copy-done.14
  65.8 0.7 copy-done.15
  66.5 2.2 %shard_map.116 = (f32[144,512]{1,0:T(8,128)}, f32[144,512]{1,0:T(8,128)}) custom-call(s32[20]{0:T(128)} %copy-done.6, bf16[136,512]{1,0:T(8,128)(2,1)} %copy-done.12, bf16[136,512]{1,0:T(8,128)(2,1)} %copy-done.13, bf16[136,512]{1,0:T(8,128)(2,1)} %copy-done.14, bf16[136,512]{1,0:T(8,128)(2,1)} %copy-done.15), custom_call_target="tpu_custom_call" | custom-call | tf_op jit(solution)/shard_map/pallas_call | solution.py:466
  68.6 0.1 collective-permute-start.14
  68.7 0.7 compare_convert_fusion.chosen
  69.4 1.0 %collective-permute-done.14.came = f32[144,512]{1,0:T(8,128)S(1)} collective-permute-done((f32[144,512]{1,0:T(8,128)}, f32[144,512]{1,0:T(8,128)S(1)}, u32[]{:S(2)}, u32[]{:S(2)}) %collective-permute-start.14) | collective-permute-done | bytes 294944 | tf_op jit(solution)/shard_map/ppermute | solution.py:473
  70.4 0.7 copy-done.11
  71.1 1.7 %shard_map.117 = (bf16[2,1,2,32,512]{4,3,2,1,0:T(8,128)(2,1)}, f32[1,3]{1,0:T(1,128)}) custom-call(f32[144,512]{1,0:T(8,128)} %get-tuple-element.40.mine, f32[144,512]{1,0:T(8,128)} %copy-done.11, f32[16,3]{1,0:T(8,128)} %compare_convert_fusion.chosen), custom_call_target="tpu_custom_call" | custom-call | tf_op jit(solution)/shard_map/pallas_call | solution.py:474
  (32 shorter events, 0.1 us)
Async XLA Ops:
  0.6 1.7 %collective-permute-start = (bf16[2,1,2,32,512]{4,3,2,1,0:T(8,128)(2,1)}, bf16[2,1,2,32,512]{4,3,2,1,0:T(8,128)(2,1)S(1)}, u32[]{:S(2)}, u32[]{:S(2)}) collective-permute-start(bf16[2,1,2,32,512]{4,3,2,1,0:T(8,128)(2,1)} %own.1), channel_id=1, source_target_pairs={{0,1},{1,0},{2,3},{3,2},{4,5},{5,4},{6,7},{7,6},{8,9},{9,8},{10,11... | collective-permute-start | bytes 393224 | tf_op jit(solution)/shard_map/ppermute | solution.py:392
  1.8 0.5 copy-start.6
  2.4 0.7 copy-start.16
  4.9 9.4 %collective-permute-start.1 = (bf16[4,2,16,512]{3,2,1,0:T(8,128)(2,1)}, bf16[4,2,16,512]{3,2,1,0:T(8,128)(2,1)S(1)}, u32[]{:S(2)}, u32[]{:S(2)}) collective-permute-start(bf16[4,2,16,512]{3,2,1,0:T(8,128)(2,1)} %get-tuple-element.29), channel_id=1, source_target_pairs={{0,12},{1,15},{2,14},{3,13},{4,8},{5,11},{6,10},{7,9},{8,4},{9,7},... | collective-permute-start | bytes 393224 | tf_op jit(solution)/shard_map/ppermute | solution.py:402
  9.8 12.3 %collective-permute-start.2 = (bf16[4,2,16,512]{3,2,1,0:T(8,128)(2,1)}, bf16[4,2,16,512]{3,2,1,0:T(8,128)(2,1)S(1)}, u32[]{:S(2)}, u32[]{:S(2)}) collective-permute-start(bf16[4,2,16,512]{3,2,1,0:T(8,128)(2,1)} %get-tuple-element.30), channel_id=1, source_target_pairs={{0,8},{1,11},{2,10},{3,9},{4,12},{5,15},{6,14},{7,13},{8,0},{9,3},... | collective-permute-start | bytes 393224 | tf_op jit(solution)/shard_map/ppermute | solution.py:402
  9.8 12.9 %copy-start.17 = (s32[16,2]{0,1:T(2,128)S(1)}, s32[16,2]{0,1:T(2,128)}, u32[]{:S(2)}) copy-start(s32[16,2]{0,1:T(2,128)} %param.13) | copy-start | bytes 388
  9.8 12.3 %collective-permute-start.3 = (bf16[4,2,16,512]{3,2,1,0:T(8,128)(2,1)}, bf16[4,2,16,512]{3,2,1,0:T(8,128)(2,1)S(1)}, u32[]{:S(2)}, u32[]{:S(2)}) collective-permute-start(bf16[4,2,16,512]{3,2,1,0:T(8,128)(2,1)} %get-tuple-element.31), channel_id=1, source_target_pairs={{0,4},{1,7},{2,6},{3,5},{4,0},{5,3},{6,2},{7,1},{8,12},{9,15},{10,... | collective-permute-start | bytes 393224 | tf_op jit(solution)/shard_map/ppermute | solution.py:402
  10.4 13.6 %copy-start.7 = (s32[20]{0:T(128)S(1)}, s32[20]{0:T(128)}, u32[]{:S(2)}) copy-start(s32[20]{0:T(128)} %copy-done.6) | copy-start | bytes 244
  10.4 13.6 %copy-start.8 = (f32[2,512]{1,0:T(2,128)S(1)}, f32[2,512]{1,0:T(2,128)}, u32[]{:S(2)}) copy-start(f32[2,512]{1,0:T(2,128)} %constant.98.clone.refs_12_) | copy-start | bytes 12292
  10.4 13.6 %copy-start.9 = (s32[4,8]{1,0:T(4,128)S(1)}, s32[4,8]{1,0:T(4,128)}, u32[]{:S(2)}) copy-start(s32[4,8]{1,0:T(4,128)} %mask.1) | copy-start | bytes 388
  10.4 12.2 %collective-permute-start.4 = (bf16[4,2,16,512]{3,2,1,0:T(8,128)(2,1)}, bf16[4,2,16,512]{3,2,1,0:T(8,128)(2,1)S(1)}, u32[]{:S(2)}, u32[]{:S(2)}) collective-permute-start(bf16[4,2,16,512]{3,2,1,0:T(8,128)(2,1)} %get-tuple-element.32), channel_id=1, source_target_pairs={{0,0},{1,3},{2,2},{3,1},{4,4},{5,7},{6,6},{7,5},{8,8},{9,11},{10,1... | collective-permute-start | bytes 393224 | tf_op jit(solution)/shard_map/ppermute | solution.py:402
  14.3 8.5 %collective-permute-start.5 = (bf16[4,2,16,512]{3,2,1,0:T(8,128)(2,1)S(1)}, bf16[4,2,16,512]{3,2,1,0:T(8,128)(2,1)S(1)}, u32[]{:S(2)}, u32[]{:S(2)}) collective-permute-start(bf16[4,2,16,512]{3,2,1,0:T(8,128)(2,1)S(1)} %collective-permute-done.1.refs_0_), channel_id=1, source_target_pairs={{0,1},{1,0},{2,3},{3,2},{4,5},{5,4},{6,7},{7,6},{8,9},{9,8},{10,11... | collective-permute-start | bytes 393224 | tf_op jit(solution)/shard_map/ppermute | solution.py:404
  22.1 1.3 %collective-permute-start.6 = (bf16[4,2,16,512]{3,2,1,0:T(8,128)(2,1)S(1)}, bf16[4,2,16,512]{3,2,1,0:T(8,128)(2,1)S(1)}, u32[]{:S(2)}, u32[]{:S(2)}) collective-permute-start(bf16[4,2,16,512]{3,2,1,0:T(8,128)(2,1)S(1)} %collective-permute-done.2.refs_1_), channel_id=1, source_target_pairs={{0,1},{1,0},{2,3},{3,2},{4,5},{5,4},{6,7},{7,6},{8,9},{9,8},{10,11... | collective-permute-start | bytes 393224 | tf_op jit(solution)/shard_map/ppermute | solution.py:404
  22.1 1.5 %collective-permute-start.7 = (bf16[4,2,16,512]{3,2,1,0:T(8,128)(2,1)S(1)}, bf16[4,2,16,512]{3,2,1,0:T(8,128)(2,1)S(1)}, u32[]{:S(2)}, u32[]{:S(2)}) collective-permute-start(bf16[4,2,16,512]{3,2,1,0:T(8,128)(2,1)S(1)} %collective-permute-done.3.refs_2_), channel_id=1, source_target_pairs={{0,1},{1,0},{2,3},{3,2},{4,5},{5,4},{6,7},{7,6},{8,9},{9,8},{10,11... | collective-permute-start | bytes 393224 | tf_op jit(solution)/shard_map/ppermute | solution.py:404
  22.7 1.3 %collective-permute-start.8 = (bf16[4,2,16,512]{3,2,1,0:T(8,128)(2,1)S(1)}, bf16[4,2,16,512]{3,2,1,0:T(8,128)(2,1)S(1)}, u32[]{:S(2)}, u32[]{:S(2)}) collective-permute-start(bf16[4,2,16,512]{3,2,1,0:T(8,128)(2,1)S(1)} %collective-permute-done.4.refs_3_), channel_id=1, source_target_pairs={{0,1},{1,0},{2,3},{3,2},{4,5},{5,4},{6,7},{7,6},{8,9},{9,8},{10,11... | collective-permute-start | bytes 393224 | tf_op jit(solution)/shard_map/ppermute | solution.py:404
  24.0 1.2 %copy-start = (bf16[1024,512]{1,0:T(8,128)(2,1)S(1)}, bf16[1024,512]{1,0:T(8,128)(2,1)}, u32[]{:S(2)}) copy-start(bf16[1024,512]{1,0:T(8,128)(2,1)} %constant.96.clone.refs_10_) | copy-start | bytes 3145732
  25.3 1.2 %copy-start.1 = (bf16[1024,512]{1,0:T(8,128)(2,1)S(1)}, bf16[1024,512]{1,0:T(8,128)(2,1)}, u32[]{:S(2)}) copy-start(bf16[1024,512]{1,0:T(8,128)(2,1)} %constant.97.clone.refs_11_) | copy-start | bytes 3145732
  26.5 1.1 %copy-start.3 = (bf16[512,640]{1,0:T(8,128)(2,1)S(1)}, bf16[512,640]{1,0:T(8,128)(2,1)}, u32[]{:S(2)}) copy-start(bf16[512,640]{1,0:T(8,128)(2,1)} %constant.94.clone.refs_8_) | copy-start | bytes 1966084
  27.6 1.0 %copy-start.4 = (bf16[512,512]{1,0:T(8,128)(2,1)S(1)}, bf16[512,512]{1,0:T(8,128)(2,1)}, u32[]{:S(2)}) copy-start(bf16[512,512]{1,0:T(8,128)(2,1)} %constant.95.clone.refs_9_) | copy-start | bytes 1572868
  44.0 1.0 %copy-start.2 = (f32[512,512]{1,0:T(8,128)}, f32[512,512]{1,0:T(8,128)S(1)}, u32[]{:S(2)}) copy-start(f32[512,512]{1,0:T(8,128)S(1)} %get-tuple-element.33.keep) | copy-start | bytes 3145732
  45.0 0.6 copy-start.5
  45.6 1.9 %collective-permute-start.9 = (bf16[520,512]{1,0:T(8,128)(2,1)S(1)}, bf16[520,512]{1,0:T(8,128)(2,1)S(1)}, u32[]{:S(2)}, u32[]{:S(2)}) collective-permute-start(bf16[520,512]{1,0:T(8,128)(2,1)S(1)} %get-tuple-element.34), channel_id=1, source_target_pairs={{0,1},{1,0},{2,3},{3,2},{4,5},{5,4},{6,7},{7,6},{8,9},{9,8},{10,11... | collective-permute-start | bytes 1597448 | tf_op jit(solution)/shard_map/ppermute | solution.py:454
  45.8 0.7 copy-start.18
  47.5 0.8 %copy-start.10 = (bf16[520,512]{1,0:T(8,128)(2,1)}, bf16[520,512]{1,0:T(8,128)(2,1)S(1)}, u32[]{:S(2)}) copy-start(bf16[520,512]{1,0:T(8,128)(2,1)S(1)} %collective-permute-done.9.came) | copy-start | bytes 1597444
  50.5 8.7 %collective-permute-start.10 = (bf16[136,512]{1,0:T(8,128)(2,1)}, bf16[136,512]{1,0:T(8,128)(2,1)S(1)}, u32[]{:S(2)}, u32[]{:S(2)}) collective-permute-start(bf16[136,512]{1,0:T(8,128)(2,1)} %get-tuple-element.36), channel_id=1, source_target_pairs={{0,12},{1,15},{2,14},{3,13},{4,8},{5,11},{6,10},{7,9},{8,4},{9,7},... | collective-permute-start | bytes 417800 | tf_op jit(solution)/shard_map/ppermute | solution.py:463
  53.0 12.1 %collective-permute-start.11 = (bf16[136,512]{1,0:T(8,128)(2,1)}, bf16[136,512]{1,0:T(8,128)(2,1)S(1)}, u32[]{:S(2)}, u32[]{:S(2)}) collective-permute-start(bf16[136,512]{1,0:T(8,128)(2,1)} %get-tuple-element.37), channel_id=1, source_target_pairs={{0,8},{1,11},{2,10},{3,9},{4,12},{5,15},{6,14},{7,13},{8,0},{9,3},... | collective-permute-start | bytes 417800 | tf_op jit(solution)/shard_map/ppermute | solution.py:463
  53.0 12.1 %collective-permute-start.12 = (bf16[136,512]{1,0:T(8,128)(2,1)}, bf16[136,512]{1,0:T(8,128)(2,1)S(1)}, u32[]{:S(2)}, u32[]{:S(2)}) collective-permute-start(bf16[136,512]{1,0:T(8,128)(2,1)} %get-tuple-element.38), channel_id=1, source_target_pairs={{0,4},{1,7},{2,6},{3,5},{4,0},{5,3},{6,2},{7,1},{8,12},{9,15},{10,... | collective-permute-start | bytes 417800 | tf_op jit(solution)/shard_map/ppermute | solution.py:463
  54.9 10.2 %collective-permute-start.13 = (bf16[136,512]{1,0:T(8,128)(2,1)}, bf16[136,512]{1,0:T(8,128)(2,1)S(1)}, u32[]{:S(2)}, u32[]{:S(2)}) collective-permute-start(bf16[136,512]{1,0:T(8,128)(2,1)} %get-tuple-element.39), channel_id=1, source_target_pairs={{0,0},{1,3},{2,2},{3,1},{4,4},{5,7},{6,6},{7,5},{8,8},{9,11},{10,1... | collective-permute-start | bytes 417800 | tf_op jit(solution)/shard_map/ppermute | solution.py:463
  59.2 5.9 %copy-start.12 = (bf16[136,512]{1,0:T(8,128)(2,1)}, bf16[136,512]{1,0:T(8,128)(2,1)S(1)}, u32[]{:S(2)}) copy-start(bf16[136,512]{1,0:T(8,128)(2,1)S(1)} %collective-permute-done.10.refs_0_) | copy-start | bytes 417796
  65.1 0.7 copy-start.13
  65.1 0.7 copy-start.14
  65.8 0.7 copy-start.15
  68.6 1.8 %collective-permute-start.14 = (f32[144,512]{1,0:T(8,128)}, f32[144,512]{1,0:T(8,128)S(1)}, u32[]{:S(2)}, u32[]{:S(2)}) collective-permute-start(f32[144,512]{1,0:T(8,128)} %get-tuple-element.41), channel_id=1, source_target_pairs={{0,1},{1,0},{2,3},{3,2},{4,5},{5,4},{6,7},{7,6},{8,9},{9,8},{10,11... | collective-permute-start | bytes 884744 | tf_op jit(solution)/shard_map/ppermute | solution.py:473
  70.4 0.7 copy-start.11

commit v2 on v1

--- a/solution.py
+++ b/solution.py
@@ -15,6 +15,7 @@
 TEAM = 8
 SUBSETS = ((0, 1), (0, 1), (0, 2), (0, 3), (1, 2), (1, 3), (2, 3), (2, 3))
 GROUP = 4
+SMALL_VMEM = 6 << 20
 HOPS = ((6, 4, 2, 0), (7, 5, 3, 1))
 
 
@@ -60,7 +61,7 @@
             for hop in HOPS[core]:
                 row += SUBSETS[rank ^ hop]
             out[rank, core] = row
-    return out
+    return out.reshape(TEAM * 2, -1)
 
 
 def pack_kernel(meta, own, other, *refs):
@@ -371,14 +372,17 @@
     swap = [(0, 1), (1, 0)]
     smem = pl.BlockSpec(memory_space=pltpu.SMEM)
     vmem = pl.BlockSpec(memory_space=pltpu.VMEM)
-    hbm = pl.BlockSpec(memory_space=pl.ANY)
+    hbm = pl.BlockSpec(memory_space=pltpu.HBM)
+    small = pltpu.CompilerParams(vmem_limit_bytes=SMALL_VMEM)
     count = len(HOPS[0])
     hop_pairs = [
         [(2 * b + c, 2 * (b ^ HOPS[c][r]) + c) for b in range(TEAM) for c in range(2)]
         for r in range(count)
     ]
-    meta = jnp.asarray(positions())[blk_index % TEAM, core]
-    meta = meta.at[0].set(blk_index // TEAM * pair_count)
+    rank = blk_index if direct else lax.rem(blk_index, TEAM)
+    meta = lax.dynamic_slice_in_dim(jnp.asarray(positions()), rank * 2 + core, 1)[0]
+    if not direct:
+        meta = meta.at[0].set(lax.div(blk_index, TEAM) * pair_count)
 
     owner_ids = owners[:, 0]
     order = jnp.arange(pair_total, dtype=jnp.int32)
@@ -388,6 +392,10 @@
     chosen = (slot[:, None] == mine_slots[None, :]).astype(jnp.float32)
     misfit_scale = 1.0 / (channels * channels * 2.0 * freq)
 
+    table_arrays = [jnp.asarray(table) for table in tables(freq)]
+    table_arrays[:4] = [
+        pltpu.with_memory_space_constraint(table, pltpu.HBM) for table in table_arrays[:4]
+    ]
     if direct:
         other = lax.ppermute(spectra, "win", swap)
         parcel_type = jax.ShapeDtypeStruct((2 * local, 2, 2 * part, freq), jnp.bfloat16)
@@ -397,6 +405,7 @@
             in_specs=[smem, vmem, vmem],
             out_specs=(vmem,) * count,
             scratch_shapes=[pltpu.VMEM((PARTS, part, freq), jnp.float32)],
+            compiler_params=small,
         )(meta, spectra, other)
         landed = [
             lax.ppermute(parcel, ("blk", "win"), pairs) for parcel, pairs in zip(parcels, hop_pairs)
@@ -411,7 +420,6 @@
         own = lax.all_to_all(outgoing, "blk", split_axis=0, concat_axis=0, tiled=True)
         came = [own, lax.ppermute(own, "win", swap)]
 
-    table_arrays = tables(freq)
     grad_shape = (blk_count, 2 * local, 2, 2 * part, freq)
     grad_bytes = math.prod(grad_shape) * 4
     rows = part * part * GROUP
@@ -458,6 +466,7 @@
             out_shape=(parcel_type,) * count,
             in_specs=[vmem] * 3,
             out_specs=(vmem,) * count,
+            compiler_params=small,
         )(own_grad, swapped, misfit)
         landed = [
             lax.ppermute(parcel, ("blk", "win"), pairs) for parcel, pairs in zip(parcels, hop_pairs)
@@ -469,6 +478,7 @@
             in_specs=[smem] + [vmem] * count,
             out_specs=(vmem, vmem),
             scratch_shapes=[pltpu.VMEM((2 * local, 2, PARTS, part, freq), jnp.float32)],
+            compiler_params=small,
         )(meta, *landed)
         swapped = lax.ppermute(give, "win", swap)
         gradient, totals = pl.pallas_call(
@@ -479,6 +489,7 @@
             ),
             in_specs=[vmem] * 3,
             out_specs=(vmem, vmem),
+            compiler_params=small,
         )(mine, swapped, chosen)
         return (gradient, totals.reshape(CAP))
 

time: 73.4 us -> 58.9 us (0.80)
  local copies, waits for them, and re-layouts: 11.1 us -> 2.34 us
  Pallas kernels: 23.4 us -> 18.4 us
  waiting for transfers between devices: 22.3 us -> 23.6 us
  starting transfers between devices: 14.5 us -> 13.3 us
    unnamed x39 -> x11, local copies, waits for them, and re-layouts: 10.4 us -> 1.65 us
    pallas_call x1, Pallas kernels: 2.22 us -> 0.09 us  [per_device(): pl.pallas_call(add_kernel, out_shape=(parcel_type,) * count, in_specs=[vm...]
    ppermute x8, starting transfers between devices: 13.1 us -> 11.5 us  [per_device(): lax.ppermute(parcel, ('blk', 'win'), pairs)]
    pallas_call x1, Pallas kernels: 2.17 us -> 0.8 us  [per_device(): pl.pallas_call(merge_kernel, out_shape=(half_type, half_type), in_specs=[...]
    pallas_call x1, Pallas kernels: 1.89 us -> 0.66 us  [per_device(): pl.pallas_call(pack_kernel, out_shape=(parcel_type,) * count, in_specs=[s...]
    pallas_call x1, Pallas kernels: 1.74 us -> 0.69 us  [per_device(): pl.pallas_call(functools.partial(finish_kernel, scale=misfit_scale), out_...]
    ppermute x8, waiting for transfers between devices: 18.7 us -> 19.6 us  [per_device(): lax.ppermute(parcel, ('blk', 'win'), pairs)]
where the time goes in v2:
time: 58.9 us; the launch traced here: 58.6 us
  waiting for transfers between devices  23.6 us (40%)
  Pallas kernels  18.4 us (31%)
  starting transfers between devices  13.3 us (23%)
  local copies, waits for them, and re-layouts  2.34 us (4%)
  between operations  0.69 us (1%)
    ppermute x8, waiting for transfers between devices, per_device(): lax.ppermute(parcel, ('blk', 'win'), pairs)  19.6 us
    pallas_call x1, Pallas kernels, per_device(): pl.pallas_call(functools.partial(pair_kernel, direct, pair_count), out_sh...  16.1 us
    ppermute x8, starting transfers between devices, per_device(): lax.ppermute(parcel, ('blk', 'win'), pairs)  11.5 us
    unnamed x11, local copies, waits for them, and re-layouts  1.65 us
    ppermute x1, waiting for transfers between devices, per_device(): swapped = lax.ppermute(give, 'win', swap)  1.4 us
    ppermute x4, waiting for transfers between devices, per_device(): came = landed + [lax.ppermute(parcel, 'win', swap) for parcel in landed]  1.19 us
  transfers between devices with their start and end apart: 15, of which 10 were waited for; matrix products, arithmetic and copies ran while one was open for 2% of the time, Pallas kernels for 0%

profile of v2, /device:TPU:0, one launch (start us, length us, event | category | flops | bytes accessed | tf_op | source)
XLA Modules:
  0.0 58.6 jit_solution(5854999321433692494)
XLA Ops:
  0.6 0.5 collective-permute-start
  1.1 0.7 %dynamic-slice_bitcast_fusion.meta = s32[20]{0:T(128)S(1)} fusion(s32[16,20]{1,0:T(8,128)} %constant.29.clone, s32[]{:T(128)S(6)} %select_n.3), kind=kLoop, calls=%fused_computation.7 | loop fusion | bytes 164 | tf_op jit(solution)/shard_map/squeeze | solution.py:383
  1.8 0.5 collective-permute-done.other
  2.3 0.0 copy-start
  2.3 0.9 %copy-done = bf16[2,1,2,32,512]{4,3,2,1,0:T(8,128)(2,1)S(1)} copy-done((bf16[2,1,2,32,512]{4,3,2,1,0:T(8,128)(2,1)S(1)}, bf16[2,1,2,32,512]{4,3,2,1,0:T(8,128)(2,1)}, u32[]{:S(2)}) %copy-start) | copy-done | bytes 131096
  3.2 0.7 %shard_map.113 = (bf16[4,2,16,512]{3,2,1,0:T(8,128)(2,1)S(1)}, bf16[4,2,16,512]{3,2,1,0:T(8,128)(2,1)S(1)}, bf16[4,2,16,512]{3,2,1,0:T(8,128)(2,1)S(1)}, bf16[4,2,16,512]{3,2,1,0:T(8,128)(2,1)S(1)}) custom-call(s32[20]{0:T(128)S(1)} %dynamic-slice_bitcast_fusion.meta, bf16[2,1,2,32,512]{4,3,2,1,0:T(8,128)(2,1)S(1)} %copy-done, ...), custom_call_target="tpu_custom_call" | custom-call | tf_op jit(solution)/shard_map/pallas_call | solution.py:402
  3.9 5.0 %collective-permute-start.1 = (bf16[4,2,16,512]{3,2,1,0:T(8,128)(2,1)S(1)}, bf16[4,2,16,512]{3,2,1,0:T(8,128)(2,1)S(1)}, u32[]{:S(2)}, u32[]{:S(2)}) collective-permute-start(bf16[4,2,16,512]{3,2,1,0:T(8,128)(2,1)S(1)} %get-tuple-element.17), channel_id=1, source_target_pairs={{0,12},{1,15},{2,14},{3,13},{4,8},{5,11},{6,10},{7,9},{8,4},{9,7},... | collective-permute-start | bytes 393224 | tf_op jit(solution)/shard_map/ppermute | solution.py:411
  8.9 0.0 collective-permute-start.2
  8.9 0.0 copy-start.3
  8.9 0.6 %collective-permute-start.3 = (bf16[4,2,16,512]{3,2,1,0:T(8,128)(2,1)S(1)}, bf16[4,2,16,512]{3,2,1,0:T(8,128)(2,1)S(1)}, u32[]{:S(2)}, u32[]{:S(2)}) collective-permute-start(bf16[4,2,16,512]{3,2,1,0:T(8,128)(2,1)S(1)} %get-tuple-element.19), channel_id=1, source_target_pairs={{0,4},{1,7},{2,6},{3,5},{4,0},{5,3},{6,2},{7,1},{8,12},{9,15},{10,... | collective-permute-start | bytes 393224 | tf_op jit(solution)/shard_map/ppermute | solution.py:411
  9.6 0.0 copy-start.1
  9.6 0.0 copy-start.2
  9.6 0.8 %collective-permute-start.4 = (bf16[4,2,16,512]{3,2,1,0:T(8,128)(2,1)S(1)}, bf16[4,2,16,512]{3,2,1,0:T(8,128)(2,1)S(1)}, u32[]{:S(2)}, u32[]{:S(2)}) collective-permute-start(bf16[4,2,16,512]{3,2,1,0:T(8,128)(2,1)S(1)} %get-tuple-element.20), channel_id=1, source_target_pairs={{0,0},{1,3},{2,2},{3,1},{4,4},{5,7},{6,6},{7,5},{8,8},{9,11},{10,1... | collective-permute-start | bytes 393224 | tf_op jit(solution)/shard_map/ppermute | solution.py:411
  10.4 2.7 %collective-permute-done.1.refs_0_ = bf16[4,2,16,512]{3,2,1,0:T(8,128)(2,1)S(1)} collective-permute-done((bf16[4,2,16,512]{3,2,1,0:T(8,128)(2,1)S(1)}, bf16[4,2,16,512]{3,2,1,0:T(8,128)(2,1)S(1)}, u32[]{:S(2)}, u32[]{:S(2)}) %collective-permute-start.1) | collective-permute-done | bytes 131104 | tf_op jit(solution)/shard_map/ppermute | solution.py:411
  13.1 0.3 collective-permute-start.5
  13.4 7.6 %collective-permute-done.2.refs_1_ = bf16[4,2,16,512]{3,2,1,0:T(8,128)(2,1)S(1)} collective-permute-done((bf16[4,2,16,512]{3,2,1,0:T(8,128)(2,1)S(1)}, bf16[4,2,16,512]{3,2,1,0:T(8,128)(2,1)S(1)}, u32[]{:S(2)}, u32[]{:S(2)}) %collective-permute-start.2) | collective-permute-done | bytes 131104 | tf_op jit(solution)/shard_map/ppermute | solution.py:411
  21.0 0.0 collective-permute-start.6
  21.0 0.0 collective-permute-done.3.refs_2_
  21.0 0.5 collective-permute-start.7
  21.5 0.0 collective-permute-done.4.refs_3_
  21.5 0.1 collective-permute-start.8
  21.6 0.0 copy-done.3
  21.6 0.1 copy.13.pairs
  21.7 0.0 collective-permute-done.5.refs_4_
  21.7 0.7 %collective-permute-done.6.refs_5_ = bf16[4,2,16,512]{3,2,1,0:T(8,128)(2,1)S(1)} collective-permute-done((bf16[4,2,16,512]{3,2,1,0:T(8,128)(2,1)S(1)}, bf16[4,2,16,512]{3,2,1,0:T(8,128)(2,1)S(1)}, u32[]{:S(2)}, u32[]{:S(2)}) %collective-permute-start.6) | collective-permute-done | bytes 131104 | tf_op jit(solution)/shard_map/ppermute | solution.py:413
  22.4 0.2 collective-permute-done.7.refs_6_
  22.6 0.3 collective-permute-done.8.refs_7_
  22.9 0.0 copy-done.1
  22.9 0.0 copy-done.2
  22.9 16.1 %shard_map.114 = (f32[512,512]{1,0:T(8,128)S(1)}, bf16[520,512]{1,0:T(8,128)(2,1)S(1)}, f32[16,128]{1,0:T(8,128)S(1)}) custom-call(s32[20]{0:T(128)S(1)} %dynamic-slice_bitcast_fusion.meta, s32[16,2]{1,0:T(8,128)S(1)} %copy.13.pairs, s32[4,8]{1,0:T(4,128)S(1)} %copy-done.2, bf16[4,2,16,512]{3,2,1,0:T(8,128)(2,1)S(1)} %collective-permute-done.1.refs_0_, ...), custom_call_target="tpu_custom_call" | custom-call | tf_op jit(solution)/shard_map/pallas_call | solution.py:450
  39.0 0.2 collective-permute-start.9
  39.3 0.7 %copy-done.4 = s32[16,1]{0,1:T(1,128)S(1)} copy-done((s32[16,1]{0,1:T(1,128)S(1)}, s32[16,1]{0,1:T(1,128)}, u32[]{:S(2)}) %copy-start.4) | copy-done | bytes 88
  39.9 0.2 convert_reduce_fusion
  40.1 0.9 %collective-permute-done.9.came = bf16[520,512]{1,0:T(8,128)(2,1)S(1)} collective-permute-done((bf16[520,512]{1,0:T(8,128)(2,1)S(1)}, bf16[520,512]{1,0:T(8,128)(2,1)S(1)}, u32[]{:S(2)}, u32[]{:S(2)}) %collective-permute-start.9) | collective-permute-done | bytes 532512 | tf_op jit(solution)/shard_map/ppermute | solution.py:462
  41.0 0.1 shard_map.115
  41.1 2.5 %collective-permute-start.10 = (bf16[136,512]{1,0:T(8,128)(2,1)S(1)}, bf16[136,512]{1,0:T(8,128)(2,1)S(1)}, u32[]{:S(2)}, u32[]{:S(2)}) collective-permute-start(bf16[136,512]{1,0:T(8,128)(2,1)S(1)} %get-tuple-element.24), channel_id=1, source_target_pairs={{0,12},{1,15},{2,14},{3,13},{4,8},{5,11},{6,10},{7,9},{8,4},{9,7},... | collective-permute-start | bytes 417800 | tf_op jit(solution)/shard_map/ppermute | solution.py:472
  43.6 0.0 collective-permute-start.11
  43.7 1.9 %collective-permute-start.12 = (bf16[136,512]{1,0:T(8,128)(2,1)S(1)}, bf16[136,512]{1,0:T(8,128)(2,1)S(1)}, u32[]{:S(2)}, u32[]{:S(2)}) collective-permute-start(bf16[136,512]{1,0:T(8,128)(2,1)S(1)} %get-tuple-element.26), channel_id=1, source_target_pairs={{0,4},{1,7},{2,6},{3,5},{4,0},{5,3},{6,2},{7,1},{8,12},{9,15},{10,... | collective-permute-start | bytes 417800 | tf_op jit(solution)/shard_map/ppermute | solution.py:472
  45.6 0.7 %collective-permute-start.13 = (bf16[136,512]{1,0:T(8,128)(2,1)S(1)}, bf16[136,512]{1,0:T(8,128)(2,1)S(1)}, u32[]{:S(2)}, u32[]{:S(2)}) collective-permute-start(bf16[136,512]{1,0:T(8,128)(2,1)S(1)} %get-tuple-element.27), channel_id=1, source_target_pairs={{0,0},{1,3},{2,2},{3,1},{4,4},{5,7},{6,6},{7,5},{8,8},{9,11},{10,1... | collective-permute-start | bytes 417800 | tf_op jit(solution)/shard_map/ppermute | solution.py:472
  46.2 3.4 %collective-permute-done.10.refs_0_ = bf16[136,512]{1,0:T(8,128)(2,1)S(1)} collective-permute-done((bf16[136,512]{1,0:T(8,128)(2,1)S(1)}, bf16[136,512]{1,0:T(8,128)(2,1)S(1)}, u32[]{:S(2)}, u32[]{:S(2)}) %collective-permute-start.10) | collective-permute-done | bytes 139296 | tf_op jit(solution)/shard_map/ppermute | solution.py:472
  49.7 5.8 %collective-permute-done.11.refs_1_ = bf16[136,512]{1,0:T(8,128)(2,1)S(1)} collective-permute-done((bf16[136,512]{1,0:T(8,128)(2,1)S(1)}, bf16[136,512]{1,0:T(8,128)(2,1)S(1)}, u32[]{:S(2)}, u32[]{:S(2)}) %collective-permute-start.11) | collective-permute-done | bytes 139296 | tf_op jit(solution)/shard_map/ppermute | solution.py:472
  55.5 0.0 collective-permute-done.12.refs_2_
  55.5 0.0 collective-permute-done.13.refs_3_
  55.5 0.8 %shard_map.116 = (f32[144,512]{1,0:T(8,128)S(1)}, f32[144,512]{1,0:T(8,128)S(1)}) custom-call(s32[20]{0:T(128)S(1)} %dynamic-slice_bitcast_fusion.meta, bf16[136,512]{1,0:T(8,128)(2,1)S(1)} %collective-permute-done.10.refs_0_, bf16[136,512]{1,0:T(8,128)(2,1)S(1)} %collective-permute-done.11.refs_1_, bf16[136,512]{1,0:T(8,128)(2,1)S(1)} %collective-permute-done.12.refs_2_, ...), custom_call_target="tpu_custom_call" | custom-call | tf_op jit(solution)/shard_map/pallas_call | solution.py:475
  56.3 0.2 collective-permute-start.14
  56.5 0.1 compare_convert_fusion.chosen
  56.5 1.4 %collective-permute-done.14.came = f32[144,512]{1,0:T(8,128)S(1)} collective-permute-done((f32[144,512]{1,0:T(8,128)S(1)}, f32[144,512]{1,0:T(8,128)S(1)}, u32[]{:S(2)}, u32[]{:S(2)}) %collective-permute-start.14) | collective-permute-done | bytes 294944 | tf_op jit(solution)/shard_map/ppermute | solution.py:483
  57.9 0.7 %shard_map.117 = (bf16[2,1,2,32,512]{4,3,2,1,0:T(8,128)(2,1)}, f32[1,3]{1,0:T(1,128)}) custom-call(f32[144,512]{1,0:T(8,128)S(1)} %get-tuple-element.28.mine, f32[144,512]{1,0:T(8,128)S(1)} %collective-permute-done.14.came, f32[16,3]{1,0:T(8,128)S(1)} %compare_convert_fusion.chosen), custom_call_target="tpu_custom_call" | custom-call | tf_op jit(solution)/shard_map/pallas_call | solution.py:484
  (3 shorter events, 0.0 us)
Async XLA Ops:
  0.6 1.7 %collective-permute-start = (bf16[2,1,2,32,512]{4,3,2,1,0:T(8,128)(2,1)}, bf16[2,1,2,32,512]{4,3,2,1,0:T(8,128)(2,1)S(1)}, u32[]{:S(2)}, u32[]{:S(2)}) collective-permute-start(bf16[2,1,2,32,512]{4,3,2,1,0:T(8,128)(2,1)} %own.1), channel_id=1, source_target_pairs={{0,1},{1,0},{2,3},{3,2},{4,5},{5,4},{6,7},{7,6},{8,9},{9,8},{10,11... | collective-permute-start | bytes 393224 | tf_op jit(solution)/shard_map/ppermute | solution.py:400
  2.3 0.9 %copy-start = (bf16[2,1,2,32,512]{4,3,2,1,0:T(8,128)(2,1)S(1)}, bf16[2,1,2,32,512]{4,3,2,1,0:T(8,128)(2,1)}, u32[]{:S(2)}) copy-start(bf16[2,1,2,32,512]{4,3,2,1,0:T(8,128)(2,1)} %own.1) | copy-start | bytes 393220
  3.9 9.2 %collective-permute-start.1 = (bf16[4,2,16,512]{3,2,1,0:T(8,128)(2,1)S(1)}, bf16[4,2,16,512]{3,2,1,0:T(8,128)(2,1)S(1)}, u32[]{:S(2)}, u32[]{:S(2)}) collective-permute-start(bf16[4,2,16,512]{3,2,1,0:T(8,128)(2,1)S(1)} %get-tuple-element.17), channel_id=1, source_target_pairs={{0,12},{1,15},{2,14},{3,13},{4,8},{5,11},{6,10},{7,9},{8,4},{9,7},... | collective-permute-start | bytes 393224 | tf_op jit(solution)/shard_map/ppermute | solution.py:411
  8.9 12.1 %collective-permute-start.2 = (bf16[4,2,16,512]{3,2,1,0:T(8,128)(2,1)S(1)}, bf16[4,2,16,512]{3,2,1,0:T(8,128)(2,1)S(1)}, u32[]{:S(2)}, u32[]{:S(2)}) collective-permute-start(bf16[4,2,16,512]{3,2,1,0:T(8,128)(2,1)S(1)} %get-tuple-element.18), channel_id=1, source_target_pairs={{0,8},{1,11},{2,10},{3,9},{4,12},{5,15},{6,14},{7,13},{8,0},{9,3},... | collective-permute-start | bytes 393224 | tf_op jit(solution)/shard_map/ppermute | solution.py:411
  8.9 12.7 %copy-start.3 = (s32[16,2]{0,1:T(2,128)S(1)}, s32[16,2]{0,1:T(2,128)}, u32[]{:S(2)}) copy-start(s32[16,2]{0,1:T(2,128)} %param.11) | copy-start | bytes 388
  8.9 12.1 %collective-permute-start.3 = (bf16[4,2,16,512]{3,2,1,0:T(8,128)(2,1)S(1)}, bf16[4,2,16,512]{3,2,1,0:T(8,128)(2,1)S(1)}, u32[]{:S(2)}, u32[]{:S(2)}) collective-permute-start(bf16[4,2,16,512]{3,2,1,0:T(8,128)(2,1)S(1)} %get-tuple-element.19), channel_id=1, source_target_pairs={{0,4},{1,7},{2,6},{3,5},{4,0},{5,3},{6,2},{7,1},{8,12},{9,15},{10,... | collective-permute-start | bytes 393224 | tf_op jit(solution)/shard_map/ppermute | solution.py:411
  9.6 13.3 %copy-start.1 = (f32[2,512]{1,0:T(2,128)S(1)}, f32[2,512]{1,0:T(2,128)}, u32[]{:S(2)}) copy-start(f32[2,512]{1,0:T(2,128)} %constant.34.clone.refs_12_) | copy-start | bytes 12292
  9.6 13.3 %copy-start.2 = (s32[4,8]{1,0:T(4,128)S(1)}, s32[4,8]{1,0:T(4,128)}, u32[]{:S(2)}) copy-start(s32[4,8]{1,0:T(4,128)} %mask.1) | copy-start | bytes 388
  9.6 12.0 %collective-permute-start.4 = (bf16[4,2,16,512]{3,2,1,0:T(8,128)(2,1)S(1)}, bf16[4,2,16,512]{3,2,1,0:T(8,128)(2,1)S(1)}, u32[]{:S(2)}, u32[]{:S(2)}) collective-permute-start(bf16[4,2,16,512]{3,2,1,0:T(8,128)(2,1)S(1)} %get-tuple-element.20), channel_id=1, source_target_pairs={{0,0},{1,3},{2,2},{3,1},{4,4},{5,7},{6,6},{7,5},{8,8},{9,11},{10,1... | collective-permute-start | bytes 393224 | tf_op jit(solution)/shard_map/ppermute | solution.py:411
  13.1 8.6 %collective-permute-start.5 = (bf16[4,2,16,512]{3,2,1,0:T(8,128)(2,1)S(1)}, bf16[4,2,16,512]{3,2,1,0:T(8,128)(2,1)S(1)}, u32[]{:S(2)}, u32[]{:S(2)}) collective-permute-start(bf16[4,2,16,512]{3,2,1,0:T(8,128)(2,1)S(1)} %collective-permute-done.1.refs_0_), channel_id=1, source_target_pairs={{0,1},{1,0},{2,3},{3,2},{4,5},{5,4},{6,7},{7,6},{8,9},{9,8},{10,11... | collective-permute-start | bytes 393224 | tf_op jit(solution)/shard_map/ppermute | solution.py:413
  21.0 1.3 %collective-permute-start.6 = (bf16[4,2,16,512]{3,2,1,0:T(8,128)(2,1)S(1)}, bf16[4,2,16,512]{3,2,1,0:T(8,128)(2,1)S(1)}, u32[]{:S(2)}, u32[]{:S(2)}) collective-permute-start(bf16[4,2,16,512]{3,2,1,0:T(8,128)(2,1)S(1)} %collective-permute-done.2.refs_1_), channel_id=1, source_target_pairs={{0,1},{1,0},{2,3},{3,2},{4,5},{5,4},{6,7},{7,6},{8,9},{9,8},{10,11... | collective-permute-start | bytes 393224 | tf_op jit(solution)/shard_map/ppermute | solution.py:413
  21.0 1.5 %collective-permute-start.7 = (bf16[4,2,16,512]{3,2,1,0:T(8,128)(2,1)S(1)}, bf16[4,2,16,512]{3,2,1,0:T(8,128)(2,1)S(1)}, u32[]{:S(2)}, u32[]{:S(2)}) collective-permute-start(bf16[4,2,16,512]{3,2,1,0:T(8,128)(2,1)S(1)} %collective-permute-done.3.refs_2_), channel_id=1, source_target_pairs={{0,1},{1,0},{2,3},{3,2},{4,5},{5,4},{6,7},{7,6},{8,9},{9,8},{10,11... | collective-permute-start | bytes 393224 | tf_op jit(solution)/shard_map/ppermute | solution.py:413
  21.5 1.3 %collective-permute-start.8 = (bf16[4,2,16,512]{3,2,1,0:T(8,128)(2,1)S(1)}, bf16[4,2,16,512]{3,2,1,0:T(8,128)(2,1)S(1)}, u32[]{:S(2)}, u32[]{:S(2)}) collective-permute-start(bf16[4,2,16,512]{3,2,1,0:T(8,128)(2,1)S(1)} %collective-permute-done.4.refs_3_), channel_id=1, source_target_pairs={{0,1},{1,0},{2,3},{3,2},{4,5},{5,4},{6,7},{7,6},{8,9},{9,8},{10,11... | collective-permute-start | bytes 393224 | tf_op jit(solution)/shard_map/ppermute | solution.py:413
  39.0 2.0 %collective-permute-start.9 = (bf16[520,512]{1,0:T(8,128)(2,1)S(1)}, bf16[520,512]{1,0:T(8,128)(2,1)S(1)}, u32[]{:S(2)}, u32[]{:S(2)}) collective-permute-start(bf16[520,512]{1,0:T(8,128)(2,1)S(1)} %get-tuple-element.22), channel_id=1, source_target_pairs={{0,1},{1,0},{2,3},{3,2},{4,5},{5,4},{6,7},{7,6},{8,9},{9,8},{10,11... | collective-permute-start | bytes 1597448 | tf_op jit(solution)/shard_map/ppermute | solution.py:462
  39.3 0.7 %copy-start.4 = (s32[16,1]{0,1:T(1,128)S(1)}, s32[16,1]{0,1:T(1,128)}, u32[]{:S(2)}) copy-start(s32[16,1]{0,1:T(1,128)} %param.12) | copy-start | bytes 196
  41.1 8.6 %collective-permute-start.10 = (bf16[136,512]{1,0:T(8,128)(2,1)S(1)}, bf16[136,512]{1,0:T(8,128)(2,1)S(1)}, u32[]{:S(2)}, u32[]{:S(2)}) collective-permute-start(bf16[136,512]{1,0:T(8,128)(2,1)S(1)} %get-tuple-element.24), channel_id=1, source_target_pairs={{0,12},{1,15},{2,14},{3,13},{4,8},{5,11},{6,10},{7,9},{8,4},{9,7},... | collective-permute-start | bytes 417800 | tf_op jit(solution)/shard_map/ppermute | solution.py:472
  43.6 11.8 %collective-permute-start.11 = (bf16[136,512]{1,0:T(8,128)(2,1)S(1)}, bf16[136,512]{1,0:T(8,128)(2,1)S(1)}, u32[]{:S(2)}, u32[]{:S(2)}) collective-permute-start(bf16[136,512]{1,0:T(8,128)(2,1)S(1)} %get-tuple-element.25), channel_id=1, source_target_pairs={{0,8},{1,11},{2,10},{3,9},{4,12},{5,15},{6,14},{7,13},{8,0},{9,3},... | collective-permute-start | bytes 417800 | tf_op jit(solution)/shard_map/ppermute | solution.py:472
  43.7 11.8 %collective-permute-start.12 = (bf16[136,512]{1,0:T(8,128)(2,1)S(1)}, bf16[136,512]{1,0:T(8,128)(2,1)S(1)}, u32[]{:S(2)}, u32[]{:S(2)}) collective-permute-start(bf16[136,512]{1,0:T(8,128)(2,1)S(1)} %get-tuple-element.26), channel_id=1, source_target_pairs={{0,4},{1,7},{2,6},{3,5},{4,0},{5,3},{6,2},{7,1},{8,12},{9,15},{10,... | collective-permute-start | bytes 417800 | tf_op jit(solution)/shard_map/ppermute | solution.py:472
  45.6 9.9 %collective-permute-start.13 = (bf16[136,512]{1,0:T(8,128)(2,1)S(1)}, bf16[136,512]{1,0:T(8,128)(2,1)S(1)}, u32[]{:S(2)}, u32[]{:S(2)}) collective-permute-start(bf16[136,512]{1,0:T(8,128)(2,1)S(1)} %get-tuple-element.27), channel_id=1, source_target_pairs={{0,0},{1,3},{2,2},{3,1},{4,4},{5,7},{6,6},{7,5},{8,8},{9,11},{10,1... | collective-permute-start | bytes 417800 | tf_op jit(solution)/shard_map/ppermute | solution.py:472
  56.3 1.6 %collective-permute-start.14 = (f32[144,512]{1,0:T(8,128)S(1)}, f32[144,512]{1,0:T(8,128)S(1)}, u32[]{:S(2)}, u32[]{:S(2)}) collective-permute-start(f32[144,512]{1,0:T(8,128)S(1)} %get-tuple-element.29), channel_id=1, source_target_pairs={{0,1},{1,0},{2,3},{3,2},{4,5},{5,4},{6,7},{7,6},{8,9},{9,8},{10,11... | collective-permute-start | bytes 884744 | tf_op jit(solution)/shard_map/ppermute | solution.py:483

commit v3 on v2

--- a/solution.py
+++ b/solution.py
@@ -62,6 +62,16 @@
                 row += SUBSETS[rank ^ hop]
             out[rank, core] = row
     return out.reshape(TEAM * 2, -1)
+
+
+def team_tables(freq_count):
+    forward_re, forward_im, _, _, weight = tables(freq_count)
+    turn = np.broadcast_to(forward_re[:, freq_count : freq_count + 1], (freq_count, 128))
+    in_hbm = [
+        pltpu.with_memory_space_constraint(jnp.asarray(table), pltpu.HBM)
+        for table in (forward_re[:, :freq_count], forward_im)
+    ]
+    return (*in_hbm, jnp.asarray(turn), jnp.asarray(weight))
 
 
 def pack_kernel(meta, own, other, *refs):
@@ -146,53 +156,31 @@
 
 
 def pair_kernel(
-    direct,
-    pair_count,
     meta,
     pairs,
     mask,
-    *refs,
+    own,
+    other,
+    forward_re,
+    forward_im,
+    back_re,
+    back_im,
+    weight,
+    own_grad,
+    other_grad,
+    misfit,
+    first,
+    second,
+    cross_re,
+    cross_im,
+    adj,
+    out_re,
+    out_im,
 ):
-    sources = 2 * len(HOPS[0]) if direct else 2
-    came, refs = refs[:sources], refs[sources:]
-    (
-        forward_re_hbm,
-        forward_im_hbm,
-        back_re_hbm,
-        back_im_hbm,
-        weight,
-        own_grad,
-        other_grad,
-        misfit,
-        first,
-        second,
-        cross_re,
-        cross_im,
-        adj,
-        out_re,
-        out_im,
-        forward_re,
-        forward_im,
-        back_re,
-        back_im,
-        sems,
-    ) = refs[:20]
-    copies = [
-        pltpu.make_async_copy(source, target, sems.at[n])
-        for n, (source, target) in enumerate(
-            (
-                (forward_re_hbm, forward_re),
-                (forward_im_hbm, forward_im),
-                (back_re_hbm, back_re),
-                (back_im_hbm, back_im),
-            )
-        )
-    ]
-    for copy in copies:
-        copy.start()
-    freq = came[0].shape[-1]
-    part = came[0].shape[-2] // 2
-    local = mask.shape[0] // 2
+    pair_count = misfit.shape[0]
+    freq = own.shape[-1]
+    part = own.shape[3] // 2
+    local = own.shape[1]
     base = meta[0]
     first_part = meta[1]
     second_part = meta[2]
@@ -200,39 +188,12 @@
     rows = part * part
     lanes = 256
 
-    if direct:
-        field, grad = refs[20:]
-        for n, parcel in enumerate(came):
-            index = meta[4 + n]
-            for w in range(2 * local):
-                m = mask[w, index].astype(jnp.float32)
-                for c in range(2):
-                    field[index, w, c] = (parcel[w, c].astype(jnp.float32) * m).reshape(2, part, freq)
-        grad[...] = jnp.zeros_like(grad)
-    else:
-        own_grad[...] = jnp.zeros_like(own_grad)
-        other_grad[...] = jnp.zeros_like(other_grad)
-
-    def block(index, w, c, which):
-        both = came[w // local][index, w % local, c].astype(jnp.float32)
+    own_grad[...] = jnp.zeros_like(own_grad)
+    other_grad[...] = jnp.zeros_like(other_grad)
+
+    def block(source, index, w, c, which):
+        both = source[index, w, c].astype(jnp.float32)
         return jnp.where(which == 0, both[:part], both[part:])
-
-    def first_row(k, i, w, c, row, cut):
-        if direct:
-            return field[i, w, c, first_part, pl.ds(row, 1), cut]
-        return first[(k * 2 * local + w) * 2 + c, pl.ds(row, 1), cut]
-
-    def second_row(k, j, w, c, row, cut):
-        if direct:
-            return field[j, w, c, second_part, pl.ds(row, 1), cut]
-        return second[(k * 2 * local + w) * 2 + c, pl.ds(row, 1), cut]
-
-    def add_to(index, w, c, which, cut, term):
-        if direct:
-            grad[index, w, c, which, :, cut] += term
-        else:
-            target = own_grad if w < local else other_grad
-            target[index, w % local, c, pl.ds(which * part, part), cut] += term
 
     def work(step, carry):
         counts = []
@@ -242,40 +203,32 @@
             j = pairs[base + p, 1]
             shared = jnp.int32(0)
             for w in range(2 * local):
-                side = core if w < local else 1 - core
-                where = w if direct else side * local + w % local
+                is_own = w < local
+                source = own if is_own else other
+                side = core if is_own else 1 - core
+                where = side * local + w % local
                 m = mask[where, i] * mask[where, j]
                 shared = shared + m
-                if direct:
-                    continue
                 m = m.astype(jnp.float32)
                 for c in range(2):
                     at = k * 4 * local + w * 2 + c
-                    first[at] = block(i, w, c, first_part) * m
-                    second[at] = block(j, w, c, second_part) * m
+                    first[at] = block(source, i, w % local, c, first_part) * m
+                    second[at] = block(source, j, w % local, c, second_part) * m
             counts.append(jnp.maximum(shared, 1).astype(jnp.float32) * (2.0 * freq))
             for chunk in range(freq // lanes):
                 cut = pl.ds(chunk * lanes, lanes)
-                if direct:
-                    right = [field[j, n // 2, n % 2, second_part, :, cut] for n in range(4 * local)]
-                else:
-                    right = [second[k * 4 * local + n, :, cut] for n in range(4 * local)]
+                right = [second[k * 4 * local + n, :, cut] for n in range(4 * local)]
                 for c1 in range(part):
                     re = None
                     for w in range(2 * local):
-                        a = first_row(k, i, w, 0, c1, cut)
-                        b = first_row(k, i, w, 1, c1, cut)
+                        a = first[k * 4 * local + 2 * w, pl.ds(c1, 1), cut]
+                        b = first[k * 4 * local + 2 * w + 1, pl.ds(c1, 1), cut]
                         aa = a * right[2 * w] + b * right[2 * w + 1]
                         ab = a * right[2 * w + 1] - b * right[2 * w]
                         re = aa if re is None else re + aa
                         im = ab if w == 0 else im + ab
                     cross_re[pl.ds(k * rows + c1 * part, part), cut] = re.astype(jnp.bfloat16)
                     cross_im[pl.ds(k * rows + c1 * part, part), cut] = im.astype(jnp.bfloat16)
-
-        @pl.when(step == 0)
-        def _():
-            for copy in copies:
-                copy.wait()
 
         cos_sum = jnp.dot(cross_re[...], forward_re[...], preferred_element_type=jnp.float32)
         sin_sum = jnp.dot(cross_im[...], forward_im[...], preferred_element_type=jnp.float32)
@@ -293,9 +246,7 @@
             adj[cut, :freq] = plus_adj.astype(jnp.bfloat16)
             adj[cut, freq:] = minus_adj.astype(jnp.bfloat16)
             total = plus_adj * plus + minus_adj * minus
-            total = jnp.sum(total, axis=0, keepdims=True)
-            total = sum(total[:, n : n + 128] for n in range(0, freq, 128))
-            misfit[pl.ds(step * GROUP + k, 1), :] = total
+            misfit[pl.ds(step * GROUP + k, 1), :] = jnp.sum(total, axis=0, keepdims=True)
         g_sum = jnp.dot(adj[...], back_re[...], preferred_element_type=jnp.float32)
         h_sum = jnp.dot(adj[...], back_im[...], preferred_element_type=jnp.float32)
         for k in range(GROUP):
@@ -311,6 +262,7 @@
             p = step * GROUP + k
             i = pairs[base + p, 0]
             j = pairs[base + p, 1]
+            at = k * 4 * local
             for chunk in range(freq // 128):
                 cut = pl.ds(chunk * 128, 128)
                 to_second = [None] * (4 * local)
@@ -320,41 +272,276 @@
                     g = out_re[chunk, pl.ds(k * rows + c * part, part)]
                     h = out_im[chunk, pl.ds(k * rows + c * part, part)]
                     for w in range(2 * local):
-                        a = first_row(k, i, w, 0, c, cut)
-                        b = first_row(k, i, w, 1, c, cut)
+                        a = first[at + 2 * w, pl.ds(c, 1), cut]
+                        b = first[at + 2 * w + 1, pl.ds(c, 1), cut]
                         to_second[2 * w] = add(to_second[2 * w], g * a - h * b)
                         to_second[2 * w + 1] = add(to_second[2 * w + 1], g * b + h * a)
                 for w in range(2 * local):
+                    target = own_grad if w < local else other_grad
                     for c in range(2):
-                        add_to(j, w, c, second_part, cut, to_second[2 * w + c])
+                        target[j, w % local, c, pl.ds(second_part * part, part), cut] += to_second[2 * w + c]
                 for c in range(part):
                     g = out_re[chunk, pl.ds(k * rows + c, part, stride=part)]
                     h = out_im[chunk, pl.ds(k * rows + c, part, stride=part)]
                     for w in range(2 * local):
-                        a = second_row(k, j, w, 0, c, cut)
-                        b = second_row(k, j, w, 1, c, cut)
+                        a = second[at + 2 * w, pl.ds(c, 1), cut]
+                        b = second[at + 2 * w + 1, pl.ds(c, 1), cut]
                         to_first[2 * w] = add(to_first[2 * w], g * a + h * b)
                         to_first[2 * w + 1] = add(to_first[2 * w + 1], g * b - h * a)
                 for w in range(2 * local):
+                    target = own_grad if w < local else other_grad
                     for c in range(2):
-                        add_to(i, w, c, first_part, cut, to_first[2 * w + c])
+                        target[i, w % local, c, pl.ds(first_part * part, part), cut] += to_first[2 * w + c]
         return carry
 
     lax.fori_loop(0, pair_count // GROUP, work, 0)
 
-    if direct:
-        count = len(HOPS[0])
-        size = 2 * part
-        for n in range(2 * count):
-            index = meta[4 + n]
-            target = own_grad if n < count else other_grad
-            for w in range(2 * local):
-                m = mask[w, index].astype(jnp.float32)
-                for c in range(2):
-                    to = pl.ds((((n % count) * 2 * local + w) * 2 + c) * size, size)
-                    term = grad[index, w, c].reshape(size, freq) * m
-                    target[to] = term.astype(target.dtype)
-        other_grad[count * 4 * local * size :] = note_of(misfit[...], pair_count // 2)
+
+def team_kernel(meta, pairs, mask, *refs):
+    count = len(HOPS[0])
+    came, refs = refs[: 2 * count], refs[2 * count :]
+    (
+        cos_hbm,
+        sin_hbm,
+        alternate,
+        weight,
+        keep,
+        give,
+        misfit,
+        field,
+        grad,
+        cross_re,
+        cross_im,
+        plus_adj,
+        minus_adj,
+        edge_adj,
+        out_re,
+        out_im,
+        cos,
+        sin,
+        sems,
+    ) = refs
+    copies = [
+        pltpu.make_async_copy(cos_hbm, cos, sems.at[0]),
+        pltpu.make_async_copy(sin_hbm, sin, sems.at[1]),
+    ]
+    for copy in copies:
+        copy.start()
+    pair_count = misfit.shape[0]
+    windows = field.shape[1]
+    chunks, part = field.shape[4:6]
+    freq = chunks * 128
+    rows = part * part
+    wide = 256
+    steps = pair_count // GROUP
+    first_part = meta[1]
+    second_part = meta[2]
+    lane = lax.broadcasted_iota(jnp.int32, (rows, 128), 1)
+
+    for n, parcel in enumerate(came):
+        index = meta[4 + n]
+        for w in range(windows):
+            m = mask[w, index].astype(jnp.float32)
+            for c in range(2):
+                both = parcel[w, c].astype(jnp.float32) * m
+                for half in range(2):
+                    for chunk in range(chunks):
+                        field[index, w, c, half, chunk] = both[
+                            half * part : (half + 1) * part, chunk * 128 : (chunk + 1) * 128
+                        ]
+    grad[...] = jnp.zeros_like(grad)
+
+    def row_of(index, w, c, half, chunk, row):
+        return field[index, w, c, half, chunk, pl.ds(row, 1)]
+
+    def scale_of(p, factor):
+        i = pairs[p, 0]
+        j = pairs[p, 1]
+        shared = jnp.int32(0)
+        for w in range(windows):
+            shared = shared + mask[w, i] * mask[w, j]
+        shared = jnp.maximum(shared, 1).astype(jnp.float32) * (2.0 * freq * factor)
+        return lax.rsqrt(jnp.full((1, 128), shared, jnp.float32))
+
+    def cross(s, k):
+        p = s * GROUP + k
+        i = pairs[p, 0]
+        j = pairs[p, 1]
+        for chunk in range(chunks):
+            to = slice(chunk * 128, (chunk + 1) * 128)
+            right = [
+                [field[j, w, c, second_part, chunk] for c in range(2)] for w in range(windows)
+            ]
+            for row in range(0, part, 2):
+                found = []
+                for c1 in (row, row + 1):
+                    re = im = None
+                    for w in range(windows):
+                        a = row_of(i, w, 0, first_part, chunk, c1)
+                        b = row_of(i, w, 1, first_part, chunk, c1)
+                        aa = a * right[w][0] + b * right[w][1]
+                        ab = a * right[w][1] - b * right[w][0]
+                        re = aa if re is None else re + aa
+                        im = ab if im is None else im + ab
+                    found.append((re, im))
+                at = slice(k * rows + row * part, k * rows + (row + 2) * part)
+                for target, n in ((cross_re, 0), (cross_im, 1)):
+                    both = jnp.concatenate([found[0][n], found[1][n]], axis=0)
+                    target[s % 2, at, to] = both.astype(jnp.bfloat16)
+
+    def forward(s, n):
+        cut = slice(n * wide, (n + 1) * wide)
+        even = jnp.dot(cross_re[s % 2], cos[:, cut], preferred_element_type=jnp.float32)
+        odd = jnp.dot(cross_im[s % 2], sin[:, cut], preferred_element_type=jnp.float32)
+        return even, odd
+
+    def forward_edge(s):
+        return jnp.dot(cross_re[s % 2], alternate[...], preferred_element_type=jnp.float32)
+
+    def shape_edge(s, edge, totals):
+        for k in range(GROUP):
+            at = slice(k * rows, (k + 1) * rows)
+            value = edge[at] * (0.5 * scale_of(s * GROUP + k, 1.0))
+            source = value * value * value * 0.125
+            edge_adj[s % 2, at] = source.astype(jnp.bfloat16).astype(jnp.float32)
+            totals[k] = jnp.where(lane == 0, source * value, 0.0)
+
+    def shape(s, n, sums, totals):
+        for k in range(GROUP):
+            at = slice(k * rows, (k + 1) * rows)
+            scale = 0.5 * scale_of(s * GROUP + k, 1.0)
+            for chunk in range(wide // 128):
+                cut = slice(chunk * 128, (chunk + 1) * 128)
+                to = slice(n * wide + chunk * 128, n * wide + (chunk + 1) * 128)
+                even = sums[0][at, cut] * scale
+                odd = sums[1][at, cut] * (3.0 * scale)
+                plus = even + odd
+                minus = even - odd
+                if n == 0 and chunk == 0:
+                    minus = jnp.where(lane == 0, 0.0, minus)
+                plus_source = plus * plus * plus * weight[0:1, to]
+                minus_source = minus * minus * minus * weight[1:2, to]
+                plus_adj[s % 2, at, to] = plus_source.astype(jnp.bfloat16)
+                minus_adj[s % 2, at, to] = minus_source.astype(jnp.bfloat16)
+                totals[k] = totals[k] + (plus_source * plus + minus_source * minus)
+
+    def tell(s, totals):
+        for k in range(GROUP):
+            p = s * GROUP + k
+            misfit[p : p + 1] = jnp.sum(totals[k], axis=0, keepdims=True)
+
+    def back(s, n, which):
+        cut = slice(n * wide, (n + 1) * wide)
+        table = sin if which else cos
+        up = jnp.dot(plus_adj[s % 2], table[:, cut], preferred_element_type=jnp.float32)
+        down = jnp.dot(minus_adj[s % 2], table[:, cut], preferred_element_type=jnp.float32)
+        return up, down
+
+    def scale_back(s, n, which, sums):
+        sign = 1.0 - 2.0 * (lane % 2).astype(jnp.float32)
+        for k in range(GROUP):
+            at = slice(k * rows, (k + 1) * rows)
+            scale = scale_of(s * GROUP + k, 4.0 * part)
+            extra = None if which else edge_adj[s % 2, at] * sign
+            for chunk in range(wide // 128):
+                cut = slice(chunk * 128, (chunk + 1) * 128)
+                if which:
+                    value = sums[0][at, cut] - sums[1][at, cut]
+                else:
+                    value = sums[0][at, cut] + sums[1][at, cut] + extra
+                value = (value * scale).astype(jnp.bfloat16).astype(jnp.float32)
+                target = out_im if which else out_re
+                target[s % 2, n * (wide // 128) + chunk, at] = value
+
+    def gradient(s, k):
+        p = s * GROUP + k
+        i = pairs[p, 0]
+        j = pairs[p, 1]
+        add = lambda total, term: term if total is None else total + term
+        for chunk in range(chunks):
+            for toward_first in (False, True):
+                sums = [[None, None] for w in range(windows)]
+                for c in range(part):
+                    if toward_first:
+                        at = pl.ds(k * rows + c, part, stride=part)
+                    else:
+                        at = pl.ds(k * rows + c * part, part)
+                    g = out_re[s % 2, chunk, at]
+                    h = out_im[s % 2, chunk, at]
+                    for w in range(windows):
+                        if toward_first:
+                            a = row_of(j, w, 0, second_part, chunk, c)
+                            b = row_of(j, w, 1, second_part, chunk, c)
+                            re, im = g * a + h * b, g * b - h * a
+                        else:
+                            a = row_of(i, w, 0, first_part, chunk, c)
+                            b = row_of(i, w, 1, first_part, chunk, c)
+                            re, im = g * a - h * b, g * b + h * a
+                        sums[w] = [add(sums[w][0], re), add(sums[w][1], im)]
+                index = i if toward_first else j
+                half = first_part if toward_first else second_part
+                for w in range(windows):
+                    for c in range(2):
+                        grad[index, w, c, half, chunk] += sums[w][c]
+
+    def start(s, fill):
+        totals = [None] * GROUP
+        edge = forward_edge(s)
+        found = [forward(s, 0)]
+        fill = list(fill)
+        for call in fill[: len(fill) // 2]:
+            call()
+        shape_edge(s, edge, totals)
+        for n in range(1, freq // wide):
+            found.append(forward(s, n))
+            shape(s, n - 1, found[n - 1], totals)
+        for call in fill[len(fill) // 2 :]:
+            call()
+        shape(s, freq // wide - 1, found[-1], totals)
+        tell(s, totals)
+
+    for k in range(GROUP):
+        cross(0, k)
+    for copy in copies:
+        copy.wait()
+    start(0, [])
+    for s in range(steps):
+        fill = []
+        late = []
+        for k in range(GROUP):
+            if s + 1 < steps:
+                fill.append(functools.partial(cross, s + 1, k))
+            if s > 0:
+                (fill if k < GROUP // 2 or s + 1 == steps else late).append(
+                    functools.partial(gradient, s - 1, k)
+                )
+        pieces = [(n, which) for n in range(freq // wide) for which in range(2)]
+        share = -(-len(fill) // len(pieces))
+        for m, (n, which) in enumerate(pieces):
+            sums = back(s, n, which)
+            for call in fill[m * share : (m + 1) * share]:
+                call()
+            scale_back(s, n, which, sums)
+        if s + 1 < steps:
+            start(s + 1, late)
+    for k in range(GROUP):
+        gradient(steps - 1, k)
+
+    size = 2 * part
+    for n in range(2 * count):
+        index = meta[4 + n]
+        target = keep if n < count else give
+        for w in range(windows):
+            m = mask[w, index].astype(jnp.float32)
+            for c in range(2):
+                at = (((n % count) * windows + w) * 2 + c) * size
+                for chunk in range(chunks):
+                    term = jnp.concatenate(
+                        [grad[index, w, c, half, chunk] for half in range(2)], axis=0
+                    )
+                    to = slice(chunk * 128, (chunk + 1) * 128)
+                    target[at : at + size, to] = (term * m).astype(target.dtype)
+    give[count * windows * 2 * size :] = note_of(misfit[...], pair_count // 2)
 
 
 def per_device(spectra, block_pairs, owners, window_mask):
@@ -392,10 +579,6 @@
     chosen = (slot[:, None] == mine_slots[None, :]).astype(jnp.float32)
     misfit_scale = 1.0 / (channels * channels * 2.0 * freq)
 
-    table_arrays = [jnp.asarray(table) for table in tables(freq)]
-    table_arrays[:4] = [
-        pltpu.with_memory_space_constraint(table, pltpu.HBM) for table in table_arrays[:4]
-    ]
     if direct:
         other = lax.ppermute(spectra, "win", swap)
         parcel_type = jax.ShapeDtypeStruct((2 * local, 2, 2 * part, freq), jnp.bfloat16)
@@ -420,46 +603,37 @@
         own = lax.all_to_all(outgoing, "blk", split_axis=0, concat_axis=0, tiled=True)
         came = [own, lax.ppermute(own, "win", swap)]
 
-    grad_shape = (blk_count, 2 * local, 2, 2 * part, freq)
-    grad_bytes = math.prod(grad_shape) * 4
     rows = part * part * GROUP
     parcel_rows = 2 * local * 2 * 2 * part
     misfit_type = jax.ShapeDtypeStruct((pair_count, 128), jnp.float32)
-    scratch = [
-        pltpu.VMEM((GROUP * 4 * local, part, freq), jnp.float32),
-        pltpu.VMEM((GROUP * 4 * local, part, freq), jnp.float32),
-        pltpu.VMEM((rows, freq), jnp.bfloat16),
-        pltpu.VMEM((rows, freq), jnp.bfloat16),
-        pltpu.VMEM((rows, 2 * freq), jnp.bfloat16),
-        pltpu.VMEM((freq // 128, rows, 128), jnp.float32),
-        pltpu.VMEM((freq // 128, rows, 128), jnp.float32),
-    ]
-    scratch += [pltpu.VMEM(table.shape, jnp.bfloat16) for table in table_arrays[:4]]
-    scratch += [pltpu.SemaphoreType.DMA((4,))]
     if direct:
-        split_shape = (blk_count, 2 * local, 2, 2, part, freq)
-        scratch += [pltpu.VMEM(split_shape, jnp.float32)] * 2
-        out_types = (
-            jax.ShapeDtypeStruct((count * parcel_rows, freq), jnp.float32),
-            jax.ShapeDtypeStruct((count * parcel_rows + pair_count // 2, freq), jnp.bfloat16),
-            misfit_type,
-        )
-    else:
-        half = jax.ShapeDtypeStruct((blk_count, local, 2, 2 * part, freq), jnp.float32)
-        out_types = (half, half, misfit_type)
-    own_grad, other_grad, misfit = pl.pallas_call(
-        functools.partial(pair_kernel, direct, pair_count),
-        out_shape=out_types,
-        in_specs=[smem] * 3 + [vmem] * len(came) + [hbm] * 4 + [vmem],
-        out_specs=(vmem, vmem, vmem),
-        scratch_shapes=scratch,
-        compiler_params=pltpu.CompilerParams(
-            vmem_limit_bytes=(16 << 20) + grad_bytes * 3 // (1 if direct else 2)
-        ),
-    )(meta, block_pairs, window_mask, *came, *table_arrays)
-
-    if direct:
-        swapped = lax.ppermute(other_grad, "win", swap)
+        split_shape = (blk_count, 2 * local, 2, 2, freq // 128, part, 128)
+        keep, give, misfit = pl.pallas_call(
+            team_kernel,
+            out_shape=(
+                jax.ShapeDtypeStruct((count * parcel_rows, freq), jnp.float32),
+                jax.ShapeDtypeStruct((count * parcel_rows + pair_count // 2, freq), jnp.bfloat16),
+                misfit_type,
+            ),
+            in_specs=[smem] * 3 + [vmem] * len(came) + [hbm] * 2 + [vmem] * 2,
+            out_specs=(vmem, vmem, vmem),
+            scratch_shapes=[
+                pltpu.VMEM(split_shape, jnp.float32),
+                pltpu.VMEM(split_shape, jnp.float32),
+                pltpu.VMEM((2, rows, freq), jnp.bfloat16),
+                pltpu.VMEM((2, rows, freq), jnp.bfloat16),
+                pltpu.VMEM((2, rows, freq), jnp.bfloat16),
+                pltpu.VMEM((2, rows, freq), jnp.bfloat16),
+                pltpu.VMEM((2, rows, 128), jnp.float32),
+                pltpu.VMEM((2, freq // 128, rows, 128), jnp.float32),
+                pltpu.VMEM((2, freq // 128, rows, 128), jnp.float32),
+                pltpu.VMEM((freq, freq), jnp.bfloat16),
+                pltpu.VMEM((freq, freq), jnp.bfloat16),
+                pltpu.SemaphoreType.DMA((2,)),
+            ],
+            compiler_params=pltpu.CompilerParams(vmem_limit_bytes=24 << 20),
+        )(meta, block_pairs, window_mask, *came, *team_tables(freq))
+        swapped = lax.ppermute(give, "win", swap)
         parcel_type = jax.ShapeDtypeStruct((parcel_rows + pair_count // 2, freq), jnp.bfloat16)
         parcels = pl.pallas_call(
             add_kernel,
@@ -467,7 +641,7 @@
             in_specs=[vmem] * 3,
             out_specs=(vmem,) * count,
             compiler_params=small,
-        )(own_grad, swapped, misfit)
+        )(keep, swapped, misfit)
         landed = [
             lax.ppermute(parcel, ("blk", "win"), pairs) for parcel, pairs in zip(parcels, hop_pairs)
         ]
@@ -492,6 +666,25 @@
             compiler_params=small,
         )(mine, swapped, chosen)
         return (gradient, totals.reshape(CAP))
+    half = jax.ShapeDtypeStruct((blk_count, local, 2, 2 * part, freq), jnp.float32)
+    own_grad, other_grad, misfit = pl.pallas_call(
+        pair_kernel,
+        out_shape=(half, half, jax.ShapeDtypeStruct((pair_count, freq), jnp.float32)),
+        in_specs=[smem] * 3 + [vmem] * 7,
+        out_specs=(vmem, vmem, vmem),
+        scratch_shapes=[
+            pltpu.VMEM((GROUP * 4 * local, part, freq), jnp.float32),
+            pltpu.VMEM((GROUP * 4 * local, part, freq), jnp.float32),
+            pltpu.VMEM((rows, freq), jnp.bfloat16),
+            pltpu.VMEM((rows, freq), jnp.bfloat16),
+            pltpu.VMEM((rows, 2 * freq), jnp.bfloat16),
+            pltpu.VMEM((freq // 128, rows, 128), jnp.float32),
+            pltpu.VMEM((freq // 128, rows, 128), jnp.float32),
+        ],
+        compiler_params=pltpu.CompilerParams(
+            vmem_limit_bytes=(16 << 20) + 3 * math.prod(half.shape) * 4
+        ),
+    )(meta, block_pairs, window_mask, *came, *tables(freq))
 
     swapped = lax.ppermute(other_grad.astype(jnp.bfloat16), "win", swap)
     terms = jnp.sum(misfit, axis=1)

time: 58.9 us -> 56.2 us (0.954)
  Pallas kernels: 18.4 us -> 15.5 us
    pallas_call x1, Pallas kernels: 16.1 us -> 13.3 us  [per_device(): pl.pallas_call(team_kernel, out_shape=(jax.ShapeDtypeStruct((count * parc...]
    ppermute x1 -> x2, waiting for transfers between devices: 1.4 us -> 2.33 us  [per_device(): swapped = lax.ppermute(give, 'win', swap)]
    ppermute x1 -> x0, waiting for transfers between devices: 0.9 us -> none  [per_device(): swapped = lax.ppermute(other_grad, 'win', swap)]
    unnamed x11 -> x13, local copies, waits for them, and re-layouts: 1.65 us -> 1.66 us
where the time goes in v3:
time: 56.2 us; the launch traced here: 55.9 us
  waiting for transfers between devices  23.7 us (42%)
  Pallas kernels  15.5 us (28%)
  starting transfers between devices  13.3 us (24%)
  local copies, waits for them, and re-layouts  2.48 us (4%)
  between operations  0.71 us (1%)
    ppermute x8, waiting for transfers between devices, per_device(): lax.ppermute(parcel, ('blk', 'win'), pairs)  19.7 us
    pallas_call x1, Pallas kernels, per_device(): pl.pallas_call(team_kernel, out_shape=(jax.ShapeDtypeStruct((count * parc...  13.3 us
    ppermute x8, starting transfers between devices, per_device(): lax.ppermute(parcel, ('blk', 'win'), pairs)  11.5 us
    ppermute x2, waiting for transfers between devices, per_device(): swapped = lax.ppermute(give, 'win', swap)  2.33 us
    unnamed x13, local copies, waits for them, and re-layouts  1.66 us
    ppermute x4, waiting for transfers between devices, per_device(): came = landed + [lax.ppermute(parcel, 'win', swap) for parcel in landed]  1.19 us
  transfers between devices with their start and end apart: 15, of which 10 were waited for; matrix products, arithmetic and copies ran while one was open for 2% of the time, Pallas kernels for 0%

profile of v3, /device:TPU:0, one launch (start us, length us, event | category | flops | bytes accessed | tf_op | source)
XLA Modules:
  0.0 55.9 jit_solution(5915321136409650655)
XLA Ops:
  0.6 0.5 collective-permute-start
  1.1 0.7 %dynamic-slice_bitcast_fusion.meta = s32[20]{0:T(128)S(1)} fusion(s32[16,20]{1,0:T(8,128)} %constant.27.clone, s32[]{:T(128)S(6)} %select_n.3), kind=kLoop, calls=%fused_computation.7 | loop fusion | bytes 164 | tf_op jit(solution)/shard_map/squeeze | solution.py:570
  1.8 0.5 collective-permute-done.other
  2.3 0.0 copy-start
  2.3 0.9 %copy-done = bf16[2,1,2,32,512]{4,3,2,1,0:T(8,128)(2,1)S(1)} copy-done((bf16[2,1,2,32,512]{4,3,2,1,0:T(8,128)(2,1)S(1)}, bf16[2,1,2,32,512]{4,3,2,1,0:T(8,128)(2,1)}, u32[]{:S(2)}) %copy-start) | copy-done | bytes 131096
  3.2 0.7 %shard_map.104 = (bf16[4,2,16,512]{3,2,1,0:T(8,128)(2,1)S(1)}, bf16[4,2,16,512]{3,2,1,0:T(8,128)(2,1)S(1)}, bf16[4,2,16,512]{3,2,1,0:T(8,128)(2,1)S(1)}, bf16[4,2,16,512]{3,2,1,0:T(8,128)(2,1)S(1)}) custom-call(s32[20]{0:T(128)S(1)} %dynamic-slice_bitcast_fusion.meta, bf16[2,1,2,32,512]{4,3,2,1,0:T(8,128)(2,1)S(1)} %copy-done, ...), custom_call_target="tpu_custom_call" | custom-call | tf_op jit(solution)/shard_map/pallas_call | solution.py:585
  3.9 5.0 %collective-permute-start.1 = (bf16[4,2,16,512]{3,2,1,0:T(8,128)(2,1)S(1)}, bf16[4,2,16,512]{3,2,1,0:T(8,128)(2,1)S(1)}, u32[]{:S(2)}, u32[]{:S(2)}) collective-permute-start(bf16[4,2,16,512]{3,2,1,0:T(8,128)(2,1)S(1)} %get-tuple-element.17), channel_id=1, source_target_pairs={{0,12},{1,15},{2,14},{3,13},{4,8},{5,11},{6,10},{7,9},{8,4},{9,7},... | collective-permute-start | bytes 393224 | tf_op jit(solution)/shard_map/ppermute | solution.py:594
  8.9 0.0 collective-permute-start.2
  8.9 0.0 copy-start.4
  8.9 0.6 %collective-permute-start.3 = (bf16[4,2,16,512]{3,2,1,0:T(8,128)(2,1)S(1)}, bf16[4,2,16,512]{3,2,1,0:T(8,128)(2,1)S(1)}, u32[]{:S(2)}, u32[]{:S(2)}) collective-permute-start(bf16[4,2,16,512]{3,2,1,0:T(8,128)(2,1)S(1)} %get-tuple-element.19), channel_id=1, source_target_pairs={{0,4},{1,7},{2,6},{3,5},{4,0},{5,3},{6,2},{7,1},{8,12},{9,15},{10,... | collective-permute-start | bytes 393224 | tf_op jit(solution)/shard_map/ppermute | solution.py:594
  9.6 0.8 %collective-permute-start.4 = (bf16[4,2,16,512]{3,2,1,0:T(8,128)(2,1)S(1)}, bf16[4,2,16,512]{3,2,1,0:T(8,128)(2,1)S(1)}, u32[]{:S(2)}, u32[]{:S(2)}) collective-permute-start(bf16[4,2,16,512]{3,2,1,0:T(8,128)(2,1)S(1)} %get-tuple-element.20), channel_id=1, source_target_pairs={{0,0},{1,3},{2,2},{3,1},{4,4},{5,7},{6,6},{7,5},{8,8},{9,11},{10,1... | collective-permute-start | bytes 393224 | tf_op jit(solution)/shard_map/ppermute | solution.py:594
  10.4 2.7 %collective-permute-done.1.refs_0_ = bf16[4,2,16,512]{3,2,1,0:T(8,128)(2,1)S(1)} collective-permute-done((bf16[4,2,16,512]{3,2,1,0:T(8,128)(2,1)S(1)}, bf16[4,2,16,512]{3,2,1,0:T(8,128)(2,1)S(1)}, u32[]{:S(2)}, u32[]{:S(2)}) %collective-permute-start.1) | collective-permute-done | bytes 131104 | tf_op jit(solution)/shard_map/ppermute | solution.py:594
  13.1 0.3 collective-permute-start.5
  13.4 7.6 %collective-permute-done.2.refs_1_ = bf16[4,2,16,512]{3,2,1,0:T(8,128)(2,1)S(1)} collective-permute-done((bf16[4,2,16,512]{3,2,1,0:T(8,128)(2,1)S(1)}, bf16[4,2,16,512]{3,2,1,0:T(8,128)(2,1)S(1)}, u32[]{:S(2)}, u32[]{:S(2)}) %collective-permute-start.2) | collective-permute-done | bytes 131104 | tf_op jit(solution)/shard_map/ppermute | solution.py:594
  21.0 0.0 collective-permute-start.6
  21.0 0.0 collective-permute-done.3.refs_2_
  21.0 0.5 collective-permute-start.7
  21.5 0.0 collective-permute-done.4.refs_3_
  21.5 0.1 collective-permute-start.8
  21.6 0.0 copy-done.4
  21.6 0.1 copy.12.pairs
  21.7 0.0 collective-permute-done.5.refs_4_
  21.7 0.7 %collective-permute-done.6.refs_5_ = bf16[4,2,16,512]{3,2,1,0:T(8,128)(2,1)S(1)} collective-permute-done((bf16[4,2,16,512]{3,2,1,0:T(8,128)(2,1)S(1)}, bf16[4,2,16,512]{3,2,1,0:T(8,128)(2,1)S(1)}, u32[]{:S(2)}, u32[]{:S(2)}) %collective-permute-start.6) | collective-permute-done | bytes 131104 | tf_op jit(solution)/shard_map/ppermute | solution.py:596
  22.4 0.2 collective-permute-done.7.refs_6_
  22.6 0.3 collective-permute-done.8.refs_7_
  22.9 0.0 copy-done.3
  22.9 0.1 jit_solution_.3.refs_10_
  23.0 0.0 copy-done.1
  23.0 0.0 copy-done.2
  23.1 13.3 %shard_map.105 = (f32[512,512]{1,0:T(8,128)S(1)}, bf16[520,512]{1,0:T(8,128)(2,1)S(1)}, f32[16,128]{1,0:T(8,128)S(1)}) custom-call(s32[20]{0:T(128)S(1)} %dynamic-slice_bitcast_fusion.meta, s32[16,2]{1,0:T(8,128)S(1)} %copy.12.pairs, s32[4,8]{1,0:T(4,128)S(1)} %copy-done.2, bf16[4,2,16,512]{3,2,1,0:T(8,128)(2,1)S(1)} %collective-permute-done.1.refs_0_, ...), custom_call_target="tpu_custom_call" | custom-call | tf_op jit(solution)/shard_map/pallas_call | solution.py:611
  36.3 0.2 collective-permute-start.9
  36.6 0.7 %copy-done.5 = s32[16,1]{0,1:T(1,128)S(1)} copy-done((s32[16,1]{0,1:T(1,128)S(1)}, s32[16,1]{0,1:T(1,128)}, u32[]{:S(2)}) %copy-start.5) | copy-done | bytes 88
  37.2 0.2 convert_reduce_fusion
  37.4 0.9 %collective-permute-done.9.came = bf16[520,512]{1,0:T(8,128)(2,1)S(1)} collective-permute-done((bf16[520,512]{1,0:T(8,128)(2,1)S(1)}, bf16[520,512]{1,0:T(8,128)(2,1)S(1)}, u32[]{:S(2)}, u32[]{:S(2)}) %collective-permute-start.9) | collective-permute-done | bytes 532512 | tf_op jit(solution)/shard_map/ppermute | solution.py:636
  38.3 0.1 shard_map.106
  38.4 2.5 %collective-permute-start.10 = (bf16[136,512]{1,0:T(8,128)(2,1)S(1)}, bf16[136,512]{1,0:T(8,128)(2,1)S(1)}, u32[]{:S(2)}, u32[]{:S(2)}) collective-permute-start(bf16[136,512]{1,0:T(8,128)(2,1)S(1)} %get-tuple-element.24), channel_id=1, source_target_pairs={{0,12},{1,15},{2,14},{3,13},{4,8},{5,11},{6,10},{7,9},{8,4},{9,7},... | collective-permute-start | bytes 417800 | tf_op jit(solution)/shard_map/ppermute | solution.py:646
  40.9 0.0 collective-permute-start.11
  41.0 1.9 %collective-permute-start.12 = (bf16[136,512]{1,0:T(8,128)(2,1)S(1)}, bf16[136,512]{1,0:T(8,128)(2,1)S(1)}, u32[]{:S(2)}, u32[]{:S(2)}) collective-permute-start(bf16[136,512]{1,0:T(8,128)(2,1)S(1)} %get-tuple-element.26), channel_id=1, source_target_pairs={{0,4},{1,7},{2,6},{3,5},{4,0},{5,3},{6,2},{7,1},{8,12},{9,15},{10,... | collective-permute-start | bytes 417800 | tf_op jit(solution)/shard_map/ppermute | solution.py:646
  42.9 0.7 %collective-permute-start.13 = (bf16[136,512]{1,0:T(8,128)(2,1)S(1)}, bf16[136,512]{1,0:T(8,128)(2,1)S(1)}, u32[]{:S(2)}, u32[]{:S(2)}) collective-permute-start(bf16[136,512]{1,0:T(8,128)(2,1)S(1)} %get-tuple-element.27), channel_id=1, source_target_pairs={{0,0},{1,3},{2,2},{3,1},{4,4},{5,7},{6,6},{7,5},{8,8},{9,11},{10,1... | collective-permute-start | bytes 417800 | tf_op jit(solution)/shard_map/ppermute | solution.py:646
  43.5 3.4 %collective-permute-done.10.refs_0_ = bf16[136,512]{1,0:T(8,128)(2,1)S(1)} collective-permute-done((bf16[136,512]{1,0:T(8,128)(2,1)S(1)}, bf16[136,512]{1,0:T(8,128)(2,1)S(1)}, u32[]{:S(2)}, u32[]{:S(2)}) %collective-permute-start.10) | collective-permute-done | bytes 139296 | tf_op jit(solution)/shard_map/ppermute | solution.py:646
  47.0 5.8 %collective-permute-done.11.refs_1_ = bf16[136,512]{1,0:T(8,128)(2,1)S(1)} collective-permute-done((bf16[136,512]{1,0:T(8,128)(2,1)S(1)}, bf16[136,512]{1,0:T(8,128)(2,1)S(1)}, u32[]{:S(2)}, u32[]{:S(2)}) %collective-permute-start.11) | collective-permute-done | bytes 139296 | tf_op jit(solution)/shard_map/ppermute | solution.py:646
  52.8 0.0 collective-permute-done.12.refs_2_
  52.8 0.0 collective-permute-done.13.refs_3_
  52.8 0.8 %shard_map.107 = (f32[144,512]{1,0:T(8,128)S(1)}, f32[144,512]{1,0:T(8,128)S(1)}) custom-call(s32[20]{0:T(128)S(1)} %dynamic-slice_bitcast_fusion.meta, bf16[136,512]{1,0:T(8,128)(2,1)S(1)} %collective-permute-done.10.refs_0_, bf16[136,512]{1,0:T(8,128)(2,1)S(1)} %collective-permute-done.11.refs_1_, bf16[136,512]{1,0:T(8,128)(2,1)S(1)} %collective-permute-done.12.refs_2_, ...), custom_call_target="tpu_custom_call" | custom-call | tf_op jit(solution)/shard_map/pallas_call | solution.py:649
  53.6 0.1 collective-permute-start.14
  53.8 0.1 compare_convert_fusion.chosen
  53.8 1.4 %collective-permute-done.14.came = f32[144,512]{1,0:T(8,128)S(1)} collective-permute-done((f32[144,512]{1,0:T(8,128)S(1)}, f32[144,512]{1,0:T(8,128)S(1)}, u32[]{:S(2)}, u32[]{:S(2)}) %collective-permute-start.14) | collective-permute-done | bytes 294944 | tf_op jit(solution)/shard_map/ppermute | solution.py:657
  55.3 0.7 %shard_map.108 = (bf16[2,1,2,32,512]{4,3,2,1,0:T(8,128)(2,1)}, f32[1,3]{1,0:T(1,128)}) custom-call(f32[144,512]{1,0:T(8,128)S(1)} %get-tuple-element.28.mine, f32[144,512]{1,0:T(8,128)S(1)} %collective-permute-done.14.came, f32[16,3]{1,0:T(8,128)S(1)} %compare_convert_fusion.chosen), custom_call_target="tpu_custom_call" | custom-call | tf_op jit(solution)/shard_map/pallas_call | solution.py:658
  (6 shorter events, 0.0 us)
Async XLA Ops:
  0.6 1.7 %collective-permute-start = (bf16[2,1,2,32,512]{4,3,2,1,0:T(8,128)(2,1)}, bf16[2,1,2,32,512]{4,3,2,1,0:T(8,128)(2,1)S(1)}, u32[]{:S(2)}, u32[]{:S(2)}) collective-permute-start(bf16[2,1,2,32,512]{4,3,2,1,0:T(8,128)(2,1)} %own.1), channel_id=1, source_target_pairs={{0,1},{1,0},{2,3},{3,2},{4,5},{5,4},{6,7},{7,6},{8,9},{9,8},{10,11... | collective-permute-start | bytes 393224 | tf_op jit(solution)/shard_map/ppermute | solution.py:583
  2.3 0.9 %copy-start = (bf16[2,1,2,32,512]{4,3,2,1,0:T(8,128)(2,1)S(1)}, bf16[2,1,2,32,512]{4,3,2,1,0:T(8,128)(2,1)}, u32[]{:S(2)}) copy-start(bf16[2,1,2,32,512]{4,3,2,1,0:T(8,128)(2,1)} %own.1) | copy-start | bytes 393220
  3.9 9.2 %collective-permute-start.1 = (bf16[4,2,16,512]{3,2,1,0:T(8,128)(2,1)S(1)}, bf16[4,2,16,512]{3,2,1,0:T(8,128)(2,1)S(1)}, u32[]{:S(2)}, u32[]{:S(2)}) collective-permute-start(bf16[4,2,16,512]{3,2,1,0:T(8,128)(2,1)S(1)} %get-tuple-element.17), channel_id=1, source_target_pairs={{0,12},{1,15},{2,14},{3,13},{4,8},{5,11},{6,10},{7,9},{8,4},{9,7},... | collective-permute-start | bytes 393224 | tf_op jit(solution)/shard_map/ppermute | solution.py:594
  8.9 12.1 %collective-permute-start.2 = (bf16[4,2,16,512]{3,2,1,0:T(8,128)(2,1)S(1)}, bf16[4,2,16,512]{3,2,1,0:T(8,128)(2,1)S(1)}, u32[]{:S(2)}, u32[]{:S(2)}) collective-permute-start(bf16[4,2,16,512]{3,2,1,0:T(8,128)(2,1)S(1)} %get-tuple-element.18), channel_id=1, source_target_pairs={{0,8},{1,11},{2,10},{3,9},{4,12},{5,15},{6,14},{7,13},{8,0},{9,3},... | collective-permute-start | bytes 393224 | tf_op jit(solution)/shard_map/ppermute | solution.py:594
  8.9 12.7 %copy-start.4 = (s32[16,2]{0,1:T(2,128)S(1)}, s32[16,2]{0,1:T(2,128)}, u32[]{:S(2)}) copy-start(s32[16,2]{0,1:T(2,128)} %param.10) | copy-start | bytes 388
  8.9 12.1 %collective-permute-start.3 = (bf16[4,2,16,512]{3,2,1,0:T(8,128)(2,1)S(1)}, bf16[4,2,16,512]{3,2,1,0:T(8,128)(2,1)S(1)}, u32[]{:S(2)}, u32[]{:S(2)}) collective-permute-start(bf16[4,2,16,512]{3,2,1,0:T(8,128)(2,1)S(1)} %get-tuple-element.19), channel_id=1, source_target_pairs={{0,4},{1,7},{2,6},{3,5},{4,0},{5,3},{6,2},{7,1},{8,12},{9,15},{10,... | collective-permute-start | bytes 393224 | tf_op jit(solution)/shard_map/ppermute | solution.py:594
  9.6 13.3 %copy-start.3 = (bf16[512]{0:T(512)(128)(2,1)S(1)}, bf16[512]{0:T(512)(128)(2,1)}, u32[]{:S(2)}) copy-start(bf16[512]{0:T(512)(128)(2,1)} %constant.30.clone) | copy-start | bytes 3076
  9.6 12.0 %collective-permute-start.4 = (bf16[4,2,16,512]{3,2,1,0:T(8,128)(2,1)S(1)}, bf16[4,2,16,512]{3,2,1,0:T(8,128)(2,1)S(1)}, u32[]{:S(2)}, u32[]{:S(2)}) collective-permute-start(bf16[4,2,16,512]{3,2,1,0:T(8,128)(2,1)S(1)} %get-tuple-element.20), channel_id=1, source_target_pairs={{0,0},{1,3},{2,2},{3,1},{4,4},{5,7},{6,6},{7,5},{8,8},{9,11},{10,1... | collective-permute-start | bytes 393224 | tf_op jit(solution)/shard_map/ppermute | solution.py:594
  13.1 8.6 %collective-permute-start.5 = (bf16[4,2,16,512]{3,2,1,0:T(8,128)(2,1)S(1)}, bf16[4,2,16,512]{3,2,1,0:T(8,128)(2,1)S(1)}, u32[]{:S(2)}, u32[]{:S(2)}) collective-permute-start(bf16[4,2,16,512]{3,2,1,0:T(8,128)(2,1)S(1)} %collective-permute-done.1.refs_0_), channel_id=1, source_target_pairs={{0,1},{1,0},{2,3},{3,2},{4,5},{5,4},{6,7},{7,6},{8,9},{9,8},{10,11... | collective-permute-start | bytes 393224 | tf_op jit(solution)/shard_map/ppermute | solution.py:596
  21.0 1.3 %collective-permute-start.6 = (bf16[4,2,16,512]{3,2,1,0:T(8,128)(2,1)S(1)}, bf16[4,2,16,512]{3,2,1,0:T(8,128)(2,1)S(1)}, u32[]{:S(2)}, u32[]{:S(2)}) collective-permute-start(bf16[4,2,16,512]{3,2,1,0:T(8,128)(2,1)S(1)} %collective-permute-done.2.refs_1_), channel_id=1, source_target_pairs={{0,1},{1,0},{2,3},{3,2},{4,5},{5,4},{6,7},{7,6},{8,9},{9,8},{10,11... | collective-permute-start | bytes 393224 | tf_op jit(solution)/shard_map/ppermute | solution.py:596
  21.0 1.5 %collective-permute-start.7 = (bf16[4,2,16,512]{3,2,1,0:T(8,128)(2,1)S(1)}, bf16[4,2,16,512]{3,2,1,0:T(8,128)(2,1)S(1)}, u32[]{:S(2)}, u32[]{:S(2)}) collective-permute-start(bf16[4,2,16,512]{3,2,1,0:T(8,128)(2,1)S(1)} %collective-permute-done.3.refs_2_), channel_id=1, source_target_pairs={{0,1},{1,0},{2,3},{3,2},{4,5},{5,4},{6,7},{7,6},{8,9},{9,8},{10,11... | collective-permute-start | bytes 393224 | tf_op jit(solution)/shard_map/ppermute | solution.py:596
  21.5 1.3 %collective-permute-start.8 = (bf16[4,2,16,512]{3,2,1,0:T(8,128)(2,1)S(1)}, bf16[4,2,16,512]{3,2,1,0:T(8,128)(2,1)S(1)}, u32[]{:S(2)}, u32[]{:S(2)}) collective-permute-start(bf16[4,2,16,512]{3,2,1,0:T(8,128)(2,1)S(1)} %collective-permute-done.4.refs_3_), channel_id=1, source_target_pairs={{0,1},{1,0},{2,3},{3,2},{4,5},{5,4},{6,7},{7,6},{8,9},{9,8},{10,11... | collective-permute-start | bytes 393224 | tf_op jit(solution)/shard_map/ppermute | solution.py:596
  21.7 1.3 %copy-start.1 = (f32[2,512]{1,0:T(2,128)S(1)}, f32[2,512]{1,0:T(2,128)}, u32[]{:S(2)}) copy-start(f32[2,512]{1,0:T(2,128)} %constant.31.clone.refs_11_) | copy-start | bytes 12292
  21.7 1.3 %copy-start.2 = (s32[4,8]{1,0:T(4,128)S(1)}, s32[4,8]{1,0:T(4,128)}, u32[]{:S(2)}) copy-start(s32[4,8]{1,0:T(4,128)} %mask.1) | copy-start | bytes 388
  36.3 2.0 %collective-permute-start.9 = (bf16[520,512]{1,0:T(8,128)(2,1)S(1)}, bf16[520,512]{1,0:T(8,128)(2,1)S(1)}, u32[]{:S(2)}, u32[]{:S(2)}) collective-permute-start(bf16[520,512]{1,0:T(8,128)(2,1)S(1)} %get-tuple-element.22), channel_id=1, source_target_pairs={{0,1},{1,0},{2,3},{3,2},{4,5},{5,4},{6,7},{7,6},{8,9},{9,8},{10,11... | collective-permute-start | bytes 1597448 | tf_op jit(solution)/shard_map/ppermute | solution.py:636
  36.6 0.7 %copy-start.5 = (s32[16,1]{0,1:T(1,128)S(1)}, s32[16,1]{0,1:T(1,128)}, u32[]{:S(2)}) copy-start(s32[16,1]{0,1:T(1,128)} %param.11) | copy-start | bytes 196
  38.4 8.6 %collective-permute-start.10 = (bf16[136,512]{1,0:T(8,128)(2,1)S(1)}, bf16[136,512]{1,0:T(8,128)(2,1)S(1)}, u32[]{:S(2)}, u32[]{:S(2)}) collective-permute-start(bf16[136,512]{1,0:T(8,128)(2,1)S(1)} %get-tuple-element.24), channel_id=1, source_target_pairs={{0,12},{1,15},{2,14},{3,13},{4,8},{5,11},{6,10},{7,9},{8,4},{9,7},... | collective-permute-start | bytes 417800 | tf_op jit(solution)/shard_map/ppermute | solution.py:646
  40.9 11.8 %collective-permute-start.11 = (bf16[136,512]{1,0:T(8,128)(2,1)S(1)}, bf16[136,512]{1,0:T(8,128)(2,1)S(1)}, u32[]{:S(2)}, u32[]{:S(2)}) collective-permute-start(bf16[136,512]{1,0:T(8,128)(2,1)S(1)} %get-tuple-element.25), channel_id=1, source_target_pairs={{0,8},{1,11},{2,10},{3,9},{4,12},{5,15},{6,14},{7,13},{8,0},{9,3},... | collective-permute-start | bytes 417800 | tf_op jit(solution)/shard_map/ppermute | solution.py:646
  41.0 11.8 %collective-permute-start.12 = (bf16[136,512]{1,0:T(8,128)(2,1)S(1)}, bf16[136,512]{1,0:T(8,128)(2,1)S(1)}, u32[]{:S(2)}, u32[]{:S(2)}) collective-permute-start(bf16[136,512]{1,0:T(8,128)(2,1)S(1)} %get-tuple-element.26), channel_id=1, source_target_pairs={{0,4},{1,7},{2,6},{3,5},{4,0},{5,3},{6,2},{7,1},{8,12},{9,15},{10,... | collective-permute-start | bytes 417800 | tf_op jit(solution)/shard_map/ppermute | solution.py:646
  42.9 9.9 %collective-permute-start.13 = (bf16[136,512]{1,0:T(8,128)(2,1)S(1)}, bf16[136,512]{1,0:T(8,128)(2,1)S(1)}, u32[]{:S(2)}, u32[]{:S(2)}) collective-permute-start(bf16[136,512]{1,0:T(8,128)(2,1)S(1)} %get-tuple-element.27), channel_id=1, source_target_pairs={{0,0},{1,3},{2,2},{3,1},{4,4},{5,7},{6,6},{7,5},{8,8},{9,11},{10,1... | collective-permute-start | bytes 417800 | tf_op jit(solution)/shard_map/ppermute | solution.py:646
  53.6 1.6 %collective-permute-start.14 = (f32[144,512]{1,0:T(8,128)S(1)}, f32[144,512]{1,0:T(8,128)S(1)}, u32[]{:S(2)}, u32[]{:S(2)}) collective-permute-start(f32[144,512]{1,0:T(8,128)S(1)} %get-tuple-element.29), channel_id=1, source_target_pairs={{0,1},{1,0},{2,3},{3,2},{4,5},{5,4},{6,7},{7,6},{8,9},{9,8},{10,11... | collective-permute-start | bytes 884744 | tf_op jit(solution)/shard_map/ppermute | solution.py:657

commit v4 on v3

--- a/solution.py
+++ b/solution.py
@@ -51,14 +51,14 @@
 
 @functools.lru_cache(maxsize=None)
 def positions():
-    out = np.zeros((TEAM, 2, 20), np.int32)
+    out = np.zeros((TEAM, 2, 28), np.int32)
     for rank in range(TEAM):
         for core in range(2):
             same = rank in (0, TEAM - 1)
             row = [0, core, core if same else 1 - core, core]
             row += [rank ^ hop for hop in HOPS[core]]
             row += [rank ^ hop for hop in HOPS[1 - core]]
-            for hop in HOPS[core]:
+            for hop in HOPS[core] + HOPS[1 - core]:
                 row += SUBSETS[rank ^ hop]
             out[rank, core] = row
     return out.reshape(TEAM * 2, -1)
@@ -111,22 +111,22 @@
     )
 
 
-def merge_kernel(meta, *refs):
-    parcels, (mine, give, total) = refs[: len(HOPS[0])], refs[len(HOPS[0]) :]
-    windows, _, _, part, freq = total.shape
-    channels = PARTS * part
-    local = windows // 2
+def merge_kernel(meta, *refs, scale):
+    parcels, (chosen, gradient, totals, total) = refs[:-4], refs[-4:]
+    local, _, _, part, freq = total.shape
     core = meta[3]
-    rows = windows * 2 * 2 * part
+    size = 2 * part
+    rows = 4 * local * size
     note = None
     total[...] = jnp.zeros_like(total)
-    for r, parcel in enumerate(parcels):
-        for w in range(windows):
+    for n, parcel in enumerate(parcels):
+        for w in range(local):
             for c in range(2):
-                for n in range(2):
-                    start = ((w * 2 + c) * 2 + n) * part
-                    term = parcel[start : start + part].astype(jnp.float32)
-                    total[w, c, meta[12 + 2 * r + n]] += term
+                start = pl.multiple_of(((core * local + w) * 2 + c) * size, size)
+                both = parcel[pl.ds(start, size)].astype(jnp.float32)
+                for half in range(2):
+                    at = slice(half * part, (half + 1) * part)
+                    total[w, c, meta[12 + 2 * n + half]] += both[at]
         tail = parcel[rows:].astype(jnp.float32)
         tail = jnp.concatenate(
             [tail[:, :128] + tail[:, 256:384], tail[:, 128:256] + tail[:, 384:512]], axis=0
@@ -134,23 +134,7 @@
         note = tail if note is None else note + tail
     for w in range(local):
         for c in range(2):
-            to = slice((w * 2 + c) * channels, (w * 2 + c + 1) * channels)
-            mine[to] = total[core * local + w, c].reshape(channels, freq)
-            give[to] = total[(1 - core) * local + w, c].reshape(channels, freq)
-    body = local * 2 * channels
-    pad = jnp.zeros((note.shape[0], freq - 128), jnp.float32)
-    mine[body:] = jnp.concatenate([note, pad], axis=1)
-    give[body:] = jnp.concatenate([note, pad], axis=1)
-
-
-def finish_kernel(mine, came, chosen, gradient, totals, scale):
-    local, _, _, channels, _ = gradient.shape
-    for w in range(local):
-        for c in range(2):
-            cut = slice((w * 2 + c) * channels, (w * 2 + c + 1) * channels)
-            gradient[w, 0, c] = (mine[cut] + came[cut]).astype(jnp.bfloat16)
-    body = local * 2 * channels
-    note = mine[body:, :128] + came[body:, :128]
+            gradient[w, 0, c] = total[w, c].reshape(PARTS * part, freq).astype(jnp.bfloat16)
     pair = jnp.sum(note, axis=1, keepdims=True) * scale
     totals[...] = jnp.sum(pair * chosen[...], axis=0, keepdims=True)
 
@@ -645,26 +629,18 @@
         landed = [
             lax.ppermute(parcel, ("blk", "win"), pairs) for parcel, pairs in zip(parcels, hop_pairs)
         ]
-        half_type = jax.ShapeDtypeStruct((local * 2 * channels + pair_count, freq), jnp.float32)
-        mine, give = pl.pallas_call(
-            merge_kernel,
-            out_shape=(half_type, half_type),
-            in_specs=[smem] + [vmem] * count,
-            out_specs=(vmem, vmem),
-            scratch_shapes=[pltpu.VMEM((2 * local, 2, PARTS, part, freq), jnp.float32)],
-            compiler_params=small,
-        )(meta, *landed)
-        swapped = lax.ppermute(give, "win", swap)
+        landed += [lax.ppermute(parcel, "win", swap) for parcel in landed]
         gradient, totals = pl.pallas_call(
-            functools.partial(finish_kernel, scale=misfit_scale),
+            functools.partial(merge_kernel, scale=misfit_scale),
             out_shape=(
                 jax.ShapeDtypeStruct(spectra.shape, jnp.bfloat16),
                 jax.ShapeDtypeStruct((1, CAP), jnp.float32),
             ),
-            in_specs=[vmem] * 3,
+            in_specs=[smem] + [vmem] * (len(landed) + 1),
             out_specs=(vmem, vmem),
+            scratch_shapes=[pltpu.VMEM((local, 2, PARTS, part, freq), jnp.float32)],
             compiler_params=small,
-        )(mine, swapped, chosen)
+        )(meta, *landed, chosen)
         return (gradient, totals.reshape(CAP))
     half = jax.ShapeDtypeStruct((blk_count, local, 2, 2 * part, freq), jnp.float32)
     own_grad, other_grad, misfit = pl.pallas_call(

time: 56.2 us -> 56.3 us (level)
    ppermute x0 -> x4, waiting for transfers between devices: none -> 1.2 us  [per_device(): landed += [lax.ppermute(parcel, 'win', swap) for parcel in landed]]
    ppermute x2 -> x1, waiting for transfers between devices: 2.33 us -> 1.16 us  [per_device(): swapped = lax.ppermute(give, 'win', swap)]
    ppermute x0 -> x4, starting transfers between devices: none -> 0.6 us  [per_device(): landed += [lax.ppermute(parcel, 'win', swap) for parcel in landed]]
    pallas_call x2 -> x1, Pallas kernels: 1.49 us -> 1.42 us  [per_device(): pl.pallas_call(functools.partial(merge_kernel, scale=misfit_scale), out_s...]
  transfers between devices with their start and end apart: 15 -> 18, of which waited for: 10 -> 12; matrix products, arithmetic and copies ran while one was open for 2% -> 2% of each run, Pallas kernels for 0% -> 0%
where the time goes in v4:
time: 56.3 us; the launch traced here: 56.1 us
  waiting for transfers between devices  23.7 us (42%)
  Pallas kernels  15.4 us (27%)
  starting transfers between devices  13.8 us (25%)
  local copies, waits for them, and re-layouts  2.23 us (4%)
  between operations  0.73 us (1%)
    ppermute x8, waiting for transfers between devices, per_device(): lax.ppermute(parcel, ('blk', 'win'), pairs)  19.6 us
    pallas_call x1, Pallas kernels, per_device(): pl.pallas_call(team_kernel, out_shape=(jax.ShapeDtypeStruct((count * parc...  13.3 us
    ppermute x8, starting transfers between devices, per_device(): lax.ppermute(parcel, ('blk', 'win'), pairs)  11.5 us
    pallas_call x1, Pallas kernels, per_device(): pl.pallas_call(functools.partial(merge_kernel, scale=misfit_scale), out_s...  1.42 us
    unnamed x13, local copies, waits for them, and re-layouts  1.41 us
    ppermute x4, waiting for transfers between devices, per_device(): landed += [lax.ppermute(parcel, 'win', swap) for parcel in landed]  1.2 us
    ppermute x4, waiting for transfers between devices, per_device(): came = landed + [lax.ppermute(parcel, 'win', swap) for parcel in landed]  1.19 us
    ppermute x1, waiting for transfers between devices, per_device(): swapped = lax.ppermute(give, 'win', swap)  1.16 us
  transfers between devices with their start and end apart: 18, of which 12 were waited for; matrix products, arithmetic and copies ran while one was open for 2% of the time, Pallas kernels for 0%

profile of v4, /device:TPU:0, one launch (start us, length us, event | category | flops | bytes accessed | tf_op | source)
XLA Modules:
  0.0 56.1 jit_solution(16185394260606937558)
XLA Ops:
  0.6 0.5 collective-permute-start
  1.1 0.7 %dynamic-slice_bitcast_fusion.meta = s32[28]{0:T(128)S(1)} fusion(s32[16,28]{1,0:T(8,128)} %constant.27.clone, s32[]{:T(128)S(6)} %select_n.3), kind=kLoop, calls=%fused_computation.7 | loop fusion | bytes 228 | tf_op jit(solution)/shard_map/squeeze | solution.py:554
  1.8 0.5 collective-permute-done.other
  2.3 0.9 %copy-done = bf16[2,1,2,32,512]{4,3,2,1,0:T(8,128)(2,1)S(1)} copy-done((bf16[2,1,2,32,512]{4,3,2,1,0:T(8,128)(2,1)S(1)}, bf16[2,1,2,32,512]{4,3,2,1,0:T(8,128)(2,1)}, u32[]{:S(2)}) %copy-start) | copy-done | bytes 131096
  3.2 0.7 %shard_map.104 = (bf16[4,2,16,512]{3,2,1,0:T(8,128)(2,1)S(1)}, bf16[4,2,16,512]{3,2,1,0:T(8,128)(2,1)S(1)}, bf16[4,2,16,512]{3,2,1,0:T(8,128)(2,1)S(1)}, bf16[4,2,16,512]{3,2,1,0:T(8,128)(2,1)S(1)}) custom-call(s32[28]{0:T(128)S(1)} %dynamic-slice_bitcast_fusion.meta, bf16[2,1,2,32,512]{4,3,2,1,0:T(8,128)(2,1)S(1)} %copy-done, ...), custom_call_target="tpu_custom_call" | custom-call | tf_op jit(solution)/shard_map/pallas_call | solution.py:569
  3.9 5.0 %collective-permute-start.1 = (bf16[4,2,16,512]{3,2,1,0:T(8,128)(2,1)S(1)}, bf16[4,2,16,512]{3,2,1,0:T(8,128)(2,1)S(1)}, u32[]{:S(2)}, u32[]{:S(2)}) collective-permute-start(bf16[4,2,16,512]{3,2,1,0:T(8,128)(2,1)S(1)} %get-tuple-element.15), channel_id=1, source_target_pairs={{0,12},{1,15},{2,14},{3,13},{4,8},{5,11},{6,10},{7,9},{8,4},{9,7},... | collective-permute-start | bytes 393224 | tf_op jit(solution)/shard_map/ppermute | solution.py:578
  8.9 0.0 collective-permute-start.2
  8.9 0.6 %collective-permute-start.3 = (bf16[4,2,16,512]{3,2,1,0:T(8,128)(2,1)S(1)}, bf16[4,2,16,512]{3,2,1,0:T(8,128)(2,1)S(1)}, u32[]{:S(2)}, u32[]{:S(2)}) collective-permute-start(bf16[4,2,16,512]{3,2,1,0:T(8,128)(2,1)S(1)} %get-tuple-element.17), channel_id=1, source_target_pairs={{0,4},{1,7},{2,6},{3,5},{4,0},{5,3},{6,2},{7,1},{8,12},{9,15},{10,... | collective-permute-start | bytes 393224 | tf_op jit(solution)/shard_map/ppermute | solution.py:578
  9.6 0.8 %collective-permute-start.4 = (bf16[4,2,16,512]{3,2,1,0:T(8,128)(2,1)S(1)}, bf16[4,2,16,512]{3,2,1,0:T(8,128)(2,1)S(1)}, u32[]{:S(2)}, u32[]{:S(2)}) collective-permute-start(bf16[4,2,16,512]{3,2,1,0:T(8,128)(2,1)S(1)} %get-tuple-element.18), channel_id=1, source_target_pairs={{0,0},{1,3},{2,2},{3,1},{4,4},{5,7},{6,6},{7,5},{8,8},{9,11},{10,1... | collective-permute-start | bytes 393224 | tf_op jit(solution)/shard_map/ppermute | solution.py:578
  10.4 2.7 %collective-permute-done.1.refs_0_ = bf16[4,2,16,512]{3,2,1,0:T(8,128)(2,1)S(1)} collective-permute-done((bf16[4,2,16,512]{3,2,1,0:T(8,128)(2,1)S(1)}, bf16[4,2,16,512]{3,2,1,0:T(8,128)(2,1)S(1)}, u32[]{:S(2)}, u32[]{:S(2)}) %collective-permute-start.1) | collective-permute-done | bytes 131104 | tf_op jit(solution)/shard_map/ppermute | solution.py:578
  13.1 0.3 collective-permute-start.5
  13.4 7.6 %collective-permute-done.2.refs_1_ = bf16[4,2,16,512]{3,2,1,0:T(8,128)(2,1)S(1)} collective-permute-done((bf16[4,2,16,512]{3,2,1,0:T(8,128)(2,1)S(1)}, bf16[4,2,16,512]{3,2,1,0:T(8,128)(2,1)S(1)}, u32[]{:S(2)}, u32[]{:S(2)}) %collective-permute-start.2) | collective-permute-done | bytes 131104 | tf_op jit(solution)/shard_map/ppermute | solution.py:578
  21.0 0.0 collective-permute-start.6
  21.0 0.0 collective-permute-done.3.refs_2_
  21.0 0.5 collective-permute-start.7
  21.5 0.0 collective-permute-done.4.refs_3_
  21.5 0.1 collective-permute-start.8
  21.6 0.1 copy.12.pairs
  21.7 0.0 collective-permute-done.5.refs_4_
  21.7 0.7 %collective-permute-done.6.refs_5_ = bf16[4,2,16,512]{3,2,1,0:T(8,128)(2,1)S(1)} collective-permute-done((bf16[4,2,16,512]{3,2,1,0:T(8,128)(2,1)S(1)}, bf16[4,2,16,512]{3,2,1,0:T(8,128)(2,1)S(1)}, u32[]{:S(2)}, u32[]{:S(2)}) %collective-permute-start.6) | collective-permute-done | bytes 131104 | tf_op jit(solution)/shard_map/ppermute | solution.py:580
  22.4 0.2 collective-permute-done.7.refs_6_
  22.6 0.3 collective-permute-done.8.refs_7_
  22.9 0.1 jit_solution_.3.refs_10_
  23.1 13.3 %shard_map.105 = (f32[512,512]{1,0:T(8,128)S(1)}, bf16[520,512]{1,0:T(8,128)(2,1)S(1)}, f32[16,128]{1,0:T(8,128)S(1)}) custom-call(s32[28]{0:T(128)S(1)} %dynamic-slice_bitcast_fusion.meta, s32[16,2]{1,0:T(8,128)S(1)} %copy.12.pairs, s32[4,8]{1,0:T(4,128)S(1)} %copy-done.2, bf16[4,2,16,512]{3,2,1,0:T(8,128)(2,1)S(1)} %collective-permute-done.1.refs_0_, ...), custom_call_target="tpu_custom_call" | custom-call | tf_op jit(solution)/shard_map/pallas_call | solution.py:595
  36.3 0.0 copy-start.5
  36.3 0.2 collective-permute-start.9
  36.6 0.4 copy-done.5
  37.0 0.2 convert_reduce_fusion
  37.2 1.2 %collective-permute-done.9.came = bf16[520,512]{1,0:T(8,128)(2,1)S(1)} collective-permute-done((bf16[520,512]{1,0:T(8,128)(2,1)S(1)}, bf16[520,512]{1,0:T(8,128)(2,1)S(1)}, u32[]{:S(2)}, u32[]{:S(2)}) %collective-permute-start.9) | collective-permute-done | bytes 532512 | tf_op jit(solution)/shard_map/ppermute | solution.py:620
  38.3 0.1 shard_map.106
  38.4 2.5 %collective-permute-start.10 = (bf16[136,512]{1,0:T(8,128)(2,1)S(1)}, bf16[136,512]{1,0:T(8,128)(2,1)S(1)}, u32[]{:S(2)}, u32[]{:S(2)}) collective-permute-start(bf16[136,512]{1,0:T(8,128)(2,1)S(1)} %get-tuple-element.22), channel_id=1, source_target_pairs={{0,12},{1,15},{2,14},{3,13},{4,8},{5,11},{6,10},{7,9},{8,4},{9,7},... | collective-permute-start | bytes 417800 | tf_op jit(solution)/shard_map/ppermute | solution.py:630
  41.0 0.0 collective-permute-start.11
  41.0 1.9 %collective-permute-start.12 = (bf16[136,512]{1,0:T(8,128)(2,1)S(1)}, bf16[136,512]{1,0:T(8,128)(2,1)S(1)}, u32[]{:S(2)}, u32[]{:S(2)}) collective-permute-start(bf16[136,512]{1,0:T(8,128)(2,1)S(1)} %get-tuple-element.24), channel_id=1, source_target_pairs={{0,4},{1,7},{2,6},{3,5},{4,0},{5,3},{6,2},{7,1},{8,12},{9,15},{10,... | collective-permute-start | bytes 417800 | tf_op jit(solution)/shard_map/ppermute | solution.py:630
  42.9 0.7 %collective-permute-start.13 = (bf16[136,512]{1,0:T(8,128)(2,1)S(1)}, bf16[136,512]{1,0:T(8,128)(2,1)S(1)}, u32[]{:S(2)}, u32[]{:S(2)}) collective-permute-start(bf16[136,512]{1,0:T(8,128)(2,1)S(1)} %get-tuple-element.25), channel_id=1, source_target_pairs={{0,0},{1,3},{2,2},{3,1},{4,4},{5,7},{6,6},{7,5},{8,8},{9,11},{10,1... | collective-permute-start | bytes 417800 | tf_op jit(solution)/shard_map/ppermute | solution.py:630
  43.6 3.4 %collective-permute-done.10.refs_0_ = bf16[136,512]{1,0:T(8,128)(2,1)S(1)} collective-permute-done((bf16[136,512]{1,0:T(8,128)(2,1)S(1)}, bf16[136,512]{1,0:T(8,128)(2,1)S(1)}, u32[]{:S(2)}, u32[]{:S(2)}) %collective-permute-start.10) | collective-permute-done | bytes 139296 | tf_op jit(solution)/shard_map/ppermute | solution.py:630
  47.0 0.0 collective-permute-start.14
  47.0 5.8 %collective-permute-done.11.refs_1_ = bf16[136,512]{1,0:T(8,128)(2,1)S(1)} collective-permute-done((bf16[136,512]{1,0:T(8,128)(2,1)S(1)}, bf16[136,512]{1,0:T(8,128)(2,1)S(1)}, u32[]{:S(2)}, u32[]{:S(2)}) %collective-permute-start.11) | collective-permute-done | bytes 139296 | tf_op jit(solution)/shard_map/ppermute | solution.py:630
  52.8 0.1 collective-permute-start.15
  52.9 0.0 collective-permute-done.12.refs_2_
  52.9 0.4 collective-permute-start.16
  53.3 0.0 collective-permute-done.13.refs_3_
  53.3 0.1 collective-permute-start.17
  53.4 0.1 compare_convert_fusion.refs_8_
  53.5 0.0 collective-permute-done.14.refs_4_
  53.5 0.7 %collective-permute-done.15.refs_5_ = bf16[136,512]{1,0:T(8,128)(2,1)S(1)} collective-permute-done((bf16[136,512]{1,0:T(8,128)(2,1)S(1)}, bf16[136,512]{1,0:T(8,128)(2,1)S(1)}, u32[]{:S(2)}, u32[]{:S(2)}) %collective-permute-start.15) | collective-permute-done | bytes 139296 | tf_op jit(solution)/shard_map/ppermute | solution.py:632
  54.2 0.2 collective-permute-done.16.refs_6_
  54.4 0.3 collective-permute-done.17.refs_7_
  54.7 1.4 %shard_map.107 = (bf16[2,1,2,32,512]{4,3,2,1,0:T(8,128)(2,1)}, f32[1,3]{1,0:T(1,128)}) custom-call(s32[28]{0:T(128)S(1)} %dynamic-slice_bitcast_fusion.meta, bf16[136,512]{1,0:T(8,128)(2,1)S(1)} %collective-permute-done.10.refs_0_, bf16[136,512]{1,0:T(8,128)(2,1)S(1)} %collective-permute-done.11.refs_1_, ...), custom_call_target="tpu_custom_call" | custom-call | tf_op jit(solution)/shard_map/pallas_call | solution.py:633
  (11 shorter events, 0.0 us)
Async XLA Ops:
  0.6 1.7 %collective-permute-start = (bf16[2,1,2,32,512]{4,3,2,1,0:T(8,128)(2,1)}, bf16[2,1,2,32,512]{4,3,2,1,0:T(8,128)(2,1)S(1)}, u32[]{:S(2)}, u32[]{:S(2)}) collective-permute-start(bf16[2,1,2,32,512]{4,3,2,1,0:T(8,128)(2,1)} %own.1), channel_id=1, source_target_pairs={{0,1},{1,0},{2,3},{3,2},{4,5},{5,4},{6,7},{7,6},{8,9},{9,8},{10,11... | collective-permute-start | bytes 393224 | tf_op jit(solution)/shard_map/ppermute | solution.py:567
  2.3 0.9 %copy-start = (bf16[2,1,2,32,512]{4,3,2,1,0:T(8,128)(2,1)S(1)}, bf16[2,1,2,32,512]{4,3,2,1,0:T(8,128)(2,1)}, u32[]{:S(2)}) copy-start(bf16[2,1,2,32,512]{4,3,2,1,0:T(8,128)(2,1)} %own.1) | copy-start | bytes 393220
  3.9 9.2 %collective-permute-start.1 = (bf16[4,2,16,512]{3,2,1,0:T(8,128)(2,1)S(1)}, bf16[4,2,16,512]{3,2,1,0:T(8,128)(2,1)S(1)}, u32[]{:S(2)}, u32[]{:S(2)}) collective-permute-start(bf16[4,2,16,512]{3,2,1,0:T(8,128)(2,1)S(1)} %get-tuple-element.15), channel_id=1, source_target_pairs={{0,12},{1,15},{2,14},{3,13},{4,8},{5,11},{6,10},{7,9},{8,4},{9,7},... | collective-permute-start | bytes 393224 | tf_op jit(solution)/shard_map/ppermute | solution.py:578
  8.9 12.1 %collective-permute-start.2 = (bf16[4,2,16,512]{3,2,1,0:T(8,128)(2,1)S(1)}, bf16[4,2,16,512]{3,2,1,0:T(8,128)(2,1)S(1)}, u32[]{:S(2)}, u32[]{:S(2)}) collective-permute-start(bf16[4,2,16,512]{3,2,1,0:T(8,128)(2,1)S(1)} %get-tuple-element.16), channel_id=1, source_target_pairs={{0,8},{1,11},{2,10},{3,9},{4,12},{5,15},{6,14},{7,13},{8,0},{9,3},... | collective-permute-start | bytes 393224 | tf_op jit(solution)/shard_map/ppermute | solution.py:578
  8.9 12.7 %copy-start.4 = (s32[16,2]{0,1:T(2,128)S(1)}, s32[16,2]{0,1:T(2,128)}, u32[]{:S(2)}) copy-start(s32[16,2]{0,1:T(2,128)} %param.10) | copy-start | bytes 388
  8.9 12.1 %collective-permute-start.3 = (bf16[4,2,16,512]{3,2,1,0:T(8,128)(2,1)S(1)}, bf16[4,2,16,512]{3,2,1,0:T(8,128)(2,1)S(1)}, u32[]{:S(2)}, u32[]{:S(2)}) collective-permute-start(bf16[4,2,16,512]{3,2,1,0:T(8,128)(2,1)S(1)} %get-tuple-element.17), channel_id=1, source_target_pairs={{0,4},{1,7},{2,6},{3,5},{4,0},{5,3},{6,2},{7,1},{8,12},{9,15},{10,... | collective-permute-start | bytes 393224 | tf_op jit(solution)/shard_map/ppermute | solution.py:578
  9.6 13.3 %copy-start.3 = (bf16[512]{0:T(512)(128)(2,1)S(1)}, bf16[512]{0:T(512)(128)(2,1)}, u32[]{:S(2)}) copy-start(bf16[512]{0:T(512)(128)(2,1)} %constant.30.clone) | copy-start | bytes 3076
  9.6 12.0 %collective-permute-start.4 = (bf16[4,2,16,512]{3,2,1,0:T(8,128)(2,1)S(1)}, bf16[4,2,16,512]{3,2,1,0:T(8,128)(2,1)S(1)}, u32[]{:S(2)}, u32[]{:S(2)}) collective-permute-start(bf16[4,2,16,512]{3,2,1,0:T(8,128)(2,1)S(1)} %get-tuple-element.18), channel_id=1, source_target_pairs={{0,0},{1,3},{2,2},{3,1},{4,4},{5,7},{6,6},{7,5},{8,8},{9,11},{10,1... | collective-permute-start | bytes 393224 | tf_op jit(solution)/shard_map/ppermute | solution.py:578
  13.1 8.6 %collective-permute-start.5 = (bf16[4,2,16,512]{3,2,1,0:T(8,128)(2,1)S(1)}, bf16[4,2,16,512]{3,2,1,0:T(8,128)(2,1)S(1)}, u32[]{:S(2)}, u32[]{:S(2)}) collective-permute-start(bf16[4,2,16,512]{3,2,1,0:T(8,128)(2,1)S(1)} %collective-permute-done.1.refs_0_), channel_id=1, source_target_pairs={{0,1},{1,0},{2,3},{3,2},{4,5},{5,4},{6,7},{7,6},{8,9},{9,8},{10,11... | collective-permute-start | bytes 393224 | tf_op jit(solution)/shard_map/ppermute | solution.py:580
  21.0 1.3 %collective-permute-start.6 = (bf16[4,2,16,512]{3,2,1,0:T(8,128)(2,1)S(1)}, bf16[4,2,16,512]{3,2,1,0:T(8,128)(2,1)S(1)}, u32[]{:S(2)}, u32[]{:S(2)}) collective-permute-start(bf16[4,2,16,512]{3,2,1,0:T(8,128)(2,1)S(1)} %collective-permute-done.2.refs_1_), channel_id=1, source_target_pairs={{0,1},{1,0},{2,3},{3,2},{4,5},{5,4},{6,7},{7,6},{8,9},{9,8},{10,11... | collective-permute-start | bytes 393224 | tf_op jit(solution)/shard_map/ppermute | solution.py:580
  21.0 1.5 %collective-permute-start.7 = (bf16[4,2,16,512]{3,2,1,0:T(8,128)(2,1)S(1)}, bf16[4,2,16,512]{3,2,1,0:T(8,128)(2,1)S(1)}, u32[]{:S(2)}, u32[]{:S(2)}) collective-permute-start(bf16[4,2,16,512]{3,2,1,0:T(8,128)(2,1)S(1)} %collective-permute-done.3.refs_2_), channel_id=1, source_target_pairs={{0,1},{1,0},{2,3},{3,2},{4,5},{5,4},{6,7},{7,6},{8,9},{9,8},{10,11... | collective-permute-start | bytes 393224 | tf_op jit(solution)/shard_map/ppermute | solution.py:580
  21.5 1.3 %collective-permute-start.8 = (bf16[4,2,16,512]{3,2,1,0:T(8,128)(2,1)S(1)}, bf16[4,2,16,512]{3,2,1,0:T(8,128)(2,1)S(1)}, u32[]{:S(2)}, u32[]{:S(2)}) collective-permute-start(bf16[4,2,16,512]{3,2,1,0:T(8,128)(2,1)S(1)} %collective-permute-done.4.refs_3_), channel_id=1, source_target_pairs={{0,1},{1,0},{2,3},{3,2},{4,5},{5,4},{6,7},{7,6},{8,9},{9,8},{10,11... | collective-permute-start | bytes 393224 | tf_op jit(solution)/shard_map/ppermute | solution.py:580
  21.7 1.3 %copy-start.1 = (f32[2,512]{1,0:T(2,128)S(1)}, f32[2,512]{1,0:T(2,128)}, u32[]{:S(2)}) copy-start(f32[2,512]{1,0:T(2,128)} %constant.31.clone.refs_11_) | copy-start | bytes 12292
  21.7 1.3 %copy-start.2 = (s32[4,8]{1,0:T(4,128)S(1)}, s32[4,8]{1,0:T(4,128)}, u32[]{:S(2)}) copy-start(s32[4,8]{1,0:T(4,128)} %mask.1) | copy-start | bytes 388
  36.3 0.7 %copy-start.5 = (s32[16,1]{0,1:T(1,128)S(1)}, s32[16,1]{0,1:T(1,128)}, u32[]{:S(2)}) copy-start(s32[16,1]{0,1:T(1,128)} %param.11) | copy-start | bytes 196
  36.3 2.0 %collective-permute-start.9 = (bf16[520,512]{1,0:T(8,128)(2,1)S(1)}, bf16[520,512]{1,0:T(8,128)(2,1)S(1)}, u32[]{:S(2)}, u32[]{:S(2)}) collective-permute-start(bf16[520,512]{1,0:T(8,128)(2,1)S(1)} %get-tuple-element.20), channel_id=1, source_target_pairs={{0,1},{1,0},{2,3},{3,2},{4,5},{5,4},{6,7},{7,6},{8,9},{9,8},{10,11... | collective-permute-start | bytes 1597448 | tf_op jit(solution)/shard_map/ppermute | solution.py:620
  38.4 8.6 %collective-permute-start.10 = (bf16[136,512]{1,0:T(8,128)(2,1)S(1)}, bf16[136,512]{1,0:T(8,128)(2,1)S(1)}, u32[]{:S(2)}, u32[]{:S(2)}) collective-permute-start(bf16[136,512]{1,0:T(8,128)(2,1)S(1)} %get-tuple-element.22), channel_id=1, source_target_pairs={{0,12},{1,15},{2,14},{3,13},{4,8},{5,11},{6,10},{7,9},{8,4},{9,7},... | collective-permute-start | bytes 417800 | tf_op jit(solution)/shard_map/ppermute | solution.py:630
  41.0 11.8 %collective-permute-start.11 = (bf16[136,512]{1,0:T(8,128)(2,1)S(1)}, bf16[136,512]{1,0:T(8,128)(2,1)S(1)}, u32[]{:S(2)}, u32[]{:S(2)}) collective-permute-start(bf16[136,512]{1,0:T(8,128)(2,1)S(1)} %get-tuple-element.23), channel_id=1, source_target_pairs={{0,8},{1,11},{2,10},{3,9},{4,12},{5,15},{6,14},{7,13},{8,0},{9,3},... | collective-permute-start | bytes 417800 | tf_op jit(solution)/shard_map/ppermute | solution.py:630
  41.0 11.9 %collective-permute-start.12 = (bf16[136,512]{1,0:T(8,128)(2,1)S(1)}, bf16[136,512]{1,0:T(8,128)(2,1)S(1)}, u32[]{:S(2)}, u32[]{:S(2)}) collective-permute-start(bf16[136,512]{1,0:T(8,128)(2,1)S(1)} %get-tuple-element.24), channel_id=1, source_target_pairs={{0,4},{1,7},{2,6},{3,5},{4,0},{5,3},{6,2},{7,1},{8,12},{9,15},{10,... | collective-permute-start | bytes 417800 | tf_op jit(solution)/shard_map/ppermute | solution.py:630
  42.9 10.4 %collective-permute-start.13 = (bf16[136,512]{1,0:T(8,128)(2,1)S(1)}, bf16[136,512]{1,0:T(8,128)(2,1)S(1)}, u32[]{:S(2)}, u32[]{:S(2)}) collective-permute-start(bf16[136,512]{1,0:T(8,128)(2,1)S(1)} %get-tuple-element.25), channel_id=1, source_target_pairs={{0,0},{1,3},{2,2},{3,1},{4,4},{5,7},{6,6},{7,5},{8,8},{9,11},{10,1... | collective-permute-start | bytes 417800 | tf_op jit(solution)/shard_map/ppermute | solution.py:630
  47.0 6.5 %collective-permute-start.14 = (bf16[136,512]{1,0:T(8,128)(2,1)S(1)}, bf16[136,512]{1,0:T(8,128)(2,1)S(1)}, u32[]{:S(2)}, u32[]{:S(2)}) collective-permute-start(bf16[136,512]{1,0:T(8,128)(2,1)S(1)} %collective-permute-done.10.refs_0_), channel_id=1, source_target_pairs={{0,1},{1,0},{2,3},{3,2},{4,5},{5,4},{6,7},{7,6},{8,9},{9,8},{10,11... | collective-permute-start | bytes 417800 | tf_op jit(solution)/shard_map/ppermute | solution.py:632
  52.8 1.4 %collective-permute-start.15 = (bf16[136,512]{1,0:T(8,128)(2,1)S(1)}, bf16[136,512]{1,0:T(8,128)(2,1)S(1)}, u32[]{:S(2)}, u32[]{:S(2)}) collective-permute-start(bf16[136,512]{1,0:T(8,128)(2,1)S(1)} %collective-permute-done.11.refs_1_), channel_id=1, source_target_pairs={{0,1},{1,0},{2,3},{3,2},{4,5},{5,4},{6,7},{7,6},{8,9},{9,8},{10,11... | collective-permute-start | bytes 417800 | tf_op jit(solution)/shard_map/ppermute | solution.py:632
  52.9 1.5 %collective-permute-start.16 = (bf16[136,512]{1,0:T(8,128)(2,1)S(1)}, bf16[136,512]{1,0:T(8,128)(2,1)S(1)}, u32[]{:S(2)}, u32[]{:S(2)}) collective-permute-start(bf16[136,512]{1,0:T(8,128)(2,1)S(1)} %collective-permute-done.12.refs_2_), channel_id=1, source_target_pairs={{0,1},{1,0},{2,3},{3,2},{4,5},{5,4},{6,7},{7,6},{8,9},{9,8},{10,11... | collective-permute-start | bytes 417800 | tf_op jit(solution)/shard_map/ppermute | solution.py:632
  53.3 1.4 %collective-permute-start.17 = (bf16[136,512]{1,0:T(8,128)(2,1)S(1)}, bf16[136,512]{1,0:T(8,128)(2,1)S(1)}, u32[]{:S(2)}, u32[]{:S(2)}) collective-permute-start(bf16[136,512]{1,0:T(8,128)(2,1)S(1)} %collective-permute-done.13.refs_3_), channel_id=1, source_target_pairs={{0,1},{1,0},{2,3},{3,2},{4,5},{5,4},{6,7},{7,6},{8,9},{9,8},{10,11... | collective-permute-start | bytes 417800 | tf_op jit(solution)/shard_map/ppermute | solution.py:632
